TPU v7x, 32 devices: a whole 2x2x4 slice. The times are simulated.
32 devices in a mesh: fsdp: 16 (over z, y, core), rep: 2 (over x).
Axes of the slice: x: 2, y: 2, z: 4, core: 2. Of those that a mesh axis runs over, the one named last changes fastest.
Arguments:
- inputs: bfloat16 [4096, 2048], P(('fsdp', 'rep')), may hold values from -12 to 12
- norm_one_gain: bfloat16 [2048], P(('fsdp', 'rep')), may hold values from 0.5 to 1.5
- norm_one_bias: bfloat16 [2048], P(('fsdp', 'rep')), may hold values from -1.25 to 1.25
- w_query: bfloat16 [2048, 2048], P(('fsdp', 'rep')), may hold values from -0.125 to 0.125
- b_query: bfloat16 [2048], P(('fsdp', 'rep')), may hold values from -1.75 to 1.75
- w_key: bfloat16 [2048, 2048], P(('fsdp', 'rep')), may hold values from -0.125 to 0.125
- w_value: bfloat16 [2048, 2048], P(('fsdp', 'rep')), may hold values from -0.125 to 0.125
- b_value: bfloat16 [2048], P(('fsdp', 'rep')), may hold values from -1.75 to 1.75
- w_out: bfloat16 [2048, 2048], P(('fsdp', 'rep')), may hold values from -0.5 to 0.5
- b_out: bfloat16 [2048], P(('fsdp', 'rep')), may hold values from -1.25 to 1.25
- norm_two_gain: bfloat16 [2048], P(('fsdp', 'rep')), may hold values from 0.5 to 1.5
- norm_two_bias: bfloat16 [2048], P(('fsdp', 'rep')), may hold values from -1.25 to 1.25
- w_up: bfloat16 [2048, 8192], P(('fsdp', 'rep')), may hold values from -0.125 to 0.125
- b_up: bfloat16 [8192], P(('fsdp', 'rep')), may hold values from -1.75 to 1.75
- w_down: bfloat16 [2048, 8192], P(('fsdp', 'rep')), may hold values from -0.0625 to 0.0625
- b_down: bfloat16 [2048], P(('fsdp', 'rep')), may hold values from -1.25 to 1.25
- parents: int32 [32], replicated, may hold values from -1 to 23, as said below
- cotangent: bfloat16 [4096, 2048], P(('fsdp', 'rep')), may hold values from -12 to 12
Outputs:
- layer_output: bfloat16 [4096, 2048], P(('fsdp', 'rep'))
- grad_inputs: float32 [4096, 2048], P(('fsdp', 'rep'))
- grad_norm_one_gain: float32 [2048], P(('fsdp', 'rep'))
- grad_norm_one_bias: float32 [2048], P(('fsdp', 'rep'))
- grad_w_query: float32 [2048, 2048], P(('fsdp', 'rep'))
- grad_b_query: float32 [2048], P(('fsdp', 'rep'))
- grad_w_key: float32 [2048, 2048], P(('fsdp', 'rep'))
- grad_w_value: float32 [2048, 2048], P(('fsdp', 'rep'))
- grad_b_value: float32 [2048], P(('fsdp', 'rep'))
- grad_w_out: float32 [2048, 2048], P(('fsdp', 'rep'))
- grad_b_out: float32 [2048], P(('fsdp', 'rep'))
- grad_norm_two_gain: float32 [2048], P(('fsdp', 'rep'))
- grad_norm_two_bias: float32 [2048], P(('fsdp', 'rep'))
- grad_w_up: float32 [2048, 8192], P(('fsdp', 'rep'))
- grad_b_up: float32 [8192], P(('fsdp', 'rep'))
- grad_w_down: float32 [2048, 8192], P(('fsdp', 'rep'))
- grad_b_down: float32 [2048], P(('fsdp', 'rep'))
Inputs may be any that keep to these rules, and one draw needn't show every extreme that they name: parents[s] is -1 for the first segment of a tree, else the segment before s on its path. Each tree fills 16 consecutive segments: a chain of 4 trunk segments in order, then four branch segments whose parent is the trunk's last, then eight leaf segments, two on each branch, in an order drawn from the seed.
All inputs are finite; a program needn't handle non-finite values.
Results may differ from a plain program's by a relative error of at most 0.014.
Values may be sent and summed in bfloat16 or wider, within the bound.
A program may use at most 384 MiB of HBM per device.

v0:
```python
from functools import partial

import jax
import jax.numpy as jnp
from jax import lax
from jax.sharding import PartitionSpec as P

HEAD_DIM = 128
TRUNK_SEGS = 4
TREE_SEGS = 16


epsilon = 1e-05


def shifted(value, axis, steps):
    count = lax.axis_size(axis)
    leading, last = (max(0, -steps), min(count, count - steps))
    return lax.ppermute(value, axis, [(source, source + steps) for source in range(leading, last)])


def layer_norm(values, gain_vec, offset_vec):
    row_mean = jnp.mean(values, axis=-1, keepdims=True)
    centred = values - row_mean
    spread = jnp.mean(centred * centred, axis=-1, keepdims=True)
    return centred * lax.rsqrt(spread + epsilon) * gain_vec + offset_vec


def contract_last(left_side, right_side):
    return lax.dot_general(
        left_side, right_side, (((1,), (1,)), ((), ())), preferred_element_type=jnp.float32
    )


def contract_first(left_side, right_side):
    return lax.dot_general(
        left_side, right_side, (((0,), (0,)), ((), ())), preferred_element_type=jnp.float32
    )


def split_heads(rows_in, head_count):
    return rows_in.reshape(rows_in.shape[0], head_count, rows_in.shape[1] // head_count)


def gather_params(attn_shards, mlp_shards):
    w_query, w_key, w_value, w_out, b_query, b_value, b_out, gain_one, bias_one = attn_shards
    w_up, w_down, b_up, b_down, gain_two, bias_two = mlp_shards
    full = (
        lax.all_gather(w_query, ("fsdp", "rep"), axis=0, tiled=True),
        lax.all_gather(w_key, ("fsdp", "rep"), axis=0, tiled=True),
        lax.all_gather(w_value, ("fsdp", "rep"), axis=0, tiled=True),
        lax.all_gather(w_out, ("fsdp", "rep"), axis=0, tiled=True),
        lax.all_gather(b_query, ("fsdp", "rep"), axis=0, tiled=True),
        lax.all_gather(b_value, ("fsdp", "rep"), axis=0, tiled=True),
        lax.all_gather(b_out, ("fsdp", "rep"), axis=0, tiled=True),
        lax.all_gather(gain_one, ("fsdp", "rep"), axis=0, tiled=True),
        lax.all_gather(bias_one, ("fsdp", "rep"), axis=0, tiled=True),
        lax.all_gather(w_up, ("fsdp", "rep"), axis=0, tiled=True),
        lax.all_gather(w_down, ("fsdp", "rep"), axis=0, tiled=True),
        lax.all_gather(b_up, ("fsdp", "rep"), axis=0, tiled=True),
        lax.all_gather(b_down, ("fsdp", "rep"), axis=0, tiled=True),
        lax.all_gather(gain_two, ("fsdp", "rep"), axis=0, tiled=True),
        lax.all_gather(bias_two, ("fsdp", "rep"), axis=0, tiled=True),
    )
    return (tuple(full[0:9]), tuple(full[9:15]))


def ancestor_chain(parents, own_seg):
    link_list = []
    current = own_seg
    for level_index in range(TRUNK_SEGS + 1):
        upper_seg = lax.dynamic_index_in_dim(parents, jnp.maximum(current, 0), keepdims=False)
        current = jnp.where(current >= 0, upper_seg, -1)
        link_list.append(current)
    return jnp.stack(link_list)


def visible_mask(chain_links, own_seg, first_seg, tok_dev, rep_size):
    key_rows = jnp.arange(tok_dev * rep_size, dtype=jnp.int32)
    key_segs = first_seg + key_rows // tok_dev
    upward = jnp.any(chain_links[:, None] == key_segs[None, :], axis=0) & (key_segs >= 0)
    causal = (key_rows % tok_dev)[None, :] <= jnp.arange(tok_dev, dtype=jnp.int32)[:, None]
    return upward[None, :] | (key_segs == own_seg)[None, :] & causal


def forward(inputs, attn_full, mlp_full, parents):
    w_query, w_key, w_value, w_out, b_query, b_value, b_out, gain_one, bias_one = attn_full
    w_up, w_down, b_up, b_down, gain_two, bias_two = mlp_full
    tok_dev, model_width = inputs.shape
    head_count = model_width // HEAD_DIM
    score_scale = HEAD_DIM ** (-0.5)
    rep_size = lax.axis_size("rep")
    fsdp_index = lax.axis_index("fsdp")
    own_seg = fsdp_index * rep_size + lax.axis_index("rep")
    chain_links = ancestor_chain(parents, own_seg)
    residual_in = inputs.astype(jnp.float32)
    norm_one = layer_norm(
        residual_in, gain_one.astype(jnp.float32), bias_one.astype(jnp.float32)
    ).astype(jnp.bfloat16)
    queries = (
        jnp.dot(norm_one, w_query, preferred_element_type=jnp.float32) + b_query.astype(jnp.float32)
    ).astype(jnp.bfloat16)
    key_rows = jnp.dot(norm_one, w_key, preferred_element_type=jnp.float32).astype(jnp.bfloat16)
    value_rows = (
        jnp.dot(norm_one, w_value, preferred_element_type=jnp.float32) + b_value.astype(jnp.float32)
    ).astype(jnp.bfloat16)
    key_value = lax.all_gather(jnp.stack([key_rows, value_rows]), "rep", axis=1, tiled=True)
    tree_blocks = TREE_SEGS // rep_size
    block_list = [key_value]
    for distance in range(1, tree_blocks):
        block_list.append(shifted(key_value, "fsdp", distance))
    queries_h = split_heads(queries, head_count)
    score_shape = (head_count, tok_dev, tok_dev * rep_size)
    score_list = []
    active_list = []
    for block_index in range(tree_blocks):
        first_seg = (fsdp_index - block_index) * rep_size
        mask_now = visible_mask(chain_links, own_seg, first_seg, tok_dev, rep_size)
        active = jnp.any(mask_now)
        keys_here = split_heads(block_list[block_index][0], head_count)

        def compute_scores(keys_here=keys_here, mask_now=mask_now):
            raw_scores = (
                jnp.einsum("qhd,khd->hqk", queries_h, keys_here, preferred_element_type=jnp.float32)
                * score_scale
            )
            return jnp.where(mask_now[None], raw_scores, -jnp.inf)

        def skip_scores():
            return jnp.full(score_shape, -jnp.inf, jnp.float32)

        score_list.append(lax.cond(active, compute_scores, skip_scores))
        active_list.append(active)
    row_max = jnp.max(score_list[0], axis=-1)
    for scores_now in score_list[1:]:
        row_max = jnp.maximum(row_max, jnp.max(scores_now, axis=-1))
    exp_total = jnp.zeros_like(row_max)
    for scores_now in score_list:
        exp_total = exp_total + jnp.sum(jnp.exp(scores_now - row_max[..., None]), axis=-1)
    log_total = row_max + jnp.log(exp_total)
    context_acc = jnp.zeros((tok_dev, head_count, HEAD_DIM), jnp.float32)
    for block_index in range(tree_blocks):
        values_here = split_heads(block_list[block_index][1], head_count)
        scores_now = score_list[block_index]

        def weigh_values(scores_now=scores_now, values_here=values_here):
            probs_low = jnp.exp(scores_now - log_total[..., None]).astype(jnp.bfloat16)
            return jnp.einsum(
                "hqk,khd->qhd", probs_low, values_here, preferred_element_type=jnp.float32
            )

        context_acc = context_acc + lax.cond(
            active_list[block_index], weigh_values, lambda: jnp.zeros_like(context_acc)
        )
    context_low = context_acc.reshape(tok_dev, model_width).astype(jnp.bfloat16)
    residual = (
        residual_in
        + jnp.dot(context_low, w_out, preferred_element_type=jnp.float32)
        + b_out.astype(jnp.float32)
    )
    norm_two = layer_norm(
        residual, gain_two.astype(jnp.float32), bias_two.astype(jnp.float32)
    ).astype(jnp.bfloat16)
    upward = jnp.dot(norm_two, w_up, preferred_element_type=jnp.float32) + b_up.astype(jnp.float32)
    active_low = jax.nn.gelu(upward, approximate=True).astype(jnp.bfloat16)
    output_rows = residual + contract_last(active_low, w_down) + b_down.astype(jnp.float32)
    return {
        "residual_in": residual_in,
        "norm_one": norm_one,
        "queries_h": queries_h,
        "block_list": block_list,
        "score_list": score_list,
        "active_list": active_list,
        "log_total": log_total,
        "context_low": context_low,
        "residual": residual,
        "norm_two": norm_two,
        "upward": upward,
        "active_low": active_low,
        "output_rows": output_rows,
    }


def body(
    inputs,
    norm_one_gain,
    norm_one_bias,
    w_query,
    b_query,
    w_key,
    w_value,
    b_value,
    w_out,
    b_out,
    norm_two_gain,
    norm_two_bias,
    w_up,
    b_up,
    w_down,
    b_down,
    parents,
    cotangent,
):
    attn_shards = (
        w_query,
        w_key,
        w_value,
        w_out,
        b_query,
        b_value,
        b_out,
        norm_one_gain,
        norm_one_bias,
    )
    mlp_shards = (w_up, w_down, b_up, b_down, norm_two_gain, norm_two_bias)
    attn_full, mlp_full = gather_params(attn_shards, mlp_shards)
    saved = forward(inputs, attn_full, mlp_full, parents)
    layer_output = saved["output_rows"].astype(jnp.bfloat16)
    attn_shards, mlp_shards, layer_output = lax.optimization_barrier(
        (attn_shards, mlp_shards, layer_output)
    )
    attn_full, mlp_full = gather_params(attn_shards, mlp_shards)
    saved = forward(inputs, attn_full, mlp_full, parents)
    (
        full_query,
        full_key,
        full_value,
        full_out,
        unused_bq,
        unused_bv,
        unused_bo,
        gain_one,
        bias_one,
    ) = attn_full
    full_up, full_down, unused_bu, unused_bd, gain_two, bias_two = mlp_full
    tok_dev, model_width = inputs.shape
    head_count = model_width // HEAD_DIM
    score_scale = HEAD_DIM ** (-0.5)
    rep_size = lax.axis_size("rep")
    tree_blocks = TREE_SEGS // rep_size
    grad_out_f = cotangent.astype(jnp.float32)
    d_active = jnp.dot(cotangent, full_down, preferred_element_type=jnp.float32)
    unused_gelu, gelu_back = jax.vjp(partial(jax.nn.gelu, approximate=True), saved["upward"])
    d_upward = gelu_back(d_active)[0].astype(jnp.bfloat16)
    d_norm_two = contract_last(d_upward, full_up)
    unused_norm, norm_two_back = jax.vjp(
        layer_norm, saved["residual"], gain_two.astype(jnp.float32), bias_two.astype(jnp.float32)
    )
    d_res_norm, grad_gain_two, grad_bias_two = norm_two_back(d_norm_two)
    d_residual = grad_out_f + d_res_norm
    d_attended = d_residual.astype(jnp.bfloat16)
    d_context = contract_last(d_attended, full_out).astype(jnp.bfloat16)
    grad_context_h = split_heads(d_context, head_count)
    queries_h = saved["queries_h"]
    log_total = saved["log_total"]
    block_list = saved["block_list"]
    score_list = saved["score_list"]
    active_list = saved["active_list"]
    delta_rows = jnp.zeros_like(log_total)
    for block_index in range(tree_blocks):
        values_here = split_heads(block_list[block_index][1], head_count)
        scores_now = score_list[block_index]

        def delta_term(scores_now=scores_now, values_here=values_here):
            prob_rows = jnp.exp(scores_now - log_total[..., None])
            grad_probs = jnp.einsum(
                "qhd,khd->hqk", grad_context_h, values_here, preferred_element_type=jnp.float32
            )
            return jnp.sum(prob_rows * grad_probs, axis=-1)

        delta_rows = delta_rows + lax.cond(
            active_list[block_index], delta_term, lambda: jnp.zeros_like(log_total)
        )
    grad_queries = jnp.zeros((tok_dev, head_count, HEAD_DIM), jnp.float32)
    block_shape = (2, tok_dev * rep_size, model_width)
    returned = jnp.zeros(block_shape, jnp.float32)
    for block_index in range(tree_blocks):
        keys_here = split_heads(block_list[block_index][0], head_count)
        values_here = split_heads(block_list[block_index][1], head_count)
        scores_now = score_list[block_index]

        def block_grads(scores_now=scores_now, keys_here=keys_here, values_here=values_here):
            prob_rows = jnp.exp(scores_now - log_total[..., None])
            grad_probs = jnp.einsum(
                "qhd,khd->hqk", grad_context_h, values_here, preferred_element_type=jnp.float32
            )
            grad_scores = (prob_rows * (grad_probs - delta_rows[..., None])).astype(jnp.bfloat16)
            grad_q = (
                jnp.einsum(
                    "hqk,khd->qhd", grad_scores, keys_here, preferred_element_type=jnp.float32
                )
                * score_scale
            )
            grad_k = (
                jnp.einsum(
                    "hqk,qhd->khd", grad_scores, queries_h, preferred_element_type=jnp.float32
                )
                * score_scale
            )
            grad_v = jnp.einsum(
                "hqk,qhd->khd",
                prob_rows.astype(jnp.bfloat16),
                grad_context_h,
                preferred_element_type=jnp.float32,
            )
            key_count = grad_k.shape[0]
            return (
                grad_q,
                jnp.stack(
                    [grad_k.reshape(key_count, model_width), grad_v.reshape(key_count, model_width)]
                ),
            )

        def skip_grads():
            return (jnp.zeros_like(grad_queries), jnp.zeros(block_shape, jnp.float32))

        grad_q_now, grad_kv_now = lax.cond(active_list[block_index], block_grads, skip_grads)
        grad_queries = grad_queries + grad_q_now
        if block_index == 0:
            returned = grad_kv_now
        else:
            returned = returned + shifted(
                grad_kv_now.astype(jnp.bfloat16), "fsdp", -block_index
            ).astype(grad_kv_now.dtype)
    own_grads = lax.psum_scatter(
        returned.astype(jnp.bfloat16), "rep", scatter_dimension=1, tiled=True
    ).astype(jnp.float32)
    d_queries = grad_queries.reshape(tok_dev, model_width).astype(jnp.bfloat16)
    d_keys = own_grads[0].astype(jnp.bfloat16)
    d_values = own_grads[1].astype(jnp.bfloat16)
    d_norm_one = (
        contract_last(d_queries, full_query)
        + contract_last(d_keys, full_key)
        + contract_last(d_values, full_value)
    )
    unused_first, norm_one_back = jax.vjp(
        layer_norm, saved["residual_in"], gain_one.astype(jnp.float32), bias_one.astype(jnp.float32)
    )
    d_in_norm, grad_gain_one, grad_bias_one = norm_one_back(d_norm_one)
    grad_inputs = d_residual + d_in_norm
    norm_one = saved["norm_one"]
    context_low = saved["context_low"]
    norm_two = saved["norm_two"]
    active_low = saved["active_low"]
    ff_width = w_up.shape[1]
    all_grads = lax.psum_scatter(
        jnp.concatenate(
            [
                contract_first(norm_one, d_queries),
                contract_first(norm_one, d_keys),
                contract_first(norm_one, d_values),
                contract_first(context_low, d_attended),
                contract_first(norm_two, d_upward),
                contract_first(cotangent, active_low),
            ],
            axis=1,
        ),
        ("fsdp", "rep"),
        scatter_dimension=0,
        tiled=True,
    )
    up_start = 4 * model_width
    grad_wq = all_grads[:, 0:model_width]
    grad_wk = all_grads[:, model_width : 2 * model_width]
    grad_wv = all_grads[:, 2 * model_width : 3 * model_width]
    grad_wo = all_grads[:, 3 * model_width : 4 * model_width]
    grad_wu = all_grads[:, up_start : up_start + ff_width]
    grad_wd = all_grads[:, up_start + ff_width : up_start + 2 * ff_width]
    small = (
        lax.psum_scatter(grad_gain_one, ("fsdp", "rep"), scatter_dimension=0, tiled=True),
        lax.psum_scatter(grad_bias_one, ("fsdp", "rep"), scatter_dimension=0, tiled=True),
        lax.psum_scatter(
            jnp.sum(d_queries.astype(jnp.float32), axis=0),
            ("fsdp", "rep"),
            scatter_dimension=0,
            tiled=True,
        ),
        lax.psum_scatter(
            jnp.sum(d_values.astype(jnp.float32), axis=0),
            ("fsdp", "rep"),
            scatter_dimension=0,
            tiled=True,
        ),
        lax.psum_scatter(
            jnp.sum(d_attended.astype(jnp.float32), axis=0),
            ("fsdp", "rep"),
            scatter_dimension=0,
            tiled=True,
        ),
        lax.psum_scatter(grad_gain_two, ("fsdp", "rep"), scatter_dimension=0, tiled=True),
        lax.psum_scatter(grad_bias_two, ("fsdp", "rep"), scatter_dimension=0, tiled=True),
        lax.psum_scatter(
            jnp.sum(d_upward.astype(jnp.float32), axis=0),
            ("fsdp", "rep"),
            scatter_dimension=0,
            tiled=True,
        ),
        lax.psum_scatter(
            jnp.sum(grad_out_f, axis=0), ("fsdp", "rep"), scatter_dimension=0, tiled=True
        ),
    )
    return (
        layer_output,
        grad_inputs,
        small[0],
        small[1],
        grad_wq,
        small[2],
        grad_wk,
        grad_wv,
        small[3],
        grad_wo,
        small[4],
        small[5],
        small[6],
        grad_wu,
        small[7],
        grad_wd,
        small[8],
    )


def solution(mesh):
    in_specs = (
        P(("fsdp", "rep"), None),
        P(("fsdp", "rep")),
        P(("fsdp", "rep")),
        P(("fsdp", "rep"), None),
        P(("fsdp", "rep")),
        P(("fsdp", "rep"), None),
        P(("fsdp", "rep"), None),
        P(("fsdp", "rep")),
        P(("fsdp", "rep"), None),
        P(("fsdp", "rep")),
        P(("fsdp", "rep")),
        P(("fsdp", "rep")),
        P(("fsdp", "rep"), None),
        P(("fsdp", "rep")),
        P(("fsdp", "rep"), None),
        P(("fsdp", "rep")),
        P(),
        P(("fsdp", "rep"), None),
    )
    out_specs = (
        P(("fsdp", "rep"), None),
        P(("fsdp", "rep"), None),
        P(("fsdp", "rep")),
        P(("fsdp", "rep")),
        P(("fsdp", "rep"), None),
        P(("fsdp", "rep")),
        P(("fsdp", "rep"), None),
        P(("fsdp", "rep"), None),
        P(("fsdp", "rep")),
        P(("fsdp", "rep"), None),
        P(("fsdp", "rep")),
        P(("fsdp", "rep")),
        P(("fsdp", "rep")),
        P(("fsdp", "rep"), None),
        P(("fsdp", "rep")),
        P(("fsdp", "rep"), None),
        P(("fsdp", "rep")),
    )
    return jax.shard_map(body, mesh=mesh, in_specs=in_specs, out_specs=out_specs, check_vma=False)
```

profile of v0, /device:TPU:0, one launch (start us, length us, event | category | flops | bytes accessed | tf_op | source)
XLA Modules:
  0.0 4473.1 jit_solution(14044280007804363002)
XLA Ops:
  15.5 42.9 all-reduce.26
  61.6 29.6 all-gather.17.cloned.1.call-done
  96.1 74.1 %all-gather.19.cloned.1.call-done = bf16[2048,2048]{1,0:T(8,128)(2,1)} async-done(((bf16[64,2048]{1,0:T(8,128)(2,1)}), bf16[2048,2048]{1,0:T(8,128)(2,1)}) %all-gather.19.cloned.1.call-update) | async-done | bytes 8388624 | tf_op jit(solution)/shard_map/all_gather | solution.py:51
  178.6 29.3 all-gather.21.cloned.1.call-done
  226.5 36.7 collective-permute-done.1
  263.3 40.3 collective-permute-start.3
  303.6 40.5 collective-permute-start.2
  349.7 314.1 %all-gather = bf16[32,1,256]{2,1,0:T(2,128)(2,1)S(1)} all-gather(bf16[1,1,256]{2,1,0:T(2,128)(2,1)S(1)} %reshape.443), channel_id=1, replica_groups=mesh['fsdp'=16,'rep'=2] {'fsdp','rep'}, dimensions={0}, use_global_device_ids=true | all-gather | bytes 16896 | tf_op jit(solution)/shard_map/all_gather | solution.py:60
  732.9 38.7 all-gather.27.cloned.1.call-done
  771.6 254.8 %all-gather.29.cloned.1.call-done = bf16[2048,8192]{1,0:T(8,128)(2,1)} async-done(((bf16[64,8192]{1,0:T(8,128)(2,1)}), bf16[2048,8192]{1,0:T(8,128)(2,1)}) %all-gather.29.cloned.1.call-update) | async-done | bytes 33554448 | tf_op jit(solution)/shard_map/all_gather | solution.py:59
  1026.4 26.5 fusion.150
  1055.7 82.1 %all-reduce.25 = (bf16[2048]{0:T(1024)(128)(2,1)S(1)}, bf16[2048]{0:T(1024)(128)(2,1)S(1)}, bf16[2048]{0:T(1024)(128)(2,1)S(1)}, bf16[2048]{0:T(1024)(128)(2,1)S...) all-reduce(bf16[2048]{0:T(1024)(128)(2,1)S(1)} %dynamic-update-slic, ...), channel_id=1, replica_groups=mesh['fsdp'=16,'rep'=2] {'fsdp','rep'}, use_global_device_ids=true, to_apply=%add.10 | all-reduce | flops 14336 | bytes 57344
  1137.8 34.7 all-gather.35.cloned.1.call-done
  1177.2 74.2 %all-gather.37.cloned.1.call-done = bf16[2048,2048]{1,0:T(8,128)(2,1)} async-done(((bf16[64,2048]{1,0:T(8,128)(2,1)}), bf16[2048,2048]{1,0:T(8,128)(2,1)}) %all-gather.37.cloned.1.call-update) | async-done | bytes 8388624 | tf_op jit(solution)/shard_map/all_gather | solution.py:51
  1259.9 29.2 all-gather.39.cloned.1.call-done
  1307.6 314.5 %all-gather.1 = bf16[32,1,256]{2,1,0:T(2,128)(2,1)S(1)} all-gather(bf16[1,1,256]{2,1,0:T(2,128)(2,1)S(1)} %reshape.445), channel_id=1, replica_groups=mesh['fsdp'=16,'rep'=2] {'fsdp','rep'}, dimensions={0}, use_global_device_ids=true | all-gather | bytes 16896 | tf_op jit(solution)/shard_map/all_gather | solution.py:60
  1622.2 270.7 %collective-permute-start.8 = (bf16[2,256,2048]{2,1,0:T(8,128)(2,1)}, bf16[2,256,2048]{2,1,0:T(8,128)(2,1)}, u32[]{:S(2)}, u32[]{:S(2)}) collective-permute-start(bf16[2,256,2048]{2,1,0:T(8,128)(2,1)} %all-gather.39.cloned.1.call-done), channel_id=1, source_target_pairs={{0,4},{2,6},{4,8},{6,10},{8,12},{10,14},{12,16},{14,18},{16,20},{1... | collective-permute-start | bytes 6291464 | tf_op jit(solution)/shard_map/ppermute | solution.py:19
  1930.2 19.5 collective-permute-done.8
  2004.1 20.0 convolution_add_fusion
  2024.1 95.4 %all-gather.31.cloned.1.call-done = bf16[2048,8192]{1,0:T(8,128)(2,1)} async-done(((bf16[64,8192]{1,0:T(8,128)(2,1)}), bf16[2048,8192]{1,0:T(8,128)(2,1)}) %all-gather.31.cloned.1.call-update) | async-done | bytes 33554448 | tf_op jit(solution)/shard_map/all_gather | solution.py:59
  2119.5 18.0 convert_reduce_fusion
  2137.5 19.8 multiply_reduce_fusion.8
  2197.8 76.2 %collective-permute-done.15 = bf16[2,256,2048]{1,2,0:T(8,128)(2,1)} collective-permute-done((bf16[2,256,2048]{1,2,0:T(8,128)(2,1)}, bf16[2,256,2048]{1,2,0:T(8,128)(2,1)}, u32[]{:S(2)}, u32[]{:S(2)}) %collective-permute-start.15) | collective-permute-done | bytes 2097184 | tf_op jit(solution)/shard_map/ppermute | solution.py:19
  2275.3 13.5 conditional.88
  2288.8 95.0 %collective-permute-done.17 = bf16[2,256,2048]{1,2,0:T(8,128)(2,1)} collective-permute-done((bf16[2,256,2048]{1,2,0:T(8,128)(2,1)}, bf16[2,256,2048]{1,2,0:T(8,128)(2,1)}, u32[]{:S(2)}, u32[]{:S(2)}) %collective-permute-start.17) | collective-permute-done | bytes 2097184 | tf_op jit(solution)/shard_map/ppermute | solution.py:19
  2388.2 16.7 collective-permute-done.19
  2404.9 18.6 collective-permute-done.20
  2460.7 199.3 %reduce-scatter.7.cloned.1.call-done = bf16[128,4096]{1,0:T(8,128)(2,1)} async-done(((bf16[256,4096]{1,0:T(8,128)(2,1)}), bf16[128,4096]{1,0:T(8,128)(2,1)}) %reduce-scatter.7.cloned.1.call-update) | async-done | bytes 1048592
  2711.6 23.4 convolution_dynamic-update-slice_fusion
  2735.1 25.6 bitcast_dynamic-update-slice_fusion
  2760.7 99.7 %all-reduce.29.cloned.1.call-done = (f32[2048]{0:T(1024)}, f32[2048]{0:T(1024)}, f32[2048]{0:T(1024)}, f32[2048]{0:T(1024)}, f32[2048]{0:T(1024)}, /*index=5*/f3...) async-done(((f32[2048]{0:T(1024)}, f32[2048]{0:T(1024)}, f32[2048]{0:T(1024)}, f32[2048]{0:T(1024)}, f32[2048]{0:T(1024)}, /*index=5*/f32[2048]{0:T(1024)}, ...) | async-done | bytes 98320
  2871.8 1587.2 %reduce-scatter.5.cloned.1.call-done = f32[64,24576]{1,0:T(8,128)} async-done(((f32[2048,24576]{1,0:T(8,128)}), f32[64,24576]{1,0:T(8,128)}) %reduce-scatter.5.cloned.1.call-update) | async-done | bytes 6291472 | tf_op jit(solution)/shard_map/reduce_scatter | solution.py:346
  (494 shorter events, 476.8 us)
Async XLA Ops:
  7.9 162.3 %all-gather.19.cloned.1.call-start = ((), (), s32[]{:S(2)}) async-start(), calls=%async_computation.3 | async-start | bytes 8650752 | tf_op jit(solution)/shard_map/all_gather | solution.py:51
  8.7 199.2 %all-gather.21.cloned.1.call-start = ((), (), s32[]{:S(2)}) async-start(), calls=%async_computation.4 | async-start | bytes 3145728 | tf_op jit(solution)/shard_map/all_gather | solution.py:107
  176.1 494.8 %all-gather.23.cloned.1.call-start = ((), (), s32[]{:S(2)}) async-start(), calls=%async_computation.5 | async-start | bytes 8650752 | tf_op jit(solution)/shard_map/all_gather | solution.py:49
  176.6 551.2 %all-gather.25.cloned.1.call-start = ((), (), s32[]{:S(2)}) async-start(), calls=%async_computation.6 | async-start | bytes 8650752 | tf_op jit(solution)/shard_map/all_gather | solution.py:52
  177.2 594.4 %all-gather.27.cloned.1.call-start = ((), (), s32[]{:S(2)}) async-start(), calls=%async_computation.7 | async-start | bytes 34603008 | tf_op jit(solution)/shard_map/all_gather | solution.py:58
  177.8 848.6 %all-gather.29.cloned.1.call-start = ((), (), s32[]{:S(2)}) async-start(), calls=%async_computation.8 | async-start | bytes 34603008 | tf_op jit(solution)/shard_map/all_gather | solution.py:59
  178.6 994.0 %all-gather.35.cloned.1.call-start = ((), (), s32[]{:S(2)}) async-start(), calls=%async_computation.11 | async-start | bytes 8650752 | tf_op jit(solution)/shard_map/all_gather | solution.py:50
  214.4 484.2 %collective-permute-start.6 = (bf16[2,256,2048]{2,1,0:T(8,128)(2,1)}, bf16[2,256,2048]{2,1,0:T(8,128)(2,1)}, u32[]{:S(2)}, u32[]{:S(2)}) collective-permute-start(bf16[2,256,2048]{2,1,0:T(8,128)(2,1)} %all-gather.21.cloned.1.call-done), channel_id=1, source_target_pairs={{0,14},{2,16},{4,18},{6,20},{8,22},{10,24},{12,26},{14,28},{16,30}... | collective-permute-start | bytes 6291464 | tf_op jit(solution)/shard_map/ppermute | solution.py:19
  220.2 476.3 %collective-permute-start.5 = (bf16[2,256,2048]{2,1,0:T(8,128)(2,1)}, bf16[2,256,2048]{2,1,0:T(8,128)(2,1)}, u32[]{:S(2)}, u32[]{:S(2)}) collective-permute-start(bf16[2,256,2048]{2,1,0:T(8,128)(2,1)} %all-gather.21.cloned.1.call-done), channel_id=1, source_target_pairs={{0,12},{2,14},{4,16},{6,18},{8,20},{10,22},{12,24},{14,26},{16,28}... | collective-permute-start | bytes 6291464 | tf_op jit(solution)/shard_map/ppermute | solution.py:19
  223.9 470.3 %collective-permute-start.4 = (bf16[2,256,2048]{2,1,0:T(8,128)(2,1)}, bf16[2,256,2048]{2,1,0:T(8,128)(2,1)}, u32[]{:S(2)}, u32[]{:S(2)}) collective-permute-start(bf16[2,256,2048]{2,1,0:T(8,128)(2,1)} %all-gather.21.cloned.1.call-done), channel_id=1, source_target_pairs={{0,10},{2,12},{4,14},{6,16},{8,18},{10,20},{12,22},{14,24},{16,26}... | collective-permute-start | bytes 6291464 | tf_op jit(solution)/shard_map/ppermute | solution.py:19
  263.3 428.9 %collective-permute-start.3 = (bf16[2,256,2048]{2,1,0:T(8,128)(2,1)}, bf16[2,256,2048]{2,1,0:T(8,128)(2,1)}, u32[]{:S(2)}, u32[]{:S(2)}) collective-permute-start(bf16[2,256,2048]{2,1,0:T(8,128)(2,1)} %all-gather.21.cloned.1.call-done), channel_id=1, source_target_pairs={{0,8},{2,10},{4,12},{6,14},{8,16},{10,18},{12,20},{14,22},{16,24},... | collective-permute-start | bytes 6291464 | tf_op jit(solution)/shard_map/ppermute | solution.py:19
  303.6 386.4 %collective-permute-start.2 = (bf16[2,256,2048]{2,1,0:T(8,128)(2,1)}, bf16[2,256,2048]{2,1,0:T(8,128)(2,1)}, u32[]{:S(2)}, u32[]{:S(2)}) collective-permute-start(bf16[2,256,2048]{2,1,0:T(8,128)(2,1)} %all-gather.21.cloned.1.call-done), channel_id=1, source_target_pairs={{0,6},{2,8},{4,10},{6,12},{8,14},{10,16},{12,18},{14,20},{16,22},{... | collective-permute-start | bytes 6291464 | tf_op jit(solution)/shard_map/ppermute | solution.py:19
  1053.0 198.5 %all-gather.37.cloned.1.call-start = ((), (), s32[]{:S(2)}) async-start(), calls=%async_computation.12 | async-start | bytes 8650752 | tf_op jit(solution)/shard_map/all_gather | solution.py:51
  1053.7 235.4 %all-gather.39.cloned.1.call-start = ((), (), s32[]{:S(2)}) async-start(), calls=%async_computation.13 | async-start | bytes 3145728 | tf_op jit(solution)/shard_map/all_gather | solution.py:107
  1257.2 635.7 %all-gather.33.cloned.1.call-start = ((), (), s32[]{:S(2)}) async-start(), calls=%async_computation.10 | async-start | bytes 8650752 | tf_op jit(solution)/shard_map/all_gather | solution.py:49
  1258.0 739.9 %all-gather.41.cloned.1.call-start = ((), (), s32[]{:S(2)}) async-start(), calls=%async_computation.14 | async-start | bytes 8650752 | tf_op jit(solution)/shard_map/all_gather | solution.py:52
  1258.5 745.6 %all-gather.43.cloned.1.call-start = ((), (), s32[]{:S(2)}) async-start(), calls=%async_computation.15 | async-start | bytes 34603008 | tf_op jit(solution)/shard_map/all_gather | solution.py:58
  1259.3 860.2 %all-gather.31.cloned.1.call-start = ((), (), s32[]{:S(2)}) async-start(), calls=%async_computation.9 | async-start | bytes 34603008 | tf_op jit(solution)/shard_map/all_gather | solution.py:59
  1259.9 1400.2 %reduce-scatter.7.cloned.1.call-start = ((), (), s32[]{:S(2)}) async-start(), calls=%async_computation.17 | async-start | bytes 3145728
  1289.1 333.1 %collective-permute-start.13 = (bf16[2,256,2048]{2,1,0:T(8,128)(2,1)}, bf16[2,256,2048]{2,1,0:T(8,128)(2,1)}, u32[]{:S(2)}, u32[]{:S(2)}) collective-permute-start(bf16[2,256,2048]{2,1,0:T(8,128)(2,1)} %all-gather.39.cloned.1.call-done), channel_id=1, source_target_pairs={{0,14},{2,16},{4,18},{6,20},{8,22},{10,24},{12,26},{14,28},{16,30}... | collective-permute-start | bytes 6291464 | tf_op jit(solution)/shard_map/ppermute | solution.py:19
  1294.1 603.7 %collective-permute-start.12 = (bf16[2,256,2048]{2,1,0:T(8,128)(2,1)}, bf16[2,256,2048]{2,1,0:T(8,128)(2,1)S(1)}, u32[]{:S(2)}, u32[]{:S(2)}) collective-permute-start(bf16[2,256,2048]{2,1,0:T(8,128)(2,1)} %all-gather.39.cloned.1.call-done), channel_id=1, source_target_pairs={{0,12},{2,14},{4,16},{6,18},{8,20},{10,22},{12,24},{14,26},{16,28}... | collective-permute-start | bytes 6291464 | tf_op jit(solution)/shard_map/ppermute | solution.py:19
  1298.5 618.9 %collective-permute-start.11 = (bf16[2,256,2048]{2,1,0:T(8,128)(2,1)}, bf16[2,256,2048]{2,1,0:T(8,128)(2,1)}, u32[]{:S(2)}, u32[]{:S(2)}) collective-permute-start(bf16[2,256,2048]{2,1,0:T(8,128)(2,1)} %all-gather.39.cloned.1.call-done), channel_id=1, source_target_pairs={{0,10},{2,12},{4,14},{6,16},{8,18},{10,20},{12,22},{14,24},{16,26}... | collective-permute-start | bytes 6291464 | tf_op jit(solution)/shard_map/ppermute | solution.py:19
  1301.3 620.4 %collective-permute-start.10 = (bf16[2,256,2048]{2,1,0:T(8,128)(2,1)}, bf16[2,256,2048]{2,1,0:T(8,128)(2,1)}, u32[]{:S(2)}, u32[]{:S(2)}) collective-permute-start(bf16[2,256,2048]{2,1,0:T(8,128)(2,1)} %all-gather.39.cloned.1.call-done), channel_id=1, source_target_pairs={{0,8},{2,10},{4,12},{6,14},{8,16},{10,18},{12,20},{14,22},{16,24},... | collective-permute-start | bytes 6291464 | tf_op jit(solution)/shard_map/ppermute | solution.py:19
  1303.9 621.9 %collective-permute-start.9 = (bf16[2,256,2048]{2,1,0:T(8,128)(2,1)}, bf16[2,256,2048]{2,1,0:T(8,128)(2,1)}, u32[]{:S(2)}, u32[]{:S(2)}) collective-permute-start(bf16[2,256,2048]{2,1,0:T(8,128)(2,1)} %all-gather.39.cloned.1.call-done), channel_id=1, source_target_pairs={{0,6},{2,8},{4,10},{6,12},{8,14},{10,16},{12,18},{14,20},{16,22},{... | collective-permute-start | bytes 6291464 | tf_op jit(solution)/shard_map/ppermute | solution.py:19
  1622.2 327.5 %collective-permute-start.8 = (bf16[2,256,2048]{2,1,0:T(8,128)(2,1)}, bf16[2,256,2048]{2,1,0:T(8,128)(2,1)}, u32[]{:S(2)}, u32[]{:S(2)}) collective-permute-start(bf16[2,256,2048]{2,1,0:T(8,128)(2,1)} %all-gather.39.cloned.1.call-done), channel_id=1, source_target_pairs={{0,4},{2,6},{4,8},{6,10},{8,12},{10,14},{12,16},{14,18},{16,20},{1... | collective-permute-start | bytes 6291464 | tf_op jit(solution)/shard_map/ppermute | solution.py:19
  2182.2 106.6 %collective-permute-start.16 = (bf16[2,256,2048]{1,2,0:T(8,128)(2,1)}, bf16[2,256,2048]{1,2,0:T(8,128)(2,1)}, u32[]{:S(2)}, u32[]{:S(2)}) collective-permute-start(bf16[2,256,2048]{1,2,0:T(8,128)(2,1)} %get-tuple-element.874), channel_id=1, source_target_pairs={{6,0},{8,2},{10,4},{12,6},{14,8},{16,10},{18,12},{20,14},{22,16},{... | collective-permute-start | bytes 6291464 | tf_op jit(solution)/shard_map/ppermute | solution.py:19
  2186.0 197.8 %collective-permute-start.17 = (bf16[2,256,2048]{1,2,0:T(8,128)(2,1)}, bf16[2,256,2048]{1,2,0:T(8,128)(2,1)}, u32[]{:S(2)}, u32[]{:S(2)}) collective-permute-start(bf16[2,256,2048]{1,2,0:T(8,128)(2,1)} %get-tuple-element.875), channel_id=1, source_target_pairs={{8,0},{10,2},{12,4},{14,6},{16,8},{18,10},{20,12},{22,14},{24,16},... | collective-permute-start | bytes 6291464 | tf_op jit(solution)/shard_map/ppermute | solution.py:19
  2189.9 198.3 %collective-permute-start.18 = (bf16[2,256,2048]{1,2,0:T(8,128)(2,1)}, bf16[2,256,2048]{1,2,0:T(8,128)(2,1)}, u32[]{:S(2)}, u32[]{:S(2)}) collective-permute-start(bf16[2,256,2048]{1,2,0:T(8,128)(2,1)} %get-tuple-element.876), channel_id=1, source_target_pairs={{10,0},{12,2},{14,4},{16,6},{18,8},{20,10},{22,12},{24,14},{26,16}... | collective-permute-start | bytes 6291464 | tf_op jit(solution)/shard_map/ppermute | solution.py:19
  2196.5 208.4 %collective-permute-start.19 = (bf16[2,256,2048]{1,2,0:T(8,128)(2,1)}, bf16[2,256,2048]{1,2,0:T(8,128)(2,1)}, u32[]{:S(2)}, u32[]{:S(2)}) collective-permute-start(bf16[2,256,2048]{1,2,0:T(8,128)(2,1)} %get-tuple-element.877), channel_id=1, source_target_pairs={{12,0},{14,2},{16,4},{18,6},{20,8},{22,10},{24,12},{26,14},{28,16}... | collective-permute-start | bytes 6291464 | tf_op jit(solution)/shard_map/ppermute | solution.py:19
  2274.0 149.4 %collective-permute-start.20 = (bf16[2,256,2048]{1,2,0:T(8,128)(2,1)}, bf16[2,256,2048]{1,2,0:T(8,128)(2,1)}, u32[]{:S(2)}, u32[]{:S(2)}) collective-permute-start(bf16[2,256,2048]{1,2,0:T(8,128)(2,1)} %get-tuple-element.878), channel_id=1, source_target_pairs={{14,0},{16,2},{18,4},{20,6},{22,8},{24,10},{26,12},{28,14},{30,16}... | collective-permute-start | bytes 6291464 | tf_op jit(solution)/shard_map/ppermute | solution.py:19
  2439.8 420.6 %all-reduce.29.cloned.1.call-start = ((), (), s32[]{:S(2)}) async-start(), calls=%async_computation.18 | async-start | bytes 196608
  2735.0 1723.9 %reduce-scatter.5.cloned.1.call-start = ((), (), s32[]{:S(2)}) async-start(), calls=%async_computation.16 | async-start | bytes 207618048 | tf_op jit(solution)/shard_map/reduce_scatter | solution.py:346
  (63 other events, 6792.1 us)
Sparse Core Ops, SparseCore 0:
  11.0 80.1 all-gather.16
  94.2 75.9 all-gather.18
  176.2 31.6 all-gather.20
  210.8 105.8 all-gather.22
  319.4 183.1 all-gather.24
  505.5 266.0 all-gather.26
  774.6 251.7 all-gather.28
  1053.1 119.3 all-gather.34
  1175.5 75.8 all-gather.36
  1257.3 31.6 all-gather.38
  1292.1 186.0 all-gather.32
  1481.0 128.4 all-gather.40
  1612.5 239.6 all-gather.42
  1855.1 264.3 all-gather.30
  2439.9 220.1 reduce-scatter.6
  2735.1 125.1 all-reduce.28
  2866.6 1592.2 reduce-scatter.4
where the time goes:
time: 4490 us; the launch traced here: 4470 us
  waiting for transfers between devices  2820 us (63%)
  blocking collectives  754 us (17%)
  starting transfers between devices  403 us (9%)
  matrix products  251 us (6%)
  local copies, waits for them, and re-layouts  167 us (4%)
  other arithmetic  52.7 us (1%)
    reduce_scatter x1, waiting for transfers between devices, body(): lax.psum_scatter(jnp.concatenate([contract_first(norm_one, d_queries), co...  1590 us
    all_gather x2, blocking collectives, gather_params(): lax.all_gather(b_up, ('fsdp', 'rep'), axis=0, tiled=True)  629 us
    ppermute x21, starting transfers between devices, shifted(): lax.ppermute(value, axis, [(source, source + steps) for source in range(l...  402 us
    all_gather x2, waiting for transfers between devices, gather_params(): lax.all_gather(w_down, ('fsdp', 'rep'), axis=0, tiled=True)  350 us
    unnamed x19, waiting for transfers between devices  306 us
    ppermute x21, waiting for transfers between devices, shifted(): lax.ppermute(value, axis, [(source, source + steps) for source in range(l...  267 us
    all_gather x2, waiting for transfers between devices, gather_params(): lax.all_gather(w_value, ('fsdp', 'rep'), axis=0, tiled=True)  148 us
    unnamed x2, blocking collectives  125 us
  transfers between devices with their start and end apart: 38, of which 19 were waited for; matrix products, arithmetic and copies ran while one was open for 6% of the time, Pallas kernels for 0%

commit v1 on v0

v1 whole, which is shorter than its diff:
```python
import functools

import jax
import jax.numpy as jnp
from jax import lax
from jax.experimental import pallas as pl
from jax.experimental.pallas import tpu as pltpu
from jax.sharding import Mesh, PartitionSpec as P

HEAD_DIM = 128
TRUNK_SEGS = 4
TREE_SEGS = 16
EPS = 1e-05
GROUP = ("blk", "rep")
ALL = ("tree", "blk", "rep")
f32 = jnp.float32
bf16 = jnp.bfloat16


def dot(a, b, ca, cb):
    return lax.dot_general(a, b, (((ca,), (cb,)), ((), ())), preferred_element_type=f32)


MESH = pl.DeviceIdType.MESH
X, Y, Z = 1, 2, 4
ORDERS = ((X, Y, Z), (Y, Z, X), (Z, X, Y))


class Place:
    def __init__(self):
        self.tree = lax.axis_index("tree")
        blk = lax.axis_index("blk")
        self.x = lax.axis_index("rep")
        self.c = lax.rem(blk, 2)
        self.y = lax.rem(blk // 2, 2)
        self.z = blk // 4

    def flipped(self, r, other=0):
        flip = lambda v, on: 1 - v if on else v
        return flip(self.z, r & Z), flip(self.y, r & Y), flip(self.c, other), flip(self.x, r & X)

    def device(self, r, other=0):
        z, y, c, x = self.flipped(r, other)
        return (self.tree, (z * 2 + y) * 2 + c, x)

    def index(self, r, other=0):
        z, y, c, x = self.flipped(r, other)
        return ((z * 2 + y) * 2 + c) * 2 + x


def greet(place):
    barrier = pltpu.get_barrier_semaphore()
    for r, other in ((X, 0), (Y, 0), (Z, 0), (0, 1)):
        pl.semaphore_signal(barrier, inc=1, device_id=place.device(r, other), device_id_type=MESH)
    pl.semaphore_wait(barrier, 4)


def part_columns(width):
    tiles = width // 128
    first = tiles - 2 * (tiles // 3)
    cuts = (0, first, first + tiles // 3, tiles)
    return [(cuts[p] * 128, (cuts[p + 1] - cuts[p]) * 128) for p in range(3)]


def gather_kernel(x_ref, o_ref, send, recv, psend, precv, local):
    place = Place()
    tok, width = x_ref.shape
    cols = part_columns(width)
    greet(place)

    def rows(r, other=0):
        return pl.ds(pl.multiple_of(place.index(r, other) * tok, tok), tok)

    def remote(src, r, p, dim):
        lo, n = cols[p]
        slot = r | dim
        return pltpu.make_async_remote_copy(
            src_ref=src, dst_ref=o_ref.at[rows(r), pl.ds(lo, n)],
            send_sem=send.at[p, slot - 1], recv_sem=recv.at[p, slot - 1],
            device_id=place.device(dim), device_id_type=MESH,
        )

    def pair(r, p):
        lo, n = cols[p]
        src = o_ref.at[rows(r), pl.ds(lo, n)]
        return pltpu.make_async_remote_copy(
            src_ref=src, dst_ref=src, send_sem=psend.at[p, r], recv_sem=precv.at[p, r],
            device_id=place.device(0, 1), device_id_type=MESH,
        )

    started = []
    own = [x_ref.at[:, pl.ds(lo, n)] for lo, n in cols]
    for step in range(3):
        for p in range(3):
            copy = remote(own[p], 0, p, ORDERS[p][step])
            copy.start()
            started.append(copy)
    keep = pltpu.make_async_copy(x_ref, o_ref.at[rows(0)], local)
    keep.start()
    for p in range(3):
        lo, n = cols[p]
        copy = pltpu.make_async_remote_copy(
            src_ref=own[p], dst_ref=o_ref.at[rows(0), pl.ds(lo, n)], send_sem=psend.at[p, 0], recv_sem=precv.at[p, 0],
            device_id=place.device(0, 1), device_id_type=MESH,
        )
        copy.start()
        started.append(copy)

    def arrived(p, slot):
        lo, n = cols[p]
        ref = o_ref.at[rows(slot), pl.ds(lo, n)]
        pltpu.make_async_remote_copy(
            src_ref=ref, dst_ref=ref, send_sem=send.at[p, slot - 1], recv_sem=recv.at[p, slot - 1],
            device_id=place.device(X), device_id_type=MESH,
        ).wait_recv()

    for which in ((1, 0, 0), (0, 1, 0), (1, 1, 0), (0, 0, 1), (1, 0, 1), (0, 1, 1), (1, 1, 1)):
        for p in range(3):
            dims = ORDERS[p]
            slot = sum(d for d, on in zip(dims, which) if on)
            arrived(p, slot)
            lo, n = cols[p]
            src = o_ref.at[rows(slot), pl.ds(lo, n)]
            top = max(j for j in range(3) if which[j])
            for j in range(top + 1, 3):
                copy = remote(src, slot, p, dims[j])
                copy.start()
                started.append(copy)
            copy = pair(slot, p)
            copy.start()
            started.append(copy)
    for copy in started:
        copy.wait_send()
    for p in range(3):
        lo, n = cols[p]
        for r in range(8):
            ref = o_ref.at[rows(r, 1), pl.ds(lo, n)]
            pltpu.make_async_remote_copy(
                src_ref=ref, dst_ref=ref, send_sem=psend.at[p, r], recv_sem=precv.at[p, r],
                device_id=place.device(0, 1), device_id_type=MESH,
            ).wait_recv()
    keep.wait()


def tree_gather(x, cid, name):
    tok, width = x.shape
    dma = pltpu.SemaphoreType.DMA
    return pl.pallas_call(
        gather_kernel,
        out_shape=jax.ShapeDtypeStruct((16 * tok, width), x.dtype),
        in_specs=[pl.BlockSpec(memory_space=pl.ANY)],
        out_specs=pl.BlockSpec(memory_space=pl.ANY),
        scratch_shapes=[dma((3, 7)), dma((3, 7)), dma((3, 8)), dma((3, 8)), dma],
        compiler_params=pltpu.CompilerParams(collective_id=cid, has_side_effects=True),
        cost_estimate=pl.CostEstimate(flops=0, bytes_accessed=64 * x.size, transcendentals=0),
        name=name,
    )(x)


def scatter_kernel(rhs_dim, tok, l_ref, r_ref, o_ref, acc, pout, pin, stage, inbox, psend, precv, send, recv):
    place = Place()
    width = o_ref.shape[1]
    cols = part_columns(width)
    greet(place)
    tile = 512

    def product(zy, other, put):
        z, y, c, _ = place.flipped(zy, other)
        start = pl.multiple_of(((z * 2 + y) * 2 + c) * 2 * tok, 2 * tok)

        def one(j):
            at = pl.multiple_of(j * tile, tile)
            left = l_ref[pl.ds(start, 2 * tok), :]
            if rhs_dim == 1:
                res = lax.dot_general(left, r_ref[pl.ds(at, tile), :], (((1,), (1,)), ((), ())), preferred_element_type=f32)
            else:
                res = lax.dot_general(left, r_ref[:, pl.ds(at, tile)], (((1,), (0,)), ((), ())), preferred_element_type=f32)
            put(at, res)

        pl.loop(0, width // tile)(one)

    def pair(k):
        return pltpu.make_async_remote_copy(
            src_ref=pout.at[k], dst_ref=pin.at[k], send_sem=psend.at[k], recv_sem=precv.at[k],
            device_id=place.device(0, 1), device_id_type=MESH,
        )

    groups = (Z | Y, Z, Y, 0)
    for k, zy in enumerate(groups):
        def put_out(at, res, k=k):
            pout[k, :, pl.ds(at, tile)] = res.astype(bf16)
        product(zy, 1, put_out)
        pair(k).start()

    def hop(p, r, step, slot):
        lo, n = cols[p]
        return pltpu.make_async_remote_copy(
            src_ref=stage.at[r - 1, :, pl.ds(lo, n)], dst_ref=inbox.at[slot, :, pl.ds(lo, n)],
            send_sem=send.at[p, r - 1], recv_sem=recv.at[p, slot],
            device_id=place.device(ORDERS[p][step]), device_id_type=MESH,
        )

    started = []
    for k, zy in enumerate(groups):
        def put_own(at, res, k=k):
            acc[k, :, pl.ds(at, tile)] = res
        product(zy, 0, put_own)
        pair(k).wait_recv()
        for rx in (X, 0):
            r = zy | rx
            xx = place.flipped(rx)[3]
            at = pl.ds(pl.multiple_of(xx * tok, tok), tok)
            for p in range(3):
                lo, n = cols[p]
                total = acc[k, at, pl.ds(lo, n)] + pin[k, at, pl.ds(lo, n)].astype(f32)
                first, second, third = ORDERS[p]
                if r & first:
                    stage[r - 1, :, pl.ds(lo, n)] = total.astype(bf16)
                    slot = 3 - (2 * bool(r & second) + bool(r & third))
                    copy = hop(p, r, 0, slot)
                    copy.start()
                    started.append(copy)
                else:
                    acc[k, at, pl.ds(lo, n)] = total

    def held(p, r):
        k = groups.index(r & (Z | Y))
        xx = place.flipped(r & X)[3]
        lo, n = cols[p]
        return acc[k, pl.ds(pl.multiple_of(xx * tok, tok), tok), pl.ds(lo, n)]

    def take(p, slot):
        lo, n = cols[p]
        hop(p, 1, 0, slot).wait_recv()
        return inbox[slot, :, pl.ds(lo, n)].astype(f32)

    for q in ((1, 1), (1, 0)):
        for p in range(3):
            first, second, third = ORDERS[p]
            lo, n = cols[p]
            r = second + third * q[1]
            stage[r - 1, :, pl.ds(lo, n)] = (held(p, r) + take(p, 3 - (2 * q[0] + q[1]))).astype(bf16)
            copy = hop(p, r, 1, 4 + (1 - q[1]))
            copy.start()
            started.append(copy)
    for p in range(3):
        third = ORDERS[p][2]
        lo, n = cols[p]
        stage[third - 1, :, pl.ds(lo, n)] = (held(p, third) + take(p, 2) + take(p, 4)).astype(bf16)
        copy = hop(p, third, 2, 6)
        copy.start()
        started.append(copy)
    for p in range(3):
        lo, n = cols[p]
        o_ref[:, pl.ds(lo, n)] = held(p, 0) + take(p, 3) + take(p, 5)
    for p in range(3):
        lo, n = cols[p]
        o_ref[:, pl.ds(lo, n)] += take(p, 6)
    for copy in started:
        copy.wait_send()
    for k in range(4):
        pair(k).wait_send()


def product_scatter(left, right, rhs_dim, cid, name):
    tokens = left.shape[0]
    width = right.shape[1 - rhs_dim]
    tok = tokens // 16
    dma = pltpu.SemaphoreType.DMA
    vmem = pl.BlockSpec(memory_space=pltpu.VMEM)
    return pl.pallas_call(
        functools.partial(scatter_kernel, rhs_dim, tok),
        out_shape=jax.ShapeDtypeStruct((tok, width), f32),
        in_specs=[vmem, vmem],
        out_specs=vmem,
        scratch_shapes=[
            pltpu.VMEM((4, 2 * tok, width), f32),
            pltpu.VMEM((4, 2 * tok, width), bf16),
            pltpu.VMEM((4, 2 * tok, width), bf16),
            pltpu.VMEM((7, tok, width), bf16),
            pltpu.VMEM((7, tok, width), bf16),
            dma((4,)), dma((4,)), dma((3, 7)), dma((3, 7)),
        ],
        compiler_params=pltpu.CompilerParams(collective_id=cid, has_side_effects=True, vmem_limit_bytes=48 * 2**20),
        cost_estimate=pl.CostEstimate(flops=2 * tokens * width * left.shape[1], bytes_accessed=64 * tok * width, transcendentals=0),
        name=name,
    )(left, right)


def norm_stats(v):
    mean = jnp.mean(v, axis=-1, keepdims=True)
    centred = v - mean
    root = lax.rsqrt(jnp.mean(centred * centred, axis=-1, keepdims=True) + EPS)
    return centred * root, root


def norm_back(d, n, root, gain):
    g = d * gain
    return root * (g - jnp.mean(g, axis=-1, keepdims=True) - n * jnp.mean(g * n, axis=-1, keepdims=True))


def gelu_pair(u):
    c = (2.0 / jnp.pi) ** 0.5
    t = jnp.tanh(c * (u + 0.044715 * u * u * u))
    act = 0.5 * u * (1.0 + t)
    der = 0.5 * (1.0 + t) + 0.5 * u * (1.0 - t * t) * c * (1.0 + 3 * 0.044715 * u * u)
    return act, der


def to_columns(w):
    rows, n = w.shape
    w = w.reshape(rows, TREE_SEGS, n // TREE_SEGS)
    w = lax.all_to_all(w, GROUP, split_axis=1, concat_axis=0, tiled=True)
    w = w.reshape(rows * TREE_SEGS, n // TREE_SEGS)
    return lax.all_gather(w, "tree", axis=0, tiled=True)


def to_rows(g, rows):
    g = lax.psum_scatter(g.astype(bf16), "tree", scatter_dimension=0, tiled=True)
    c = g.shape[1]
    g = g.reshape(TREE_SEGS, rows, c)
    g = lax.all_to_all(g, GROUP, split_axis=0, concat_axis=2, tiled=True)
    return g.reshape(rows, TREE_SEGS * c).astype(f32)


def visible_mask(parents, tok):
    tree = lax.axis_index("tree")
    own = tree * TREE_SEGS + jnp.arange(TREE_SEGS, dtype=jnp.int32)
    cur = own
    seen = jnp.zeros((TREE_SEGS, TREE_SEGS), jnp.bool_)
    for _ in range(TRUNK_SEGS + 1):
        up = jnp.take(parents, jnp.maximum(cur, 0))
        cur = jnp.where(cur >= 0, up, -1)
        seen = seen | (cur[:, None] == own[None, :])
    tri = jnp.arange(tok)[None, :] <= jnp.arange(tok)[:, None]
    full = seen[:, None, :, None] | (jnp.eye(TREE_SEGS, dtype=jnp.bool_)[:, None, :, None] & tri[None, :, None, :])
    return full.reshape(TREE_SEGS * tok, TREE_SEGS * tok)


def body(
    inputs, gain_one, bias_one, w_query, b_query, w_key, w_value, b_value, w_out, b_out,
    gain_two, bias_two, w_up, b_up, w_down, b_down, parents, cotangent,
):
    tok, width = inputs.shape
    rows = w_query.shape[0]
    ff = w_up.shape[1]
    trees = lax.axis_size("tree")
    me = lax.axis_index(GROUP)
    scale = HEAD_DIM ** -0.5

    smalls = (gain_one, bias_one, b_query, b_value, b_out, gain_two, bias_two, b_down)
    packed = jnp.concatenate([jnp.stack(smalls).reshape(-1), b_up])
    packed = lax.all_gather(packed, ALL, axis=0, tiled=False)
    n_small = len(smalls)
    small_part = packed[:, : n_small * rows].reshape(-1, n_small, rows)
    vecs = small_part.transpose(1, 0, 2).reshape(n_small, width).astype(f32)
    gain_one, bias_one, b_query, b_value, b_out, gain_two, bias_two, b_down = vecs
    b_up = packed[:, n_small * rows :].reshape(-1).astype(f32)
    head = lambda v: lax.dynamic_slice_in_dim(v, me * HEAD_DIM, HEAD_DIM)

    x_full = tree_gather(inputs, 0, "gather_inputs")
    c_full = tree_gather(cotangent, 1, "gather_cotangent")

    w_qkv = to_columns(jnp.concatenate(
        [w.reshape(rows, TREE_SEGS, HEAD_DIM) for w in (w_query, w_key, w_value, w_out)], axis=2
    ).reshape(rows, -1))
    w_ocol = w_qkv[:, 3 * HEAD_DIM :]
    w_qkv = w_qkv[:, : 3 * HEAD_DIM]
    w_orow = lax.all_to_all(
        w_ocol.reshape(TREE_SEGS, HEAD_DIM, HEAD_DIM), GROUP, split_axis=0, concat_axis=2, tiled=True
    ).reshape(HEAD_DIM, width)
    fs = ff // TREE_SEGS
    w_mlp = to_columns(jnp.concatenate(
        [w.reshape(rows, TREE_SEGS, fs) for w in (w_up, w_down)], axis=2
    ).reshape(rows, -1))
    wu, wd = w_mlp[:, :fs], w_mlp[:, fs:]

    n_full, _ = norm_stats(x_full.astype(f32))
    norm_one = (n_full * gain_one + bias_one).astype(bf16)
    qkv = dot(norm_one, w_qkv, 1, 0)
    bias = jnp.concatenate([head(b_query), jnp.zeros((HEAD_DIM,), f32), head(b_value)])
    qkv = (qkv + bias).astype(bf16)
    q, k, v = qkv[:, :HEAD_DIM], qkv[:, HEAD_DIM : 2 * HEAD_DIM], qkv[:, 2 * HEAD_DIM :]
    mask = visible_mask(parents, tok)
    s = jnp.where(mask, dot(q, k, 1, 1) * scale, -jnp.inf)
    e = jnp.exp(s - jnp.max(s, axis=-1, keepdims=True))
    probs = e / jnp.sum(e, axis=-1, keepdims=True)
    probs_low = probs.astype(bf16)
    context = dot(probs_low, v, 1, 0).astype(bf16)

    att = product_scatter(context, w_orow, 0, 2, "scatter_attended")
    x_own = inputs.astype(f32)
    residual = x_own + att + b_out
    n_two, root_two = norm_stats(residual)
    norm_two = (n_two * gain_two + bias_two).astype(bf16)
    nt_full = tree_gather(norm_two, 3, "gather_norm_two")

    upward = dot(nt_full, wu, 1, 0) + lax.dynamic_slice_in_dim(b_up, me * fs, fs)
    act, der = gelu_pair(upward)
    active = act.astype(bf16)
    d_up = (dot(c_full, wd, 1, 0) * der).astype(bf16)
    d_norm_two = product_scatter(d_up, wu, 1, 4, "scatter_d_norm_two")
    mlp = product_scatter(active, wd, 1, 5, "scatter_mlp")
    layer_output = (residual + mlp + b_down).astype(bf16)
    g_up = dot(nt_full, d_up, 0, 0)
    g_down = dot(c_full, active, 0, 0)
    g_mlp = to_rows(jnp.concatenate([g_up, g_down], axis=1), rows).reshape(rows, TREE_SEGS, 2, fs)
    g_up = g_mlp[:, :, 0].reshape(rows, ff)
    g_down = g_mlp[:, :, 1].reshape(rows, ff)
    gb_up = jnp.sum(d_up.astype(f32), axis=0)

    cot = cotangent.astype(f32)
    d_res = cot + norm_back(d_norm_two, n_two, root_two, gain_two)
    d_att = d_res.astype(bf16)
    da_full = tree_gather(d_att, 6, "gather_d_attended")
    d_ctx = dot(da_full, w_orow, 1, 1).astype(bf16)
    g_orow = dot(context, da_full, 0, 0).astype(bf16)
    g_out = lax.all_to_all(
        g_orow.reshape(HEAD_DIM, TREE_SEGS, HEAD_DIM), GROUP, split_axis=1, concat_axis=0, tiled=True
    ).reshape(width, HEAD_DIM)
    dp = dot(d_ctx, v, 1, 1)
    ds = (probs * (dp - jnp.sum(probs * dp, axis=-1, keepdims=True))).astype(bf16)
    d_q = (dot(ds, k, 1, 0) * scale).astype(bf16)
    d_k = (dot(ds, q, 0, 0) * scale).astype(bf16)
    d_v = dot(probs_low, d_ctx, 0, 0).astype(bf16)
    d_qkv = jnp.concatenate([d_q, d_k, d_v], axis=1)
    d_norm_one = product_scatter(d_qkv, w_qkv, 1, 7, "scatter_d_norm_one")
    g_att = to_rows(jnp.concatenate([dot(norm_one, d_qkv, 0, 0).astype(bf16), g_out], axis=1), rows)
    g_att = g_att.reshape(rows, TREE_SEGS, 4, HEAD_DIM)
    g_q, g_k, g_v, g_o = (g_att[:, :, j].reshape(rows, width) for j in range(4))

    n_one, root_one = norm_stats(x_own)
    grad_inputs = d_res + norm_back(d_norm_one, n_one, root_one, gain_one)

    def placed(vec, total):
        return lax.dynamic_update_slice_in_dim(jnp.zeros((total,), f32), vec, me * vec.shape[0], axis=0)

    col = lambda a: jnp.sum(a, axis=0)
    sums = [
        col(d_norm_one * n_one), col(d_norm_one),
        placed(col(d_q.astype(f32)), width), placed(col(d_v.astype(f32)), width),
        col(d_att.astype(f32)), col(d_norm_two * n_two), col(d_norm_two), col(cot),
    ]
    sums = jnp.stack(sums).reshape(len(sums), -1, rows).transpose(1, 0, 2).reshape(-1, len(sums) * rows)
    sums = jnp.concatenate([sums, placed(gb_up, ff).reshape(sums.shape[0], -1)], axis=1)
    sums = lax.psum_scatter(sums, ALL, scatter_dimension=0, tiled=True)[0]
    parts = [sums[j * rows : (j + 1) * rows] for j in range(8)]
    gb_up = sums[8 * rows :]
    return (
        layer_output, grad_inputs, parts[0], parts[1], g_q, parts[2], g_k, g_v, parts[3], g_o, parts[4],
        parts[5], parts[6], g_up, gb_up, g_down, parts[7],
    )


def solution(mesh):
    names = mesh.axis_names
    shape = mesh.devices.shape
    blk = TREE_SEGS // shape[1]
    inner = Mesh(mesh.devices.reshape(shape[0] // blk, blk, shape[1]), ALL)
    mat, vec = P(ALL, None), P(ALL)
    in_specs = (
        mat, vec, vec, mat, vec, mat, mat, vec, mat, vec, vec, vec, mat, vec, mat, vec, P(), mat,
    )
    out_specs = (
        mat, mat, vec, vec, mat, vec, mat, mat, vec, mat, vec, vec, vec, mat, vec, mat, vec,
    )
    return jax.shard_map(body, mesh=inner, in_specs=in_specs, out_specs=out_specs, check_vma=False)
```

time: 4490 us -> 978 us (0.22)
  waiting for transfers between devices: 2820 us -> 289 us
  blocking collectives: 754 us -> 75.6 us
  starting transfers between devices: 403 us -> 26 us
  Pallas kernels: 0 us -> 335 us
  matrix products: 251 us -> 98.7 us
  local copies, waits for them, and re-layouts: 167 us -> 64.2 us
    reduce_scatter x1 -> x2, waiting for transfers between devices: 1590 us -> 130 us  [to_rows(): lax.psum_scatter(g.astype(bf16), 'tree', scatter_dimension=0, tiled=True)]
    all_gather x14 -> x2, waiting for transfers between devices: 660 us -> 22.2 us  [to_columns(): return lax.all_gather(w, 'tree', axis=0, tiled=True)]
    all_gather x2 -> x1, blocking collectives: 629 us -> 75.6 us  [body(): packed = lax.all_gather(packed, ALL, axis=0, tiled=False)]
    ppermute x21 -> x0, starting transfers between devices: 402 us -> none  [shifted(): lax.ppermute(value, axis, [(source, source + steps) for source in range(l...]
    pallas_call x0 -> x8, Pallas kernels: none -> 335 us  [the longest x4 203 us: product_scatter(): pl.pallas_call(functools.partial(scatter_kernel, rhs_dim, tok), out_shape...]
    ppermute x21 -> x0, waiting for transfers between devices: 267 us -> none  [shifted(): lax.ppermute(value, axis, [(source, source + steps) for source in range(l...]
    unnamed x19 -> x6, waiting for transfers between devices: 306 us -> 117 us
    dot_general x31 -> x14, matrix products: 251 us -> 98.7 us  [dot(): lax.dot_general(a, b, (((ca,), (cb,)), ((), ())), preferred_element_type=...]
  transfers between devices with their start and end apart: 38 -> 11, of which waited for: 19 -> 6; matrix products, arithmetic and copies ran while one was open for 6% -> 13% of each run, Pallas kernels for 0% -> 23%
where the time goes in v1:
time: 978 us; the launch traced here: 965 us
  Pallas kernels  335 us (34%)
  waiting for transfers between devices  289 us (30%)
  matrix products  98.7 us (10%)
  blocking collectives  75.6 us (8%)
  local copies, waits for them, and re-layouts  64.2 us (7%)
  other arithmetic  61.3 us (6%)
  starting transfers between devices  26 us (3%)
  between operations  15.1 us (2%)
    pallas_call x4, Pallas kernels, product_scatter(): pl.pallas_call(functools.partial(scatter_kernel, rhs_dim, tok), out_shape...  203 us
    pallas_call x4, Pallas kernels, tree_gather(): pl.pallas_call(gather_kernel, out_shape=jax.ShapeDtypeStruct((16 * tok, w...  132 us
    reduce_scatter x2, waiting for transfers between devices, to_rows(): lax.psum_scatter(g.astype(bf16), 'tree', scatter_dimension=0, tiled=True)  130 us
    unnamed x6, waiting for transfers between devices  117 us
    dot_general x14, matrix products, dot(): lax.dot_general(a, b, (((ca,), (cb,)), ((), ())), preferred_element_type=...  98.7 us
    all_gather x1, blocking collectives, body(): packed = lax.all_gather(packed, ALL, axis=0, tiled=False)  75.6 us
    all_gather x2, waiting for transfers between devices, to_columns(): return lax.all_gather(w, 'tree', axis=0, tiled=True)  22.2 us
  transfers between devices with their start and end apart: 11, of which 6 were waited for; matrix products, arithmetic and copies ran while one was open for 13% of the time, Pallas kernels for 23%

profile of v1, /device:TPU:0, one launch (start us, length us, event | category | flops | bytes accessed | tf_op | source)
XLA Modules:
  0.0 965.0 jit_solution(17042896517145777436)
XLA Ops:
  11.5 6.3 all-to-all-start
  18.1 75.6 %all-gather.1 = bf16[32,1,768]{2,1,0:T(2,128)(2,1)S(1)} all-gather(bf16[1,1,768]{2,1,0:T(2,128)(2,1)S(1)} %reshape.451), channel_id=2, replica_groups=mesh['tree'=2,'blk'=8,'rep'=2] {'tree','blk','rep'}, dimensions={0}, use_global_device_ids=true | all-gather | bytes 50688 | tf_op jit(solution)/shard_map/all_gather | solution.py:353
  98.3 30.2 %gather_inputs.1 = bf16[2048,2048]{1,0:T(8,128)(2,1)} custom-call(bf16[128,2048]{1,0:T(8,128)(2,1)} %x_ref.2), custom_call_target="tpu_custom_call" | custom-call | bytes 16777216 | tf_op jit(solution)/shard_map/gather_inputs/pallas_call | solution.py:148
  128.5 35.8 %gather_cotangent.1 = bf16[2048,2048]{1,0:T(8,128)(2,1)} custom-call(bf16[128,2048]{1,0:T(8,128)(2,1)} %x_ref.3), custom_call_target="tpu_custom_call" | custom-call | bytes 16777216 | tf_op jit(solution)/shard_map/gather_cotangent/pallas_call | solution.py:148
  175.0 5.7 fusion.2
  180.8 8.6 fusion.5
  194.2 19.2 %all-to-all-done.2 = bf16[64,16,1024]{2,0,1:T(8,128)(2,1)S(1)} async-done(((bf16[64,16,1024]{2,0,1:T(8,128)(2,1)}), bf16[64,16,1024]{2,0,1:T(8,128)(2,1)S(1)}, u32[]{:S(2)}, u32[]{:S(2)}) %all-to-all-start.2) | async-done | bytes 2097184 | tf_op jit(solution)/shard_map/all_to_all | solution.py:313
  214.7 22.2 %all-gather.5.cloned.1.call-done = bf16[2048,512]{1,0:T(8,128)(2,1)} async-done(((bf16[1024,512]{1,0:T(8,128)(2,1)}), bf16[2048,512]{1,0:T(8,128)(2,1)}) %all-gather.5.cloned.1.call-update) | async-done | bytes 2097168 | tf_op jit(solution)/shard_map/all_gather | solution.py:315
  242.6 9.7 %add_convert_fusion = bf16[2048,384]{1,0:T(8,128)(2,1)S(1)} fusion(bf16[2048,2048]{1,0:T(8,128)(2,1)} %fusion.5, f32[384]{0:T(512)S(1)} %pad_maximum_fusion.7, bf16[2048,512]{1,0:T(8,128)(2,1)} %all-gather.5.cloned.1.call-done), kind=kOutput, calls=%fused_computation.37 | convolution fusion | flops 3222798336 | bytes 11535872 | tf_op jit(solution)/shard_map/dot_general | solution.py:21
  252.3 7.6 fusion.60
  260.0 8.1 fusion.7
  268.0 8.7 fusion.22.l_ref
  277.2 77.8 %scatter_attended.1 = f32[128,2048]{1,0:T(8,128)S(1)} custom-call(bf16[2048,128]{1,0:T(8,128)(2,1)S(1)} %fusion.22.l_ref, bf16[128,2048]{1,0:T(8,128)(2,1)S(1)} %bitcast.175), custom_call_target="tpu_custom_call" | custom-call | flops 1073741824 | bytes 16777216 | tf_op jit(solution)/shard_map/scatter_attended/pallas_call | solution.py:271
  358.0 32.5 %gather_norm_two.1 = bf16[2048,2048]{1,0:T(8,128)(2,1)} custom-call(bf16[128,2048]{1,0:T(8,128)(2,1)} %add_convert_fusion.2.x_ref), custom_call_target="tpu_custom_call" | custom-call | bytes 16777216 | tf_op jit(solution)/shard_map/gather_norm_two/pallas_call | solution.py:148
  394.0 8.6 multiply_convert_fusion.1
  402.6 7.4 convert_reduce_fusion.1
  410.1 38.4 %scatter_d_norm_two.1 = f32[128,2048]{1,0:T(8,128)S(1)} custom-call(bf16[2048,512]{1,0:T(8,128)(2,1)S(1)} %get-tuple-element.73.l_ref, bf16[2048,512]{1,0:T(8,128)(2,1)S(1)} %get-tuple-element.49.r_ref), custom_call_target="tpu_custom_call" | custom-call | flops 4294967296 | bytes 16777216 | tf_op jit(solution)/shard_map/scatter_d_norm_two/pallas_call | solution.py:271
  449.0 36.9 %scatter_mlp.1 = f32[128,2048]{1,0:T(8,128)S(1)} custom-call(bf16[2048,512]{1,0:T(8,128)(2,1)S(1)} %get-tuple-element.68.l_ref, bf16[2048,512]{1,0:T(8,128)(2,1)S(1)} %get-tuple-element.50.r_ref), custom_call_target="tpu_custom_call" | custom-call | flops 4294967296 | bytes 16777216 | tf_op jit(solution)/shard_map/scatter_mlp/pallas_call | solution.py:271
  488.0 33.1 %gather_d_attended.1 = bf16[2048,2048]{1,0:T(8,128)(2,1)} custom-call(bf16[128,2048]{1,0:T(8,128)(2,1)} %get-tuple-element.35.x_ref), custom_call_target="tpu_custom_call" | custom-call | bytes 16777216 | tf_op jit(solution)/shard_map/gather_d_attended/pallas_call | solution.py:148
  521.1 5.9 convolution_convert_fusion.4
  528.3 9.5 convert_reduce_fusion.5
  537.9 8.6 multiply_reduce_fusion
  546.5 8.7 multiply_convert_fusion
  566.3 8.4 convolution_convert_fusion.2
  578.9 8.3 fusion.19
  587.3 8.2 convolution_convert_fusion.1
  598.0 35.1 %reduce-scatter.3.cloned.1.call-done = bf16[1024,512]{0,1:T(8,128)(2,1)} async-done(((bf16[2048,512]{0,1:T(8,128)(2,1)}), bf16[1024,512]{0,1:T(8,128)(2,1)}) %reduce-scatter.3.cloned.1.call-update) | async-done | bytes 1048592 | tf_op jit(solution)/shard_map/reduce_scatter | solution.py:319
  639.1 95.4 %reduce-scatter.5.cloned.1.call-done = bf16[1024,1024]{0,1:T(8,128)(2,1)} async-done(((bf16[2048,1024]{0,1:T(8,128)(2,1)}), bf16[1024,1024]{0,1:T(8,128)(2,1)}) %reduce-scatter.5.cloned.1.call-update) | async-done | bytes 2097168 | tf_op jit(solution)/shard_map/reduce_scatter | solution.py:319
  748.0 49.9 %scatter_d_norm_one.1 = f32[128,2048]{1,0:T(8,128)S(1)} custom-call(bf16[2048,384]{1,0:T(8,128)(2,1)S(1)} %pad_maximum_fusion.3.l_ref, bf16[2048,384]{1,0:T(8,128)(2,1)S(1)} %slice.151.r_ref), custom_call_target="tpu_custom_call" | custom-call | flops 3221225472 | bytes 16777216 | tf_op jit(solution)/shard_map/scatter_d_norm_one/pallas_call | solution.py:271
  802.2 116.7 %all-reduce.3.cloned.1.call-done = f32[32,768]{1,0:T(8,128)} async-done(((f32[32,768]{1,0:T(8,128)}), f32[32,768]{1,0:T(8,128)}) %all-reduce.3.cloned.1.call-update) | async-done | bytes 98320
  936.2 6.8 reshape.401
  943.0 7.7 fusion.57
  (232 shorter events, 108.2 us)
Async XLA Ops:
  7.2 10.6 %copy-start.33 = (bf16[64]{0:T(256)(128)(2,1)S(1)}, bf16[64]{0:T(256)(128)(2,1)}, u32[]{:S(2)}) copy-start(bf16[64]{0:T(256)(128)(2,1)} %param.35) | copy-start | bytes 388
  7.2 10.6 %copy-start.32 = (bf16[64]{0:T(256)(128)(2,1)S(1)}, bf16[64]{0:T(256)(128)(2,1)}, u32[]{:S(2)}) copy-start(bf16[64]{0:T(256)(128)(2,1)} %param.31) | copy-start | bytes 388
  7.2 10.6 %copy-start.31 = (bf16[64]{0:T(256)(128)(2,1)S(1)}, bf16[64]{0:T(256)(128)(2,1)}, u32[]{:S(2)}) copy-start(bf16[64]{0:T(256)(128)(2,1)} %param.30) | copy-start | bytes 388
  7.2 10.6 %copy-start.30 = (bf16[64]{0:T(256)(128)(2,1)S(1)}, bf16[64]{0:T(256)(128)(2,1)}, u32[]{:S(2)}) copy-start(bf16[64]{0:T(256)(128)(2,1)} %param.29) | copy-start | bytes 388
  7.3 10.6 %copy-start.29 = (bf16[64]{0:T(256)(128)(2,1)S(1)}, bf16[64]{0:T(256)(128)(2,1)}, u32[]{:S(2)}) copy-start(bf16[64]{0:T(256)(128)(2,1)} %param.27) | copy-start | bytes 388
  7.3 10.8 %copy-start.34 = (bf16[256]{0:T(256)(128)(2,1)S(1)}, bf16[256]{0:T(256)(128)(2,1)}, u32[]{:S(2)}) copy-start(bf16[256]{0:T(256)(128)(2,1)} %param.33) | copy-start | bytes 1540
  7.3 86.5 %copy-start.4 = (s32[32]{0:T(128)S(1)}, s32[32]{0:T(128)}, u32[]{:S(2)}) copy-start(s32[32]{0:T(128)} %param.36) | copy-start | bytes 388
  11.5 158.7 %all-to-all-start = ((bf16[64,16,512]{2,0,1:T(8,128)(2,1)}), bf16[64,16,512]{2,0,1:T(8,128)(2,1)S(1)}, u32[]{:S(2)}, u32[]{:S(2)}) async-start(bf16[64,16,512]{2,0,1:T(8,128)(2,1)} %pad_maximum_fusion.4), calls=%async_computation | async-start | bytes 2097152 | tf_op jit(solution)/shard_map/all_to_all | solution.py:313
  98.1 82.7 %copy-start.22 = (f32[2048]{0:T(1024)}, f32[2048]{0:T(1024)S(1)}, u32[]{:S(2)}) copy-start(f32[2048]{0:T(1024)S(1)} %mul.194) | copy-start | bytes 24580
  128.5 35.9 %copy-start.9 = (bf16[128,2048]{1,0:T(8,128)(2,1)S(1)}, bf16[128,2048]{1,0:T(8,128)(2,1)}, u32[]{:S(2)}) copy-start(bf16[128,2048]{1,0:T(8,128)(2,1)} %x_ref.2) | copy-start | bytes 1572868
  128.5 36.1 %copy-start.18 = (bf16[64,8192]{1,0:T(8,128)(2,1)S(1)}, bf16[64,8192]{1,0:T(8,128)(2,1)}, u32[]{:S(2)}) copy-start(bf16[64,8192]{1,0:T(8,128)(2,1)} %param.34) | copy-start | bytes 3145732
  167.8 187.3 %copy-start.24 = (f32[128]{0:T(128)}, f32[128]{0:T(128)S(1)}, u32[]{:S(2)}) copy-start(f32[128]{0:T(128)S(1)} %broadcast_multiply_fusion.3) | copy-start | bytes 1540
  171.2 42.2 %all-to-all-start.2 = ((bf16[64,16,1024]{2,0,1:T(8,128)(2,1)}), bf16[64,16,1024]{2,0,1:T(8,128)(2,1)S(1)}, u32[]{:S(2)}, u32[]{:S(2)}) async-start(bf16[64,16,1024]{2,0,1:T(8,128)(2,1)} %pad_maximum_fusion.1), calls=%async_computation.2 | async-start | bytes 4194304 | tf_op jit(solution)/shard_map/all_to_all | solution.py:313
  174.9 62.0 %all-gather.5.cloned.1.call-start = ((), (), s32[]{:S(2)}) async-start(), calls=%async_computation.8 | async-start | bytes 3145728 | tf_op jit(solution)/shard_map/all_gather | solution.py:315
  180.7 209.8 %all-gather.7.cloned.1.call-start = ((), (), s32[]{:S(2)}) async-start(), calls=%async_computation.9 | async-start | bytes 6291456 | tf_op jit(solution)/shard_map/all_gather | solution.py:315
  238.8 37.9 %all-to-all-start.1 = ((bf16[16,128,128]{2,1,0:T(8,128)(2,1)}), bf16[16,128,128]{2,1,0:T(8,128)(2,1)S(1)}, u32[]{:S(2)}, u32[]{:S(2)}) async-start(bf16[16,128,128]{2,1,0:T(8,128)(2,1)} %bitcast.14), calls=%async_computation.1 | async-start | bytes 1048576 | tf_op jit(solution)/shard_map/all_to_all | solution.py:369
  252.3 15.7 %copy-start.36 = (bf16[2048,384]{1,0:T(8,128)(2,1)}, bf16[2048,384]{1,0:T(8,128)(2,1)S(1)}, u32[]{:S(2)}) copy-start(bf16[2048,384]{1,0:T(8,128)(2,1)S(1)} %add_convert_fusion) | copy-start | bytes 4718596
  390.5 12.1 %slice-start.4 = ((s8[8388608]{0:T(1024)(128)(4,1)}), s8[4194304]{0:T(1024)(128)(4,1)S(1)}, s32[]{:S(2)}) async-start(s8[8388608]{0:T(1024)(128)(4,1)} %bitcast.178), calls=%async_computation.17 | async-start | bytes 8388608
  410.1 38.5 %copy-start.2 = (bf16[2048,512]{1,0:T(8,128)(2,1)}, bf16[2048,512]{1,0:T(8,128)(2,1)S(1)}, u32[]{:S(2)}) copy-start(bf16[2048,512]{1,0:T(8,128)(2,1)S(1)} %get-tuple-element.73.l_ref) | copy-start | bytes 6291460
  410.1 38.5 %copy-start.8 = (f32[128,2048]{1,0:T(8,128)S(1)}, f32[128,2048]{1,0:T(8,128)}, u32[]{:S(2)}) copy-start(f32[128,2048]{1,0:T(8,128)} %copy-done.7) | copy-start | bytes 3145732
  449.0 36.9 %copy-start.17 = (bf16[128,2048]{1,0:T(8,128)(2,1)S(1)}, bf16[128,2048]{1,0:T(8,128)(2,1)}, u32[]{:S(2)}) copy-start(bf16[128,2048]{1,0:T(8,128)(2,1)} %x_ref.3) | copy-start | bytes 1572868
  527.0 10.9 %slice-start = ((s8[16777216]{0:T(1024)(128)(4,1)}), s8[4194304]{0:T(1024)(128)(4,1)S(1)}, s32[]{:S(2)}) async-start(s8[16777216]{0:T(1024)(128)(4,1)} %bitcast.176), calls=%async_computation.13 | async-start | bytes 8388608
  562.7 12.7 %all-to-all-start.3 = ((bf16[128,16,128]{0,2,1:T(8,128)(2,1)}), bf16[128,16,128]{0,2,1:T(8,128)(2,1)S(1)}, u32[]{:S(2)}, u32[]{:S(2)}) async-start(bf16[128,16,128]{0,2,1:T(8,128)(2,1)} %bitcast.191), calls=%async_computation.3 | async-start | bytes 1048576 | tf_op jit(solution)/shard_map/all_to_all | solution.py:418
  566.3 66.8 %reduce-scatter.3.cloned.1.call-start = ((), (), s32[]{:S(2)}) async-start(), calls=%async_computation.10 | async-start | bytes 3145728 | tf_op jit(solution)/shard_map/reduce_scatter | solution.py:319
  578.9 155.6 %reduce-scatter.5.cloned.1.call-start = ((), (), s32[]{:S(2)}) async-start(), calls=%async_computation.11 | async-start | bytes 6291456 | tf_op jit(solution)/shard_map/reduce_scatter | solution.py:319
  635.3 103.1 %all-to-all-start.4 = ((bf16[16,64,512]{2,1,0:T(8,128)(2,1)}), bf16[16,64,512]{2,1,0:T(8,128)(2,1)S(1)}, u32[]{:S(2)}, u32[]{:S(2)}) async-start(bf16[16,64,512]{2,1,0:T(8,128)(2,1)} %bitcast.29), calls=%async_computation.5 | async-start | bytes 2097152 | tf_op jit(solution)/shard_map/all_to_all | solution.py:322
  738.5 193.8 %all-to-all-start.5 = ((bf16[16,64,1024]{2,1,0:T(8,128)(2,1)}), bf16[16,64,1024]{2,1,0:T(8,128)(2,1)}, u32[]{:S(2)}, u32[]{:S(2)}) async-start(bf16[16,64,1024]{2,1,0:T(8,128)(2,1)} %bitcast.38), calls=%async_computation.7 | async-start | bytes 4194304 | tf_op jit(solution)/shard_map/all_to_all | solution.py:322
  743.2 175.7 %all-reduce.3.cloned.1.call-start = ((), (), s32[]{:S(2)}) async-start(), calls=%async_computation.12 | async-start | bytes 196608
  748.0 49.9 %copy-start.10 = (bf16[128,2048]{1,0:T(8,128)(2,1)S(1)}, bf16[128,2048]{1,0:T(8,128)(2,1)}, u32[]{:S(2)}) copy-start(bf16[128,2048]{1,0:T(8,128)(2,1)} %x_ref.2) | copy-start | bytes 1572868
  748.0 49.9 %copy-start.23 = (f32[2048]{0:T(1024)S(1)}, f32[2048]{0:T(1024)}, u32[]{:S(2)}) copy-start(f32[2048]{0:T(1024)} %copy-done.22) | copy-start | bytes 24580
  748.0 49.9 %copy-start.25 = (f32[128]{0:T(128)S(1)}, f32[128]{0:T(128)}, u32[]{:S(2)}) copy-start(f32[128]{0:T(128)} %copy-done.24) | copy-start | bytes 1540
  797.9 123.8 %copy-start.13 = (bf16[16,64,512]{2,1,0:T(8,128)(2,1)S(1)}, bf16[16,64,512]{2,1,0:T(8,128)(2,1)}, u32[]{:S(2)}) copy-start(bf16[16,64,512]{2,1,0:T(8,128)(2,1)} %copy-done.12) | copy-start | bytes 3145732
  (23 other events, 156.9 us)
Sparse Core Ops, SparseCore 0:
  180.9 56.0 all-gather.4
  239.0 101.6 all-gather.6
  579.0 54.0 reduce-scatter.2
  635.3 99.1 reduce-scatter.4
  799.7 119.2 all-reduce.2

commit v2 on v1

v2 whole, which is shorter than its diff:
```python
import functools

import jax
import jax.numpy as jnp
from jax import lax
from jax.experimental import pallas as pl
from jax.experimental.pallas import tpu as pltpu
from jax.sharding import Mesh, PartitionSpec as P

HEAD_DIM = 128
TRUNK_SEGS = 4
TREE_SEGS = 16
EPS = 1e-05
GROUP = ("blk", "rep")
ALL = ("tree", "blk", "rep")
f32 = jnp.float32
bf16 = jnp.bfloat16


def dot(a, b, ca, cb):
    return lax.dot_general(a, b, (((ca,), (cb,)), ((), ())), preferred_element_type=f32)


MESH = pl.DeviceIdType.MESH
X, Y, Z = 1, 2, 4
COMM_BYTES = 120_000_000
EVEN = ((6, (X, Y, Z)), (5, (Y, Z, X)), (5, (Z, X, Y)))
ROOM = ((8, (X, Z, Y)), (8, (Y, Z, X)))
LIGHT = ((7, (Z, X, Y)), (7, (Z, Y, X)), (2, (X, Y, Z)))


class Place:
    def __init__(self, trees):
        self.trees = trees
        self.tree = lax.axis_index("tree")
        blk = lax.axis_index("blk")
        self.x = lax.axis_index("rep")
        self.c = lax.rem(blk, 2)
        self.y = lax.rem(blk // 2, 2)
        self.z = blk // 4
        self.at = blk * 2 + self.x
        self.flat = self.tree * TREE_SEGS + self.at
        self.closing = False

    def flipped(self, r, other=0):
        flip = lambda v, on: 1 - v if on else v
        return flip(self.z, r & Z), flip(self.y, r & Y), flip(self.c, other), flip(self.x, r & X)

    def device(self, r, other=0):
        z, y, c, x = self.flipped(r, other)
        return (self.tree, (z * 2 + y) * 2 + c, x)

    def index(self, r, other=0):
        z, y, c, x = self.flipped(r, other)
        return ((z * 2 + y) * 2 + c) * 2 + x

    def in_tree(self, k):
        return (lax.rem(self.tree + k, self.trees), self.at // 2, self.x)

    def peer(self, k):
        j = lax.rem(self.at + k, TREE_SEGS)
        return j, (self.tree, j // 2, lax.rem(j, 2))

    def of_flat(self, flat):
        j = lax.rem(flat, TREE_SEGS)
        return (flat // TREE_SEGS, j // 2, lax.rem(j, 2))


def signal(device):
    pl.semaphore_signal(pltpu.get_barrier_semaphore(), inc=1, device_id=device, device_id_type=MESH)


def greet(place, extras=()):
    count = 0
    if any(e.peers for e in extras):
        pl.loop(1, TREE_SEGS)(lambda k: signal(place.peer(k)[1]))
        count += TREE_SEGS - 1
    else:
        for r, other in ((X, 0), (Y, 0), (Z, 0), (0, 1)):
            signal(place.device(r, other))
        count += 4
    if any(e.trees for e in extras):
        for k in range(1, place.trees):
            signal(place.in_tree(k))
        count += place.trees - 1
    for e in extras:
        count += e.greet(place)
    pl.semaphore_wait(pltpu.get_barrier_semaphore(), count)


def push(src, dst, send, recv, device):
    return pltpu.make_async_remote_copy(
        src_ref=src, dst_ref=dst, send_sem=send, recv_sem=recv, device_id=device, device_id_type=MESH
    )


def drain(ref, sem):
    pltpu.make_async_copy(ref, ref, sem).wait()


DMA = pltpu.SemaphoreType.DMA
ANYWHERE = pl.BlockSpec(memory_space=pl.ANY)
IN_VMEM = pl.BlockSpec(memory_space=pltpu.VMEM)


class Extra:
    peers = trees = False
    ins, in_specs, outs, out_specs, scratch = (), (), (), (), ()

    def greet(self, place):
        return 0


class SpreadSmall(Extra):
    trees = True

    def __init__(self, block):
        n = lax.axis_size("tree")
        self.ins, self.in_specs = (block,), (IN_VMEM,)
        self.outs, self.out_specs = (jax.ShapeDtypeStruct((16, n) + block.shape, block.dtype),), (IN_VMEM,)
        self.scratch = (DMA((14 + n,)), DMA((14 + n,)))

    def stages(self, place, src, box, send, recv):
        here = place.at
        box[here, place.tree] = src[...]
        new = []
        for k in range(1, place.trees):
            new.append(push(src, box.at[here, place.tree], send.at[14 + k], recv.at[14 + k], place.in_tree(k)))
            new[-1].start()
        done = list(new)
        yield
        for j, dim in enumerate(((X, 0), (Y, 0), (Z, 0), (0, 1))):
            for copy in new:
                copy.wait_recv()
            new = []
            for sub in range(1 << j):
                block = box.at[place.index(sub)]
                slot = (1 << j) - 1 + sub
                new.append(push(block, block, send.at[slot], recv.at[slot], place.device(*dim)))
                new[-1].start()
            done += new
            yield
        for copy in new:
            copy.wait_recv()
        for copy in done:
            copy.wait_send()


class ReduceSmall(Extra):
    trees = True

    def __init__(self, sums):
        n = sums.shape[1]
        tail = sums.shape[2:]
        self.ins, self.in_specs = (sums,), (IN_VMEM,)
        self.outs, self.out_specs = (jax.ShapeDtypeStruct(tail, f32),), (IN_VMEM,)
        self.scratch = (
            pltpu.VMEM((8, n) + tail, f32), pltpu.VMEM((15, n) + tail, f32), pltpu.VMEM((max(n - 1, 1),) + tail, f32),
            DMA((14 + n,)), DMA((14 + n,)),
        )

    def stages(self, place, src, out, acc, inbox, tbox, send, recv):
        done = []

        def go(block, slot, target):
            done.append(push(block, inbox.at[slot], send.at[slot], recv.at[slot], target))
            done[-1].start()

        for r in range(8):
            go(src.at[place.index(r, 1)], r, place.device(0, 1))
        yield
        for r in range(8):
            done[r].wait_recv()
            acc[r] = src[place.index(r)] + inbox[r]
        at = 8
        for bit in (Z, Y, X):
            for r in range(bit):
                go(acc.at[bit | r], at + r, place.device(bit))
            yield
            for r in range(bit):
                done[at + r].wait_recv()
                acc[r] = acc[r] + inbox[at + r]
            at += bit
        far = []
        for k in range(1, place.trees):
            tree = lax.rem(place.tree + k, place.trees)
            far.append(push(acc.at[0, tree], tbox.at[k - 1], send.at[14 + k], recv.at[14 + k], place.in_tree(k)))
            far[-1].start()
        yield
        total = acc[0, place.tree]
        for k in range(1, place.trees):
            far[k - 1].wait_recv()
            total = total + tbox[k - 1]
        out[...] = total
        for copy in done + far:
            copy.wait_send()


class ToTrees(Extra):
    trees = True

    def __init__(self, src):
        n = lax.axis_size("tree")
        self.ins, self.in_specs = (src,), (ANYWHERE,)
        self.outs, self.out_specs = (jax.ShapeDtypeStruct((n,) + src.shape, src.dtype),), (ANYWHERE,)
        self.scratch = (DMA((n,)), DMA((n,)))

    def stages(self, place, src, dst, send, recv):
        copies = [
            push(src, dst.at[place.tree], send.at[k - 1], recv.at[k - 1], place.in_tree(k)) for k in range(1, place.trees)
        ]
        copies.append(pltpu.make_async_copy(src, dst.at[place.tree], send.at[place.trees - 1]))
        for copy in copies:
            copy.start()
        while not place.closing:
            yield
        for copy in copies:
            copy.wait()


class SwapTrees(Extra):
    trees = True

    def __init__(self, src):
        n = lax.axis_size("tree")
        self.ins, self.in_specs = (src,), (ANYWHERE,)
        shape = (max(n - 1, 1), src.shape[0] // n) + src.shape[1:]
        self.outs, self.out_specs = (jax.ShapeDtypeStruct(shape, src.dtype),), (ANYWHERE,)
        self.scratch = (DMA((n,)), DMA((n,)))

    def stages(self, place, src, dst, send, recv):
        share = dst.shape[1]
        copies = []
        for k in range(1, place.trees):
            tree = lax.rem(place.tree + k, place.trees)
            rows = src.at[pl.ds(pl.multiple_of(tree * share, share), share)]
            copies.append(push(rows, dst.at[k - 1], send.at[k - 1], recv.at[k - 1], place.in_tree(k)))
            copies[-1].start()
        while not place.closing:
            yield
        for copy in copies:
            copy.wait()


class DealColumns(Extra):
    peers = True

    def __init__(self, mats, all_trees=False):
        n = lax.axis_size("tree")
        self.trees = self.all_trees = all_trees
        self.widths = [m.shape[1] // TREE_SEGS for m in mats]
        rows, total = mats[0].shape[0], sum(self.widths)
        self.ins, self.in_specs = tuple(mats), (ANYWHERE,) * len(mats)
        shape = (TREE_SEGS, rows, total)
        shape = (n,) + shape if all_trees else shape
        self.outs, self.out_specs = (jax.ShapeDtypeStruct(shape, bf16),), (ANYWHERE,)
        self.scratch = (DMA, DMA, DMA, DMA((n,)), DMA((n,)))

    def start(self, place, *refs):
        mats, (out, send, recv, keep, _, _) = refs[:-6], refs[-6:]
        box = out.at[place.tree] if self.all_trees else out

        def pieces(j):
            lo = 0
            for m, c in zip(mats, self.widths):
                yield m.at[:, pl.ds(pl.multiple_of(j * c, c), c)], box.at[place.at, :, pl.ds(lo, c)]
                lo += c

        def one(k):
            j, device = place.peer(k)
            for src, dst in pieces(j):
                push(src, dst, send, recv, device).start()

        pl.loop(1, TREE_SEGS)(one)
        for src, dst in pieces(place.at):
            pltpu.make_async_copy(src, dst, keep).start()

    def finish(self, place, *refs):
        mats, (out, send, recv, keep, _, _) = refs[:-6], refs[-6:]
        box = out.at[place.tree] if self.all_trees else out
        most = box.at[pl.ds(0, TREE_SEGS - 1)]
        drain(most, send)
        drain(most, recv)
        drain(box.at[0], keep)

    def stages(self, place, *refs):
        self.start(place, *refs)
        copies = []
        if self.all_trees:
            self.finish(place, *refs)
            mine, far_send, far_recv = refs[-6].at[place.tree], refs[-2], refs[-1]
            for k in range(1, place.trees):
                copies.append(push(mine, mine, far_send.at[k - 1], far_recv.at[k - 1], place.in_tree(k)))
                copies[-1].start()
        while not place.closing:
            yield
        if not self.all_trees:
            self.finish(place, *refs)
        for copy in copies:
            copy.wait()


class DealRows(Extra):
    peers = True

    def __init__(self, src, widths):
        self.widths = widths
        rows = src.shape[1]
        self.ins, self.in_specs = (src,), (ANYWHERE,)
        self.outs = tuple(jax.ShapeDtypeStruct((rows, TREE_SEGS * c), bf16) for c in widths)
        self.out_specs = (ANYWHERE,) * len(widths)
        self.scratch = (DMA, DMA, DMA)

    def start(self, place, src, *refs):
        outs, (send, recv, keep) = refs[:-3], refs[-3:]

        def pieces(j):
            lo = 0
            for out, c in zip(outs, self.widths):
                yield src.at[j, :, pl.ds(lo, c)], out.at[:, pl.ds(pl.multiple_of(place.at * c, c), c)]
                lo += c

        def one(k):
            j, device = place.peer(k)
            for block, dst in pieces(j):
                push(block, dst, send, recv, device).start()

        pl.loop(1, TREE_SEGS)(one)
        for block, dst in pieces(place.at):
            pltpu.make_async_copy(block, dst, keep).start()

    def finish(self, place, src, *refs):
        send, recv, keep = refs[-3:]
        most = src.at[pl.ds(0, TREE_SEGS - 1)]
        drain(most, send)
        drain(most, recv)
        drain(src.at[0], keep)

    def stages(self, place, *refs):
        self.start(place, *refs)
        while not place.closing:
            yield
        self.finish(place, *refs)


class SwapAndDeal(DealRows):
    trees = True

    def __init__(self, src, rows, widths):
        n = lax.axis_size("tree")
        self.widths = widths
        self.ins, self.in_specs = (src,), (IN_VMEM,)
        self.outs = tuple(jax.ShapeDtypeStruct((rows, TREE_SEGS * c), bf16) for c in widths)
        self.out_specs = (ANYWHERE,) * len(widths)
        block = (TREE_SEGS * rows, src.shape[1])
        self.scratch = (
            pltpu.VMEM((max(n - 1, 1),) + block, bf16), pltpu.VMEM((TREE_SEGS, rows, src.shape[1]), bf16),
            DMA((n,)), DMA((n,)), DMA, DMA, DMA,
        )

    def stages(self, place, src, *refs):
        n = len(self.widths)
        outs, (box, total, far_send, far_recv), sems = refs[:n], refs[n : n + 4], refs[n + 4 :]
        rows = total.shape[1]
        share = TREE_SEGS * rows
        copies = []
        for k in range(1, place.trees):
            tree = lax.rem(place.tree + k, place.trees)
            theirs = src.at[pl.ds(pl.multiple_of(tree * share, share), share)]
            copies.append(push(theirs, box.at[k - 1], far_send.at[k - 1], far_recv.at[k - 1], place.in_tree(k)))
            copies[-1].start()
        while not place.closing:
            yield
        for copy in copies:
            copy.wait_recv()

        def add(j):
            at = pl.ds(pl.multiple_of(j * rows, rows), rows)
            value = src[pl.ds(pl.multiple_of(place.tree * share + j * rows, rows), rows), :].astype(f32)
            for k in range(1, place.trees):
                value = value + box[k - 1, at, :].astype(f32)
            total[j] = value.astype(bf16)

        pl.loop(0, TREE_SEGS)(add)
        self.start(place, total, *outs, *sems)
        self.finish(place, total, *outs, *sems)
        for copy in copies:
            copy.wait_send()


class HeadRows(Extra):
    def __init__(self, shard):
        self.rows = shard.shape[0]
        self.ins, self.in_specs = (shard,), (ANYWHERE,)
        self.outs = (jax.ShapeDtypeStruct((HEAD_DIM, shard.shape[1]), shard.dtype),)
        self.out_specs = (ANYWHERE,)
        self.scratch = (DMA((lax.axis_size("tree"),)), DMA)

    def greet(self, place):
        per_head = HEAD_DIM // self.rows
        for b in range(per_head):
            signal(place.of_flat(place.at * per_head + b))
        return place.trees

    def stages(self, place, src, out, send, recv):
        at = place.flat * self.rows
        head = at // HEAD_DIM
        dst = out.at[pl.ds(pl.multiple_of(lax.rem(at, HEAD_DIM), self.rows), self.rows)]

        def each(do_far, do_own):
            for t in range(place.trees):
                own = (place.tree == t) & (place.at == head)
                pl.when(jnp.logical_not(own))(lambda t=t: do_far(
                    push(src, dst, send.at[t], recv, (t, head // 2, lax.rem(head, 2)))
                ))
                if do_own:
                    pl.when(own)(lambda: do_own(pltpu.make_async_copy(src, dst, recv)))

        each(lambda copy: copy.start(), lambda copy: copy.start())
        while not place.closing:
            yield
        each(lambda copy: copy.wait_send(), None)
        drain(out, recv)


class HeadRowsBack(Extra):
    def __init__(self, grad, rows):
        self.rows = rows
        n = lax.axis_size("tree")
        self.ins, self.in_specs = (grad,), (ANYWHERE,)
        self.outs, self.out_specs = (jax.ShapeDtypeStruct((n, rows, grad.shape[1]), grad.dtype),), (ANYWHERE,)
        self.scratch = (DMA((HEAD_DIM // rows,)), DMA)

    def greet(self, place):
        head = place.flat * self.rows // HEAD_DIM
        for t in range(place.trees):
            signal((t, head // 2, lax.rem(head, 2)))
        return HEAD_DIM // self.rows

    def each(self, place, src, out, send, recv, do_far, do_own):
        per_head = HEAD_DIM // self.rows
        for b in range(per_head):
            flat = place.at * per_head + b
            own = place.flat == flat
            block, dst = src.at[pl.ds(b * self.rows, self.rows)], out.at[place.tree]
            pl.when(jnp.logical_not(own))(lambda b=b, block=block, dst=dst, flat=flat: do_far(
                push(block, dst, send.at[b], recv, place.of_flat(flat))
            ))
            if do_own:
                pl.when(own)(lambda block=block, dst=dst: do_own(pltpu.make_async_copy(block, dst, recv)))

    def start(self, place, *refs):
        self.each(place, *refs, lambda copy: copy.start(), lambda copy: copy.start())

    def finish(self, place, *refs):
        self.each(place, *refs, lambda copy: copy.wait_send(), None)
        drain(refs[1], refs[3])


def finish(place, extras, running):
    place.closing = True
    order = [s for e, s in zip(extras, running) if isinstance(e, GatherRows)]
    order += [s for s in running if s not in order]
    for stages in order:
        for _ in stages:
            pass


def sorted_refs(extras, refs, n_in, n_out):
    refs = list(refs)
    take = lambda n: [refs.pop(0) for _ in range(n)]
    own_in, ins = take(n_in), [take(len(e.ins)) for e in extras]
    own_out, outs = take(n_out), [take(len(e.outs)) for e in extras]
    scratch = [take(len(e.scratch)) for e in extras]
    return own_in, own_out, refs, [i + o + s for i, o, s in zip(ins, outs, scratch)]


def call(kernel, extras, args, in_specs, out_shape, out_specs, scratch, cid, name, flops=0, vmem=None):
    out = pl.pallas_call(
        functools.partial(kernel, extras, lax.axis_size("tree")),
        out_shape=out_shape + [o for e in extras for o in e.outs],
        in_specs=in_specs + [i for e in extras for i in e.in_specs],
        out_specs=out_specs + [o for e in extras for o in e.out_specs],
        scratch_shapes=[i for e in extras for i in e.scratch] + scratch,
        compiler_params=pltpu.CompilerParams(collective_id=cid, has_side_effects=True, vmem_limit_bytes=vmem),
        cost_estimate=pl.CostEstimate(flops=flops, bytes_accessed=COMM_BYTES, transcendentals=0),
        name=name,
    )(*args, *[a for e in extras for a in e.ins])
    return out if len(out) > 1 else out[0]


def part_columns(width, plan):
    cuts = [0]
    for share, _ in plan:
        cuts.append(cuts[-1] + share * width // 16)
    return [(cuts[p], cuts[p + 1] - cuts[p]) for p in range(len(plan))]


class GatherRows(Extra):
    def __init__(self, x, plan):
        tok, width = x.shape
        self.plan = plan
        n = len(plan)
        self.ins, self.in_specs = (x,), (ANYWHERE,)
        self.outs, self.out_specs = (jax.ShapeDtypeStruct((16 * tok, width), x.dtype),), (ANYWHERE,)
        self.scratch = (DMA((n, 7)), DMA((n, 7)), DMA((n, 8)), DMA((n, 8)), DMA)

    def stages(self, place, x_ref, o_ref, send, recv, psend, precv, local):
        orders = [order for _, order in self.plan]
        tok, width = x_ref.shape
        cols = part_columns(width, self.plan)

        def rows(r, other=0):
            return pl.ds(pl.multiple_of(place.index(r, other) * tok, tok), tok)

        def remote(src, r, p, dim):
            lo, n = cols[p]
            slot = r | dim
            return pltpu.make_async_remote_copy(
                src_ref=src, dst_ref=o_ref.at[rows(r), pl.ds(lo, n)],
                send_sem=send.at[p, slot - 1], recv_sem=recv.at[p, slot - 1],
                device_id=place.device(dim), device_id_type=MESH,
            )

        def pair(r, p):
            lo, n = cols[p]
            src = o_ref.at[rows(r), pl.ds(lo, n)]
            return pltpu.make_async_remote_copy(
                src_ref=src, dst_ref=src, send_sem=psend.at[p, r], recv_sem=precv.at[p, r],
                device_id=place.device(0, 1), device_id_type=MESH,
            )

        started = []
        own = [x_ref.at[:, pl.ds(lo, n)] for lo, n in cols]
        for step in range(3):
            for p in range(len(orders)):
                copy = remote(own[p], 0, p, orders[p][step])
                copy.start()
                started.append(copy)
        keep = pltpu.make_async_copy(x_ref, o_ref.at[rows(0)], local)
        keep.start()
        for p in range(len(orders)):
            lo, n = cols[p]
            copy = pltpu.make_async_remote_copy(
                src_ref=own[p], dst_ref=o_ref.at[rows(0), pl.ds(lo, n)], send_sem=psend.at[p, 0], recv_sem=precv.at[p, 0],
                device_id=place.device(0, 1), device_id_type=MESH,
            )
            copy.start()
            started.append(copy)

        def arrived(p, slot):
            lo, n = cols[p]
            ref = o_ref.at[rows(slot), pl.ds(lo, n)]
            pltpu.make_async_remote_copy(
                src_ref=ref, dst_ref=ref, send_sem=send.at[p, slot - 1], recv_sem=recv.at[p, slot - 1],
                device_id=place.device(X), device_id_type=MESH,
            ).wait_recv()

        for which in ((1, 0, 0), (0, 1, 0), (1, 1, 0), (0, 0, 1), (1, 0, 1), (0, 1, 1), (1, 1, 1)):
            yield
            for p in range(len(orders)):
                dims = orders[p]
                slot = sum(d for d, on in zip(dims, which) if on)
                arrived(p, slot)
                lo, n = cols[p]
                src = o_ref.at[rows(slot), pl.ds(lo, n)]
                top = max(j for j in range(3) if which[j])
                for j in range(top + 1, 3):
                    copy = remote(src, slot, p, dims[j])
                    copy.start()
                    started.append(copy)
                copy = pair(slot, p)
                copy.start()
                started.append(copy)
        for copy in started:
            copy.wait_send()
        for p in range(len(orders)):
            lo, n = cols[p]
            for r in range(8):
                ref = o_ref.at[rows(r, 1), pl.ds(lo, n)]
                pltpu.make_async_remote_copy(
                    src_ref=ref, dst_ref=ref, send_sem=psend.at[p, r], recv_sem=precv.at[p, r],
                    device_id=place.device(0, 1), device_id_type=MESH,
                ).wait_recv()
        keep.wait()


def gather_kernel(extras, trees, *refs):
    _, _, _, extra_refs = sorted_refs(extras, refs, 0, 0)
    place = Place(trees)
    greet(place, extras)
    running = [e.stages(place, *r) for e, r in zip(extras, extra_refs)]
    for _ in range(8):
        for stages in running:
            next(stages, None)
    finish(place, extras, running)


def tree_gather(x, cid, name, plan=EVEN, extras=()):
    out = call(gather_kernel, tuple(extras) + (GatherRows(x, plan),), [], [], [], [], [], cid, name)
    return (out[-1], *out[:-1]) if extras else out


def scatter_kernel(plan, rhs_dim, tok, extras, trees, *refs):
    orders = [order[::-1] for _, order in plan]
    (l_ref, r_ref), (o_ref,), scratch, extra_refs = sorted_refs(extras, refs, 2, 1)
    acc, pout, pin, stage, inbox, psend, precv, send, recv = scratch
    place = Place(trees)
    width = o_ref.shape[1]
    cols = part_columns(width, plan)
    greet(place, extras)
    tile = 512

    running = [e.stages(place, *r) for e, r in zip(extras, extra_refs)]

    def advance():
        for stages in running:
            next(stages, None)

    advance()

    def product(zy, other, put):
        z, y, c, _ = place.flipped(zy, other)
        start = pl.multiple_of(((z * 2 + y) * 2 + c) * 2 * tok, 2 * tok)

        def one(j):
            at = pl.multiple_of(j * tile, tile)
            left = l_ref[pl.ds(start, 2 * tok), :]
            if rhs_dim == 1:
                res = lax.dot_general(left, r_ref[pl.ds(at, tile), pl.ds(0, l_ref.shape[1])], (((1,), (1,)), ((), ())), preferred_element_type=f32)
            else:
                res = lax.dot_general(left, r_ref[:, pl.ds(at, tile)], (((1,), (0,)), ((), ())), preferred_element_type=f32)
            put(at, res)

        pl.loop(0, width // tile)(one)

    def pair(k):
        return pltpu.make_async_remote_copy(
            src_ref=pout.at[k], dst_ref=pin.at[k], send_sem=psend.at[k], recv_sem=precv.at[k],
            device_id=place.device(0, 1), device_id_type=MESH,
        )

    groups = (Z | Y, Z, Y, 0)
    for k, zy in enumerate(groups):
        def put_out(at, res, k=k):
            pout[k, :, pl.ds(at, tile)] = res.astype(bf16)
        product(zy, 1, put_out)
        pair(k).start()
    advance()

    def hop(p, r, step, slot):
        lo, n = cols[p]
        return pltpu.make_async_remote_copy(
            src_ref=stage.at[r - 1, :, pl.ds(lo, n)], dst_ref=inbox.at[slot, :, pl.ds(lo, n)],
            send_sem=send.at[p, r - 1], recv_sem=recv.at[p, slot],
            device_id=place.device(orders[p][step]), device_id_type=MESH,
        )

    started = []
    for k, zy in enumerate(groups):
        def put_own(at, res, k=k):
            acc[k, :, pl.ds(at, tile)] = res
        product(zy, 0, put_own)
        pair(k).wait_recv()
        for rx in (X, 0):
            r = zy | rx
            xx = place.flipped(rx)[3]
            at = pl.ds(pl.multiple_of(xx * tok, tok), tok)
            for p in range(len(plan)):
                lo, n = cols[p]
                total = acc[k, at, pl.ds(lo, n)] + pin[k, at, pl.ds(lo, n)].astype(f32)
                first, second, third = orders[p]
                if r & first:
                    stage[r - 1, :, pl.ds(lo, n)] = total.astype(bf16)
                    slot = 3 - (2 * bool(r & second) + bool(r & third))
                    copy = hop(p, r, 0, slot)
                    copy.start()
                    started.append(copy)
                else:
                    acc[k, at, pl.ds(lo, n)] = total

    def held(p, r):
        k = groups.index(r & (Z | Y))
        xx = place.flipped(r & X)[3]
        lo, n = cols[p]
        return acc[k, pl.ds(pl.multiple_of(xx * tok, tok), tok), pl.ds(lo, n)]

    def take(p, slot):
        lo, n = cols[p]
        hop(p, 1, 0, slot).wait_recv()
        return inbox[slot, :, pl.ds(lo, n)].astype(f32)

    advance()
    for q in ((1, 1), (1, 0)):
        for p in range(len(plan)):
            first, second, third = orders[p]
            lo, n = cols[p]
            r = second + third * q[1]
            stage[r - 1, :, pl.ds(lo, n)] = (held(p, r) + take(p, 3 - (2 * q[0] + q[1]))).astype(bf16)
            copy = hop(p, r, 1, 4 + (1 - q[1]))
            copy.start()
            started.append(copy)
        advance()
    for p in range(len(plan)):
        third = orders[p][2]
        lo, n = cols[p]
        stage[third - 1, :, pl.ds(lo, n)] = (held(p, third) + take(p, 2) + take(p, 4)).astype(bf16)
        copy = hop(p, third, 2, 6)
        copy.start()
        started.append(copy)
    advance()
    for p in range(len(plan)):
        lo, n = cols[p]
        o_ref[:, pl.ds(lo, n)] = held(p, 0) + take(p, 3) + take(p, 5)
    for p in range(len(plan)):
        lo, n = cols[p]
        o_ref[:, pl.ds(lo, n)] += take(p, 6)
    advance()
    for copy in started:
        copy.wait_send()
    for k in range(4):
        pair(k).wait_send()
    finish(place, extras, running)


def product_scatter(left, right, rhs_dim, cid, name, plan=EVEN, extras=()):
    tokens, inner = left.shape
    width = right.shape[1 - rhs_dim]
    tok = tokens // 16
    n = len(plan)
    scratch = [
        pltpu.VMEM((4, 2 * tok, width), f32),
        pltpu.VMEM((4, 2 * tok, width), bf16),
        pltpu.VMEM((4, 2 * tok, width), bf16),
        pltpu.VMEM((7, tok, width), bf16),
        pltpu.VMEM((7, tok, width), bf16),
        DMA((4,)), DMA((4,)), DMA((n, 7)), DMA((n, 7)),
    ]
    return call(
        functools.partial(scatter_kernel, plan, rhs_dim, tok), extras, [left, right], [IN_VMEM, IN_VMEM],
        [jax.ShapeDtypeStruct((tok, width), f32)], [IN_VMEM],
        scratch, cid, name, 2 * tokens * width * inner, 48 * 2**20,
    )


def norm_stats(v):
    mean = jnp.mean(v, axis=-1, keepdims=True)
    centred = v - mean
    root = lax.rsqrt(jnp.mean(centred * centred, axis=-1, keepdims=True) + EPS)
    return centred * root, root


def norm_back(d, n, root, gain):
    g = d * gain
    return root * (g - jnp.mean(g, axis=-1, keepdims=True) - n * jnp.mean(g * n, axis=-1, keepdims=True))


def gelu_pair(u):
    c = (2.0 / jnp.pi) ** 0.5
    t = jnp.tanh(c * (u + 0.044715 * u * u * u))
    act = 0.5 * u * (1.0 + t)
    der = 0.5 * (1.0 + t) + 0.5 * u * (1.0 - t * t) * c * (1.0 + 3 * 0.044715 * u * u)
    return act, der


def own_rows(g, swapped, rows):
    share = swapped.shape[1]
    mine = lax.dynamic_slice_in_dim(g, lax.axis_index("tree") * share, share)
    if lax.axis_size("tree") > 1:
        mine = (mine.astype(f32) + jnp.sum(swapped.astype(f32), axis=0)).astype(bf16)
    return mine.reshape(TREE_SEGS, rows, -1)


def scores_of(qkv_ref, parent_ref, s, tok):
    hd = HEAD_DIM
    own = pl.ds(pl.multiple_of(s * tok, tok), tok)
    branches = [pl.ds((TRUNK_SEGS + b) * tok, tok) for b in range(4)]
    trunk = pl.ds(0, TRUNK_SEGS * tok)
    parent = parent_ref[s]

    def rows(col):
        up = qkv_ref[branches[0], col]
        for b in range(1, 4):
            up = jnp.where(parent == TRUNK_SEGS + b, qkv_ref[branches[b], col], up)
        return jnp.concatenate([qkv_ref[trunk, col], up, qkv_ref[own, col]], axis=0)

    q = qkv_ref[own, pl.ds(0, hd)]
    k, v = rows(pl.ds(hd, hd)), rows(pl.ds(2 * hd, hd))
    raw = dot(q, k, 1, 1) * HEAD_DIM ** -0.5
    n_trunk = TRUNK_SEGS * tok
    row = lax.broadcasted_iota(jnp.int32, raw.shape, 0)
    col = lax.broadcasted_iota(jnp.int32, raw.shape, 1)
    limit_up = jnp.where(s >= 2 * TRUNK_SEGS, n_trunk + tok, 0)
    limit_own = jnp.where(s >= TRUNK_SEGS, n_trunk + tok, -1)
    in_trunk = (col < n_trunk) & (col <= s * tok + row)
    in_up = (col >= n_trunk) & (col < limit_up)
    in_own = (col >= n_trunk + tok) & (col <= limit_own + row)
    seen = in_trunk | in_up | in_own
    raw = jnp.where(seen, raw, -jnp.inf)
    e = jnp.exp(raw - jnp.max(raw, axis=-1, keepdims=True))
    probs = e / jnp.sum(e, axis=-1, keepdims=True)
    return q, k, v, probs, own, trunk, branches, parent


def attend_kernel(deal, trees, *refs):
    (parent_ref, x_ref, gain_ref, bias_ref, w_ref, b_ref), (n_ref, qkv_ref, ctx_ref), (held,), deal_refs = sorted_refs(
        (deal,), refs, 6, 3
    )
    place = Place(trees)

    @pl.when(pl.program_id(0) == 0)
    def _():
        greet(place, (deal,))
        deal.start(place, *deal_refs[0])

    step = pl.program_id(0)
    rows = x_ref.shape[0]
    tok = held.shape[0] // TREE_SEGS
    n, _ = norm_stats(x_ref[...].astype(f32))
    norm = (n * gain_ref[...] + bias_ref[...]).astype(bf16)
    n_ref[...] = norm
    qkv = (dot(norm, w_ref[...], 1, 0) + b_ref[...]).astype(bf16)
    qkv_ref[...] = qkv
    held[pl.ds(pl.multiple_of(step * rows, rows), rows), :] = qkv

    @pl.when(step == pl.num_programs(0) - 1)
    def _():
        def one(s):
            _, _, v, probs, own, _, _, _ = scores_of(held, parent_ref, s, tok)
            ctx_ref[own, :] = dot(probs.astype(bf16), v, 1, 0).astype(bf16)

        pl.loop(0, TREE_SEGS, unroll=2)(one)
        deal.finish(place, *deal_refs[0])


def attend(parent, x_full, gain, bias, w, b, deal, cid):
    tokens, width = x_full.shape
    n = 3 * HEAD_DIM
    rows = 256
    whole = lambda shape: pl.BlockSpec(shape, lambda i: (0,) * len(shape))
    by_row = lambda cols: pl.BlockSpec((rows, cols), lambda i: (i, 0))
    return pl.pallas_call(
        functools.partial(attend_kernel, deal, lax.axis_size("tree")),
        grid=(tokens // rows,),
        in_specs=[
            pl.BlockSpec(memory_space=pltpu.SMEM), by_row(width), whole((1, width)), whole((1, width)), whole((width, n)),
            whole((1, n)), *deal.in_specs,
        ],
        out_specs=[by_row(width), by_row(n), whole((tokens, HEAD_DIM)), *deal.out_specs],
        scratch_shapes=[*deal.scratch, pltpu.VMEM((tokens, n), bf16)],
        out_shape=[
            jax.ShapeDtypeStruct((tokens, width), bf16),
            jax.ShapeDtypeStruct((tokens, n), bf16),
            jax.ShapeDtypeStruct((tokens, HEAD_DIM), bf16),
            *deal.outs,
        ],
        compiler_params=pltpu.CompilerParams(collective_id=cid, has_side_effects=True, vmem_limit_bytes=40 * 2**20),
        cost_estimate=pl.CostEstimate(flops=2 * tokens * width * n, bytes_accessed=60_000_000, transcendentals=0),
        name="attend",
    )(parent, x_full, gain, bias, w, b, *deal.ins)


def attend_back_kernel(extras, trees, *refs):
    (parent_ref, qkv_ref, d_ref, w_ref), (o_ref,), (dk, dv, d_ctx), extra_refs = sorted_refs(extras, refs, 4, 1)
    place = Place(trees)
    step = pl.program_id(0)

    @pl.when(step == 0)
    def _():
        greet(place, extras)
        for e, r in zip(extras, extra_refs):
            e.start(place, *r)

    rows = d_ref.shape[0]
    tok = qkv_ref.shape[0] // TREE_SEGS
    hd = HEAD_DIM
    scale = HEAD_DIM ** -0.5
    d_ctx[pl.ds(pl.multiple_of(step * rows, rows), rows), :] = dot(d_ref[...], w_ref[...], 1, 1).astype(bf16)

    @pl.when(step == pl.num_programs(0) - 1)
    def _():
        dk[...] = jnp.zeros_like(dk)
        dv[...] = jnp.zeros_like(dv)

        def one(s):
            q, k, v, probs, own, trunk, branches, parent = scores_of(qkv_ref, parent_ref, s, tok)
            dc = d_ctx[own, :]
            dp = dot(dc, v, 1, 1)
            ds = (probs * (dp - jnp.sum(probs * dp, axis=-1, keepdims=True))).astype(bf16)
            o_ref[own, pl.ds(0, hd)] = (dot(ds, k, 1, 0) * scale).astype(bf16)
            gk = dot(ds, q, 0, 0)
            gv = dot(probs.astype(bf16), dc, 0, 0)
            n_trunk = TRUNK_SEGS * tok
            for acc, g in ((dk, gk), (dv, gv)):
                acc[trunk, :] += g[:n_trunk]
                for b in range(4):
                    acc[branches[b], :] += jnp.where(parent == TRUNK_SEGS + b, g[n_trunk : n_trunk + tok], 0.0)
                acc[own, :] += g[n_trunk + tok :]

        pl.loop(0, TREE_SEGS, unroll=2)(one)
        o_ref[:, pl.ds(hd, hd)] = (dk[...] * scale).astype(bf16)
        o_ref[:, pl.ds(2 * hd, hd)] = dv[...].astype(bf16)
        for e, r in zip(extras, extra_refs):
            e.finish(place, *r)


def attend_back(parent, qkv, d_full, w_rows, extras, cid):
    tokens, width = d_full.shape
    n = qkv.shape[1]
    rows = 256
    whole = lambda shape: pl.BlockSpec(shape, lambda i: (0,) * len(shape))
    return pl.pallas_call(
        functools.partial(attend_back_kernel, extras, lax.axis_size("tree")),
        grid=(tokens // rows,),
        in_specs=[
            pl.BlockSpec(memory_space=pltpu.SMEM), whole((tokens, n)), pl.BlockSpec((rows, width), lambda i: (i, 0)),
            whole((HEAD_DIM, width)), *[i for e in extras for i in e.in_specs],
        ],
        out_specs=[whole((tokens, n)), *[o for e in extras for o in e.out_specs]],
        scratch_shapes=[
            *[i for e in extras for i in e.scratch],
            pltpu.VMEM((tokens, HEAD_DIM), f32), pltpu.VMEM((tokens, HEAD_DIM), f32), pltpu.VMEM((tokens, HEAD_DIM), bf16),
        ],
        out_shape=[jax.ShapeDtypeStruct((tokens, n), bf16), *[o for e in extras for o in e.outs]],
        compiler_params=pltpu.CompilerParams(collective_id=cid, has_side_effects=True, vmem_limit_bytes=40 * 2**20),
        cost_estimate=pl.CostEstimate(flops=2 * tokens * width * HEAD_DIM, bytes_accessed=60_000_000, transcendentals=0),
        name="attend_back",
    )(parent, qkv, d_full, w_rows, *[a for e in extras for a in e.ins])


def body(
    inputs, gain_one, bias_one, w_query, b_query, w_key, w_value, b_value, w_out, b_out,
    gain_two, bias_two, w_up, b_up, w_down, b_down, parents, cotangent,
):
    tok, width = inputs.shape
    rows = w_query.shape[0]
    ff = w_up.shape[1]
    fs = ff // TREE_SEGS
    trees = lax.axis_size("tree")
    devices = trees * TREE_SEGS
    tree = lax.axis_index("tree")
    me = lax.axis_index(GROUP)
    head = lambda v: lax.dynamic_slice_in_dim(v, me * HEAD_DIM, HEAD_DIM)

    smalls = jnp.concatenate([gain_one, bias_one, b_query, b_value, b_out, gain_two, bias_two, b_down, b_up])
    n_small = smalls.shape[0]
    block = jnp.pad(smalls, (0, 16 * 128 - n_small)).reshape(16, 128)

    x_full, box, w_orow, w_att, share_up = tree_gather(inputs, 0, "gather_inputs", ROOM, extras=(
        SpreadSmall(block), HeadRows(w_out), DealColumns((w_query, w_key, w_value), all_trees=True), DealColumns((w_up,)),
    ))
    w_att = w_att.reshape(width, -1)
    packed = box.transpose(1, 0, 2, 3).reshape(devices, -1)[:, :n_small]
    vecs = packed[:, : 8 * rows].reshape(devices, 8, rows).transpose(1, 0, 2).reshape(8, width).astype(f32)
    gain_one, bias_one, b_query, b_value, b_out, gain_two, bias_two, b_down = vecs
    b_up = packed[:, 8 * rows :].reshape(-1).astype(f32)

    local_seg = jnp.arange(TREE_SEGS, dtype=jnp.int32)
    own_parents = lax.dynamic_slice_in_dim(parents, tree * TREE_SEGS, TREE_SEGS) - tree * TREE_SEGS
    parent = jnp.where(local_seg >= 2 * TRUNK_SEGS, own_parents, local_seg)

    b_qkv = jnp.concatenate([head(b_query), jnp.zeros((HEAD_DIM,), f32), head(b_value)])
    norm_one, qkv, context, share_down = attend(
        parent, x_full, gain_one[None], bias_one[None], w_att, b_qkv[None], DealColumns((w_down,)), 9
    )
    att, wu, c_full = product_scatter(context, w_orow, 0, 2, "scatter_attended", ROOM, extras=(
        ToTrees(share_up.reshape(-1, fs)), GatherRows(cotangent, ROOM),
    ))
    wu = wu.reshape(width, fs)
    x_own = inputs.astype(f32)
    residual = x_own + att + b_out
    n_two, root_two = norm_stats(residual)
    norm_two = (n_two * gain_two + bias_two).astype(bf16)
    nt_full, wd = tree_gather(norm_two, 3, "gather_norm_two", ROOM, extras=(ToTrees(share_down.reshape(-1, fs)),))
    wd = wd.reshape(width, fs)

    upward = dot(nt_full, wu, 1, 0) + lax.dynamic_slice_in_dim(b_up, me * fs, fs)
    act, der = gelu_pair(upward)
    active = act.astype(bf16)
    d_up = (dot(c_full, wd, 1, 0) * der).astype(bf16)
    g_up = dot(nt_full, d_up, 0, 0).astype(bf16)
    g_down = dot(c_full, active, 0, 0).astype(bf16)
    g_up, g_down, d_up = lax.optimization_barrier((g_up, g_down, d_up))
    d_norm_two, swap_up = product_scatter(d_up, wu, 1, 4, "scatter_d_norm_two", LIGHT, extras=(SwapTrees(g_up),))

    cot = cotangent.astype(f32)
    d_res = cot + norm_back(d_norm_two, n_two, root_two, gain_two)
    d_att = d_res.astype(bf16)
    mlp, swap_down, da_full = product_scatter(active, wd, 1, 5, "scatter_mlp", ROOM, extras=(
        SwapTrees(g_down), GatherRows(d_att, ROOM),
    ))
    g_up, g_down = own_rows(g_up, swap_up, rows), own_rows(g_down, swap_down, rows)
    g_orow = dot(context, da_full, 0, 0).astype(bf16)
    d_qkv, g_up, g_o = attend_back(
        parent, qkv, da_full, w_orow, (DealRows(g_up, (fs,)), HeadRowsBack(g_orow, rows)), 10
    )

    g_qkv = dot(norm_one, d_qkv, 0, 0)
    s_qkv = jnp.sum(d_qkv.astype(f32), axis=0)
    w_f = w_att.astype(f32)
    gb_one = jnp.sum(w_f * s_qkv, axis=1)
    gg_one = (jnp.sum(w_f * g_qkv, axis=1) - bias_one * gb_one) / gain_one
    g_att = g_qkv.astype(bf16)

    def placed(vec, total):
        return lax.dynamic_update_slice_in_dim(jnp.zeros((total,), f32), vec, me * vec.shape[0], axis=0)

    col = lambda a: jnp.sum(a, axis=0)
    sums = [
        gg_one, gb_one, placed(s_qkv[:HEAD_DIM], width), placed(s_qkv[2 * HEAD_DIM :], width),
        col(d_att.astype(f32)), col(d_norm_two * n_two), col(d_norm_two), col(cot),
    ]
    sums = jnp.stack(sums).reshape(8, devices, rows).transpose(1, 0, 2).reshape(devices, 8 * rows)
    sums = jnp.concatenate([sums, placed(col(d_up.astype(f32)), ff).reshape(devices, -1)], axis=1)
    sums = jnp.pad(sums, ((0, 0), (0, 1024 - n_small))).reshape(trees, TREE_SEGS, 8, 128).transpose(1, 0, 2, 3)
    d_norm_one, g_q, g_k, g_v, sums, g_down = product_scatter(d_qkv, w_att, 1, 7, "scatter_d_norm_one", LIGHT, extras=(
        SwapAndDeal(g_att, rows, (HEAD_DIM,) * 3), ReduceSmall(sums), DealRows(g_down, (fs,)),
    ))
    sums = sums.reshape(-1)
    parts = [sums[j * rows : (j + 1) * rows] for j in range(8)]
    gb_up = sums[8 * rows : n_small]

    n_one, root_one = norm_stats(x_own)
    grad_inputs = d_res + norm_back(d_norm_one, n_one, root_one, gain_one)

    layer_output = (residual + mlp + b_down).astype(bf16)
    g_q, g_k, g_v, g_up, g_down = (g.astype(f32) for g in (g_q, g_k, g_v, g_up, g_down))
    g_o = jnp.sum(g_o.astype(f32), axis=0)
    return (
        layer_output, grad_inputs, parts[0], parts[1], g_q, parts[2], g_k, g_v, parts[3], g_o, parts[4],
        parts[5], parts[6], g_up, gb_up, g_down, parts[7],
    )


def solution(mesh):
    names = mesh.axis_names
    shape = mesh.devices.shape
    blk = TREE_SEGS // shape[1]
    inner = Mesh(mesh.devices.reshape(shape[0] // blk, blk, shape[1]), ALL)
    mat, vec = P(ALL, None), P(ALL)
    in_specs = (
        mat, vec, vec, mat, vec, mat, mat, vec, mat, vec, vec, vec, mat, vec, mat, vec, P(), mat,
    )
    out_specs = (
        mat, mat, vec, vec, mat, vec, mat, mat, vec, mat, vec, vec, vec, mat, vec, mat, vec,
    )
    return jax.shard_map(body, mesh=inner, in_specs=in_specs, out_specs=out_specs, check_vma=False)
```

time: 978 us -> 580 us (0.59)
  waiting for transfers between devices: 289 us -> 0 us
  Pallas kernels: 335 us -> 475 us
  blocking collectives: 75.6 us -> 0 us
  matrix products: 98.7 us -> 41.3 us
  local copies, waits for them, and re-layouts: 64.2 us -> 22.9 us
  other arithmetic: 61.3 us -> 30.6 us
  starting transfers between devices: 26 us -> 0 us
  between operations: 15.1 us -> 1.63 us
    pallas_call x8, Pallas kernels: 335 us -> 475 us  [the longest x6 425 us: call(): pl.pallas_call(functools.partial(kernel, extras, lax.axis_size('tree')),...]
    reduce_scatter x2 -> x0, waiting for transfers between devices: 130 us -> none  [to_rows(): lax.psum_scatter(g.astype(bf16), 'tree', scatter_dimension=0, tiled=True)]
    unnamed x6 -> x0, waiting for transfers between devices: 117 us -> none
    all_gather x1 -> x0, blocking collectives: 75.6 us -> none  [body(): packed = lax.all_gather(packed, ALL, axis=0, tiled=False)]
    dot_general x14 -> x6, matrix products: 98.7 us -> 41.3 us  [dot(): lax.dot_general(a, b, (((ca,), (cb,)), ((), ())), preferred_element_type=...]
    all_to_all x6 -> x0, starting transfers between devices: 25.8 us -> none  [the longest x2 10 us: to_columns(): w = lax.all_to_all(w, GROUP, split_axis=1, concat_axis=0, tiled=True)]
    all_gather x2 -> x0, waiting for transfers between devices: 22.2 us -> none  [to_columns(): return lax.all_gather(w, 'tree', axis=0, tiled=True)]
    slice x12 -> x1, local copies, waits for them, and re-layouts: 20.7 us -> 0.56 us  [body(): gb_up = sums[8 * rows:n_small]]
  transfers between devices with their start and end apart: 11 -> 0, of which waited for: 6 -> 0; matrix products, arithmetic and copies ran while one was open for 13% -> 0% of each run, Pallas kernels for 23% -> 0%
where the time goes in v2:
time: 580 us; the launch traced here: 571 us
  Pallas kernels  475 us (82%)
  matrix products  41.3 us (7%)
  other arithmetic  30.6 us (5%)
  local copies, waits for them, and re-layouts  22.9 us (4%)
    pallas_call x6, Pallas kernels, call(): pl.pallas_call(functools.partial(kernel, extras, lax.axis_size('tree')),...  425 us
    dot_general x6, matrix products, dot(): lax.dot_general(a, b, (((ca,), (cb,)), ((), ())), preferred_element_type=...  41.3 us
    pallas_call x1, Pallas kernels, attend_back(): pl.pallas_call(functools.partial(attend_back_kernel, extras, lax.axis_siz...  25.1 us
    pallas_call x1, Pallas kernels, attend(): pl.pallas_call(functools.partial(attend_kernel, deal, lax.axis_size('tree...  24.9 us

profile of v2, /device:TPU:0, one launch (start us, length us, event | category | flops | bytes accessed | tf_op | source)
XLA Modules:
  0.0 571.5 jit_solution(15853691614454325288)
XLA Ops:
  0.7 6.1 %concatenate.10 = bf16[768]{0:T(1024)(128)(2,1)S(1)} concatenate(bf16[64]{0:T(256)(128)(2,1)} %param.19, bf16[64]{0:T(256)(128)(2,1)} %param.20, bf16[64]{0:T(256)(128)(2,1)} %param.22, bf16[64]{0:T(256)(128)(2,1)} %param.25, bf16[64]{0:T(256)(128)(2,1)} %param.27, bf16[64]{0:T(256)(128)(2,1)} %param.28, bf16[64]{0:T(256)(128)(2,1)} %param.29, bf16[64]{0:T(256)(128)(2,1)} %param.33, ...), dimensions={0} | concatenate | bytes 3072 | tf_op jit(solution)/shard_map/concatenate | solution.py:945
  7.3 85.7 %gather_inputs.1 = (bf16[16,2,16,128]{3,2,1,0:T(8,128)(2,1)}, bf16[128,2048]{1,0:T(8,128)(2,1)}, bf16[2,16,64,384]{3,2,1,0:T(8,128)(2,1)}, bf16[16,64,512]{2,1,0:T(8,128)(2,1)}, bf16[2048,2048]{1,0:T(8,128)(2,1)}) custom-call(bf16[16,128]{1,0:T(8,128)(2,1)} %pad_bitcast_fusion.refs_0_, bf16[64,2048]{1,0:T(8,128)(2,1)} %refs_1_.1, bf16[64,2048]{1,0:T(8,128)(2,1)} %refs_2_.1, ...), custom_call_target="tpu_custom_call" | custom-call | bytes 120000000 | tf_op jit(solution)/shard_map/gather_inputs/pallas_call | solution.py:479
  95.6 1.4 copy-done.2
  97.1 1.2 copy-done.19
  98.3 24.9 %attend.1 = (bf16[2048,2048]{1,0:T(8,128)(2,1)S(1)}, bf16[2048,384]{1,0:T(8,128)(2,1)S(1)}, bf16[2048,128]{1,0:T(8,128)(2,1)S(1)}, bf16[16,64,512]{2,1,0:T(8,128)(2,1)S(1)}) custom-call(s32[16]{0:T(128)S(1)} %compare_select_fusion.refs_0_, bf16[2048,2048]{1,0:T(8,128)(2,1)} %get-tuple-element.48.refs_1_, f32[1,2048]{1,0:T(1,128)S(1)} %unstack.37.refs_2_, ...), custom_call_target="tpu_custom_call" | custom-call | flops 3221225472 | bytes 60000000 | tf_op jit(solution)/shard_map/attend/pallas_call | solution.py:842
  123.2 1.2 copy-done
  125.4 3.2 copy-done.23
  128.7 74.9 %scatter_attended.1 = (f32[128,2048]{1,0:T(8,128)S(1)}, bf16[2,1024,512]{2,1,0:T(8,128)(2,1)S(1)}, bf16[2048,2048]{1,0:T(8,128)(2,1)}) custom-call(bf16[2048,128]{1,0:T(8,128)(2,1)S(1)} %get-tuple-element.51.refs_0_, bf16[128,2048]{1,0:T(8,128)(2,1)S(1)} %copy-done.14, bf16[1024,512]{1,0:T(8,128)(2,1)S(1)} %bitcast.70, bf16[128,2048]{1,0:T(8,128)(2,1)S(1)} %copy-done.17), custom_call_target="tpu_custom_call" | custom-call | flops 1073741824 | bytes 120000000 | tf_op jit(solution)/shard_map/scatter_attended/pallas_call | solution.py:479
  203.8 1.5 fusion.23
  205.5 1.6 multiply_reduce_fusion.4
  207.1 2.3 add_convert_fusion.1.refs_1_
  209.4 50.8 %gather_norm_two.1 = (bf16[2,1024,512]{2,1,0:T(8,128)(2,1)}, bf16[2048,2048]{1,0:T(8,128)(2,1)}) custom-call(bf16[1024,512]{1,0:T(8,128)(2,1)} %bitcast.67, bf16[128,2048]{1,0:T(8,128)(2,1)} %add_convert_fusion.1.refs_1_), custom_call_target="tpu_custom_call" | custom-call | bytes 120000000 | tf_op jit(solution)/shard_map/gather_norm_two/pallas_call | solution.py:479
  260.3 7.9 %multiply_convert_fusion = (bf16[2048,512]{1,0:T(8,128)(2,1)S(1)}, f32[2048,512]{1,0:T(8,128)S(1)}) fusion(f32[512]{0:T(512)S(1)} %dynamic_slice.27, bf16[2048,2048]{1,0:T(8,128)(2,1)} %get-tuple-element.56, bf16[2048,512]{1,0:T(8,128)(2,1)S(1)} %bitcast.72), kind=kOutput, calls=%fused_computation.10 | convolution fusion | flops 4305453056 | bytes 16779264 | tf_op jit(solution)/shard_map/dot_general | solution.py:21
  268.3 10.8 %fusion.6.refs_0_ = bf16[2048,512]{1,0:T(8,128)(2,1)S(1)} fusion(f32[2048,512]{1,0:T(8,128)S(1)} %get-tuple-element.112, bf16[2048,2048]{1,0:T(8,128)(2,1)} %get-tuple-element.59, bf16[2048,512]{1,0:T(8,128)(2,1)S(1)} %bitcast.90, f32[512]{0:T(512)S(1)} %dynamic_slice.27), kind=kOutput, calls=%fused_computation.8 | convolution fusion | flops 4315938816 | bytes 16779264 | tf_op jit(solution)/shard_map/dot_general | solution.py:21
  279.1 5.8 %convolution_convert_fusion.1.refs_2_ = bf16[2048,512]{1,0:T(8,128)(2,1)} fusion(bf16[2048,2048]{1,0:T(8,128)(2,1)S(1)} %bitcast.88, bf16[2048,512]{1,0:T(8,128)(2,1)S(1)} %fusion.6.refs_0_), kind=kOutput, calls=%fused_computation.15 | convolution fusion | flops 4296015872 | bytes 12582912 | tf_op jit(solution)/shard_map/dot_general | solution.py:21
  284.9 5.7 %convolution_convert_fusion.refs_2_ = bf16[2048,512]{1,0:T(8,128)(2,1)} fusion(bf16[2048,2048]{1,0:T(8,128)(2,1)S(1)} %bitcast.92, bf16[2048,512]{1,0:T(8,128)(2,1)S(1)} %get-tuple-element.111.refs_0_), kind=kOutput, calls=%fused_computation.14 | convolution fusion | flops 4296015872 | bytes 12582912 | tf_op jit(solution)/shard_map/dot_general | solution.py:21
  290.7 67.6 %scatter_d_norm_two.1 = (f32[128,2048]{1,0:T(8,128)S(1)}, bf16[1,1024,512]{2,1,0:T(8,128)(2,1)S(1)}) custom-call(bf16[2048,512]{1,0:T(8,128)(2,1)S(1)} %fusion.6.refs_0_, bf16[2048,512]{1,0:T(8,128)(2,1)} %bitcast.71, bf16[2048,512]{1,0:T(8,128)(2,1)} %convolution_convert_fusion.1.refs_2_), custom_call_target="tpu_custom_call" | custom-call | flops 4294967296 | bytes 120000000 | tf_op jit(solution)/shard_map/scatter_d_norm_two/pallas_call | solution.py:479
  358.7 1.7 convert_reduce_fusion.5
  360.4 76.5 %scatter_mlp.1 = (f32[128,2048]{1,0:T(8,128)S(1)}, bf16[1,1024,512]{2,1,0:T(8,128)(2,1)S(1)}, bf16[2048,2048]{1,0:T(8,128)(2,1)}) custom-call(bf16[2048,512]{1,0:T(8,128)(2,1)S(1)} %get-tuple-element.111.refs_0_, bf16[2048,512]{1,0:T(8,128)(2,1)} %bitcast.89, bf16[2048,512]{1,0:T(8,128)(2,1)} %convolution_convert_fusion.refs_2_, ...), custom_call_target="tpu_custom_call" | custom-call | flops 4294967296 | bytes 120000000 | tf_op jit(solution)/shard_map/scatter_mlp/pallas_call | solution.py:479
  438.9 2.5 add_convert_fusion
  441.4 2.0 fusion.8
  443.4 4.8 convolution_convert_fusion.2.refs_5_
  448.2 25.1 %attend_back.1 = (bf16[2048,384]{1,0:T(8,128)(2,1)S(1)}, bf16[64,8192]{1,0:T(8,128)(2,1)S(1)}, bf16[2,64,2048]{2,1,0:T(8,128)(2,1)S(1)}) custom-call(s32[16]{0:T(128)S(1)} %compare_select_fusion.refs_0_, bf16[2048,384]{1,0:T(8,128)(2,1)S(1)} %copy-done.1, bf16[2048,2048]{1,0:T(8,128)(2,1)} %get-tuple-element.66.refs_2_, bf16[128,2048]{1,0:T(8,128)(2,1)S(1)} %copy-done.14, ...), custom_call_target="tpu_custom_call" | custom-call | flops 1073741824 | bytes 60000000 | tf_op jit(solution)/shard_map/attend_back/pallas_call | solution.py:912
  473.4 6.2 %multiply_reduce_fusion.1 = (f32[2048]{0:T(1024)S(1)}, bf16[2048,384]{1,0:T(8,128)(2,1)}) fusion(bf16[2,16,64,384]{3,2,1,0:T(8,128)(2,1)S(1)} %copy-done.3, bf16[2048,2048]{1,0:T(8,128)(2,1)S(1)} %bitcast.74, bf16[2048,384]{1,0:T(8,128)(2,1)S(1)} %get-tuple-element.68.refs_0_), kind=kOutput, calls=%fused_computation.13 | convolution fusion | flops 3224369152 | bytes 13115392 | tf_op jit(solution)/shard_map/dot_general | solution.py:21
  480.3 1.9 convert_reduce_fusion.1
  482.1 1.8 multiply_reduce_fusion
  486.9 1.8 fusion.7
  488.7 69.5 %scatter_d_norm_one.1 = (f32[128,2048]{1,0:T(8,128)S(1)}, bf16[64,2048]{1,0:T(8,128)(2,1)S(1)}, bf16[64,2048]{1,0:T(8,128)(2,1)S(1)}, bf16[64,2048]{1,0:T(8,128)...) custom-call(bf16[2048,384]{1,0:T(8,128)(2,1)S(1)} %copy-done.5, bf16[2048,384]{1,0:T(8,128)(2,1)} %bitcast.65, ...), custom_call_target="tpu_custom_call" | custom-call | flops 3221225472 | bytes 120000000 | tf_op jit(solution)/shard_map/scatter_d_norm_one/pallas_call | solution.py:479
  559.3 1.5 multiply_reduce_fusion.5
  560.8 2.8 fusion.16
  567.5 1.5 convert_element_type.129
  569.6 1.5 convert_element_type.130
  (129 shorter events, 16.2 us)
Async XLA Ops:
  95.6 1.4 copy-start.2
  97.0 1.2 copy-start.19
  98.3 30.4 %copy-start.14 = (bf16[128,2048]{1,0:T(8,128)(2,1)S(1)}, bf16[128,2048]{1,0:T(8,128)(2,1)}, u32[]{:S(2)}) copy-start(bf16[128,2048]{1,0:T(8,128)(2,1)} %get-tuple-element.52.refs_1_.refs_3_) | copy-start | bytes 1572868
  98.3 30.4 %copy-start.17 = (bf16[128,2048]{1,0:T(8,128)(2,1)S(1)}, bf16[128,2048]{1,0:T(8,128)(2,1)}, u32[]{:S(2)}) copy-start(bf16[128,2048]{1,0:T(8,128)(2,1)} %refs_3_.3) | copy-start | bytes 1572868
  98.3 30.4 %copy-start.20 = (bf16[16,64,512]{2,1,0:T(8,128)(2,1)S(1)}, bf16[16,64,512]{2,1,0:T(8,128)(2,1)}, u32[]{:S(2)}) copy-start(bf16[16,64,512]{2,1,0:T(8,128)(2,1)} %get-tuple-element.53) | copy-start | bytes 3145732
  123.2 1.2 copy-start
  124.5 1.0 copy-start.10
  125.4 3.2 copy-start.23
  128.7 75.0 %copy-start.25 = (bf16[128,2048]{1,0:T(8,128)(2,1)S(1)}, bf16[128,2048]{1,0:T(8,128)(2,1)}, u32[]{:S(2)}) copy-start(bf16[128,2048]{1,0:T(8,128)(2,1)} %refs_6_.2) | copy-start | bytes 1572868
  203.6 1.7 copy-start.21
  205.3 55.0 %copy-start.22 = (bf16[2,1024,512]{2,1,0:T(8,128)(2,1)S(1)}, bf16[2,1024,512]{2,1,0:T(8,128)(2,1)}, u32[]{:S(2)}) copy-start(bf16[2,1024,512]{2,1,0:T(8,128)(2,1)} %copy-done.21) | copy-start | bytes 6291460
  260.2 8.0 %copy-start.26 = (bf16[2,1024,512]{2,1,0:T(8,128)(2,1)S(1)}, bf16[2,1024,512]{2,1,0:T(8,128)(2,1)}, u32[]{:S(2)}) copy-start(bf16[2,1024,512]{2,1,0:T(8,128)(2,1)} %get-tuple-element.58) | copy-start | bytes 6291460
  260.3 18.8 %slice-start.2 = ((s8[8388608]{0:T(1024)(128)(4,1)}), s8[4194304]{0:T(1024)(128)(4,1)S(1)}, s32[]{:S(2)}) async-start(s8[8388608]{0:T(1024)(128)(4,1)} %bitcast.87), calls=%async_computation.2 | async-start | bytes 8388608
  260.3 24.7 %slice-start.4 = ((s8[8388608]{0:T(1024)(128)(4,1)}), s8[4194304]{0:T(1024)(128)(4,1)S(1)}, s32[]{:S(2)}) async-start(s8[8388608]{0:T(1024)(128)(4,1)} %bitcast.91), calls=%async_computation.4 | async-start | bytes 8388608
  268.2 10.9 %slice-start.3 = ((s8[8388608]{0:T(1024)(128)(4,1)}), s8[4194304]{0:T(1024)(128)(4,1)S(1)}, s32[]{:S(2)}) async-start(s8[8388608]{0:T(1024)(128)(4,1)} %bitcast.87), calls=%async_computation.3 | async-start | bytes 8388608
  268.2 16.7 %slice-start.5 = ((s8[8388608]{0:T(1024)(128)(4,1)}), s8[4194304]{0:T(1024)(128)(4,1)S(1)}, s32[]{:S(2)}) async-start(s8[8388608]{0:T(1024)(128)(4,1)} %bitcast.91), calls=%async_computation.5 | async-start | bytes 8388608
  290.6 67.6 %copy-start.24 = (f32[128,2048]{1,0:T(8,128)S(1)}, f32[128,2048]{1,0:T(8,128)}, u32[]{:S(2)}) copy-start(f32[128,2048]{1,0:T(8,128)} %get-tuple-element.97) | copy-start | bytes 3145732
  290.6 68.1 %copy-start.18 = (bf16[128,2048]{1,0:T(8,128)(2,1)S(1)}, bf16[128,2048]{1,0:T(8,128)(2,1)}, u32[]{:S(2)}) copy-start(bf16[128,2048]{1,0:T(8,128)(2,1)} %refs_3_.3) | copy-start | bytes 1572868
  358.2 2.1 copy-start.12
  436.9 1.0 copy-start.11
  441.4 32.0 %slice-start = ((s8[8388608]{0:T(1024)(128)(4,1)}), s8[4194304]{0:T(1024)(128)(4,1)S(1)}, s32[]{:S(2)}) async-start(s8[8388608]{0:T(1024)(128)(4,1)} %bitcast.73), calls=%async_computation | async-start | bytes 8388608
  443.4 4.8 copy-start.1
  443.4 30.1 %slice-start.1 = ((s8[8388608]{0:T(1024)(128)(4,1)}), s8[4194304]{0:T(1024)(128)(4,1)S(1)}, s32[]{:S(2)}) async-start(s8[8388608]{0:T(1024)(128)(4,1)} %bitcast.73), calls=%async_computation.1 | async-start | bytes 8388608
  448.2 25.2 %copy-start.3 = (bf16[2,16,64,384]{3,2,1,0:T(8,128)(2,1)S(1)}, bf16[2,16,64,384]{3,2,1,0:T(8,128)(2,1)}, u32[]{:S(2)}) copy-start(bf16[2,16,64,384]{3,2,1,0:T(8,128)(2,1)} %get-tuple-element.50) | copy-start | bytes 4718596
  473.4 6.2 %copy-start.4 = (bf16[2048,384]{1,0:T(8,128)(2,1)}, bf16[2048,384]{1,0:T(8,128)(2,1)S(1)}, u32[]{:S(2)}) copy-start(bf16[2048,384]{1,0:T(8,128)(2,1)S(1)} %get-tuple-element.68.refs_0_) | copy-start | bytes 4718596
  473.4 6.2 %copy-start.6 = (bf16[64,8192]{1,0:T(8,128)(2,1)}, bf16[64,8192]{1,0:T(8,128)(2,1)S(1)}, u32[]{:S(2)}) copy-start(bf16[64,8192]{1,0:T(8,128)(2,1)S(1)} %get-tuple-element.77) | copy-start | bytes 3145732
  473.4 6.2 %copy-start.15 = (bf16[2,64,2048]{2,1,0:T(8,128)(2,1)}, bf16[2,64,2048]{2,1,0:T(8,128)(2,1)S(1)}, u32[]{:S(2)}) copy-start(bf16[2,64,2048]{2,1,0:T(8,128)(2,1)S(1)} %get-tuple-element.76) | copy-start | bytes 1572868
  480.0 8.7 %copy-start.5 = (bf16[2048,384]{1,0:T(8,128)(2,1)S(1)}, bf16[2048,384]{1,0:T(8,128)(2,1)}, u32[]{:S(2)}) copy-start(bf16[2048,384]{1,0:T(8,128)(2,1)} %copy-done.4) | copy-start | bytes 4718596
  558.2 1.0 copy-start.8
  559.2 7.5 %copy-start.16 = (bf16[2,64,2048]{2,1,0:T(8,128)(2,1)S(1)}, bf16[2,64,2048]{2,1,0:T(8,128)(2,1)}, u32[]{:S(2)}) copy-start(bf16[2,64,2048]{2,1,0:T(8,128)(2,1)} %copy-done.15) | copy-start | bytes 1572868
  559.3 8.3 %copy-start.7 = (bf16[64,8192]{1,0:T(8,128)(2,1)S(1)}, bf16[64,8192]{1,0:T(8,128)(2,1)}, u32[]{:S(2)}) copy-start(bf16[64,8192]{1,0:T(8,128)(2,1)} %copy-done.6) | copy-start | bytes 3145732
  563.6 6.0 %copy-start.9 = (bf16[64,8192]{1,0:T(8,128)(2,1)S(1)}, bf16[64,8192]{1,0:T(8,128)(2,1)}, u32[]{:S(2)}) copy-start(bf16[64,8192]{1,0:T(8,128)(2,1)} %copy-done.8) | copy-start | bytes 3145732
  (1 other events, 1.0 us)

commit v3 on v2

--- a/solution.py
+++ b/solution.py
@@ -27,6 +27,7 @@
 EVEN = ((6, (X, Y, Z)), (5, (Y, Z, X)), (5, (Z, X, Y)))
 ROOM = ((8, (X, Z, Y)), (8, (Y, Z, X)))
 LIGHT = ((7, (Z, X, Y)), (7, (Z, Y, X)), (2, (X, Y, Z)))
+MIXED = ((6, (X, Z, Y)), (6, (Y, Z, X)), (4, (Z, X, Y)))
 
 
 class Place:
@@ -72,6 +73,11 @@
 
 def greet(place, extras=()):
     count = 0
+    if any(e.everyone for e in extras):
+        devices = place.trees * TREE_SEGS
+        pl.loop(1, devices)(lambda k: signal(place.of_flat(lax.rem(place.flat + k, devices))))
+        pl.semaphore_wait(pltpu.get_barrier_semaphore(), devices - 1)
+        return
     if any(e.peers for e in extras):
         pl.loop(1, TREE_SEGS)(lambda k: signal(place.peer(k)[1]))
         count += TREE_SEGS - 1
@@ -104,7 +110,8 @@
 
 
 class Extra:
-    peers = trees = False
+    peers = trees = everyone = False
+    bulk = 2
     ins, in_specs, outs, out_specs, scratch = (), (), (), (), ()
 
     def greet(self, place):
@@ -113,6 +120,7 @@
 
 class SpreadSmall(Extra):
     trees = True
+    bulk = 0
 
     def __init__(self, block):
         n = lax.axis_size("tree")
@@ -245,59 +253,100 @@
 class DealColumns(Extra):
     peers = True
 
-    def __init__(self, mats, all_trees=False):
-        n = lax.axis_size("tree")
-        self.trees = self.all_trees = all_trees
-        self.widths = [m.shape[1] // TREE_SEGS for m in mats]
-        rows, total = mats[0].shape[0], sum(self.widths)
-        self.ins, self.in_specs = tuple(mats), (ANYWHERE,) * len(mats)
-        shape = (TREE_SEGS, rows, total)
-        shape = (n,) + shape if all_trees else shape
-        self.outs, self.out_specs = (jax.ShapeDtypeStruct(shape, bf16),), (ANYWHERE,)
-        self.scratch = (DMA, DMA, DMA, DMA((n,)), DMA((n,)))
-
-    def start(self, place, *refs):
-        mats, (out, send, recv, keep, _, _) = refs[:-6], refs[-6:]
-        box = out.at[place.tree] if self.all_trees else out
-
-        def pieces(j):
-            lo = 0
-            for m, c in zip(mats, self.widths):
-                yield m.at[:, pl.ds(pl.multiple_of(j * c, c), c)], box.at[place.at, :, pl.ds(lo, c)]
-                lo += c
+    def __init__(self, mat):
+        rows, c = mat.shape[0], mat.shape[1] // TREE_SEGS
+        self.ins, self.in_specs = (mat,), (ANYWHERE,)
+        self.outs, self.out_specs = (jax.ShapeDtypeStruct((TREE_SEGS, rows, c), bf16),), (ANYWHERE,)
+        self.scratch = (DMA, DMA, DMA)
+
+    def start(self, place, mat, out, send, recv, keep):
+        c = out.shape[2]
+        columns = lambda j: mat.at[:, pl.ds(pl.multiple_of(j * c, c), c)]
 
         def one(k):
             j, device = place.peer(k)
-            for src, dst in pieces(j):
-                push(src, dst, send, recv, device).start()
+            push(columns(j), out.at[place.at], send, recv, device).start()
 
         pl.loop(1, TREE_SEGS)(one)
-        for src, dst in pieces(place.at):
-            pltpu.make_async_copy(src, dst, keep).start()
-
-    def finish(self, place, *refs):
-        mats, (out, send, recv, keep, _, _) = refs[:-6], refs[-6:]
-        box = out.at[place.tree] if self.all_trees else out
-        most = box.at[pl.ds(0, TREE_SEGS - 1)]
+        pltpu.make_async_copy(columns(place.at), out.at[place.at], keep).start()
+
+    def finish(self, place, mat, out, send, recv, keep):
+        most = out.at[pl.ds(0, TREE_SEGS - 1)]
         drain(most, send)
         drain(most, recv)
-        drain(box.at[0], keep)
+        drain(out.at[0], keep)
 
     def stages(self, place, *refs):
         self.start(place, *refs)
-        copies = []
-        if self.all_trees:
-            self.finish(place, *refs)
-            mine, far_send, far_recv = refs[-6].at[place.tree], refs[-2], refs[-1]
-            for k in range(1, place.trees):
-                copies.append(push(mine, mine, far_send.at[k - 1], far_recv.at[k - 1], place.in_tree(k)))
-                copies[-1].start()
         while not place.closing:
             yield
-        if not self.all_trees:
-            self.finish(place, *refs)
-        for copy in copies:
-            copy.wait()
+        self.finish(place, *refs)
+
+
+class DealAll(Extra):
+    everyone = True
+
+    def __init__(self, *mats):
+        devices = lax.axis_size("tree") * TREE_SEGS
+        self.widths = [m.shape[1] // TREE_SEGS for m in mats]
+        self.ins, self.in_specs = tuple(mats), (ANYWHERE,) * len(mats)
+        self.outs = (jax.ShapeDtypeStruct((devices, mats[0].shape[0], sum(self.widths)), bf16),)
+        self.out_specs = (ANYWHERE,)
+        self.scratch = (DMA, DMA, DMA)
+
+    def pieces(self, place, refs, tree, j):
+        mats, out = refs[:-4], refs[-4]
+        lo = 0
+        for m, c in zip(mats, self.widths):
+            yield m.at[:, pl.ds(pl.multiple_of(j * c, c), c)], out.at[place.flat, :, pl.ds(lo, c)]
+            lo += c
+
+    def blocks(self, refs):
+        return refs[-4]
+
+    def stages(self, place, *refs):
+        send, recv, keep = refs[-3:]
+
+        def one(tree, j):
+            device = (tree, j // 2, lax.rem(j, 2))
+            for src, dst in self.pieces(place, refs, tree, j):
+                push(src, dst, send, recv, device).start()
+
+        for k in range(1, place.trees):
+            tree = lax.rem(place.tree + k, place.trees)
+            pl.loop(0, TREE_SEGS)(lambda i: one(tree, lax.rem(place.at + i, TREE_SEGS)))
+        pl.loop(1, TREE_SEGS)(lambda i: one(place.tree, lax.rem(place.at + i, TREE_SEGS)))
+        for src, dst in self.pieces(place, refs, place.tree, place.at):
+            pltpu.make_async_copy(src, dst, keep).start()
+        while not place.closing:
+            yield
+        whole = self.blocks(refs)
+        most = whole.at[pl.ds(0, whole.shape[0] - 1)]
+        drain(most, send)
+        drain(most, recv)
+        drain(whole.at[0], keep)
+
+
+class DealAllRows(DealAll):
+    def __init__(self, src, widths):
+        self.widths = widths
+        rows = src.shape[1]
+        self.ins, self.in_specs = (src,), (ANYWHERE,)
+        shape = lambda c: (src.shape[0] // TREE_SEGS, rows, TREE_SEGS * c)
+        self.outs = tuple(jax.ShapeDtypeStruct(shape(c), bf16) for c in widths)
+        self.out_specs = (ANYWHERE,) * len(widths)
+        self.scratch = (DMA, DMA, DMA)
+
+    def pieces(self, place, refs, tree, j):
+        src, outs = refs[0], refs[1:-3]
+        lo = 0
+        for out, c in zip(outs, self.widths):
+            columns = pl.ds(pl.multiple_of(place.at * c, c), c)
+            yield src.at[tree * TREE_SEGS + j, :, pl.ds(lo, c)], out.at[place.tree, :, columns]
+            lo += c
+
+    def blocks(self, refs):
+        return refs[0]
 
 
 class DealRows(Extra):
@@ -343,51 +392,6 @@
         self.finish(place, *refs)
 
 
-class SwapAndDeal(DealRows):
-    trees = True
-
-    def __init__(self, src, rows, widths):
-        n = lax.axis_size("tree")
-        self.widths = widths
-        self.ins, self.in_specs = (src,), (IN_VMEM,)
-        self.outs = tuple(jax.ShapeDtypeStruct((rows, TREE_SEGS * c), bf16) for c in widths)
-        self.out_specs = (ANYWHERE,) * len(widths)
-        block = (TREE_SEGS * rows, src.shape[1])
-        self.scratch = (
-            pltpu.VMEM((max(n - 1, 1),) + block, bf16), pltpu.VMEM((TREE_SEGS, rows, src.shape[1]), bf16),
-            DMA((n,)), DMA((n,)), DMA, DMA, DMA,
-        )
-
-    def stages(self, place, src, *refs):
-        n = len(self.widths)
-        outs, (box, total, far_send, far_recv), sems = refs[:n], refs[n : n + 4], refs[n + 4 :]
-        rows = total.shape[1]
-        share = TREE_SEGS * rows
-        copies = []
-        for k in range(1, place.trees):
-            tree = lax.rem(place.tree + k, place.trees)
-            theirs = src.at[pl.ds(pl.multiple_of(tree * share, share), share)]
-            copies.append(push(theirs, box.at[k - 1], far_send.at[k - 1], far_recv.at[k - 1], place.in_tree(k)))
-            copies[-1].start()
-        while not place.closing:
-            yield
-        for copy in copies:
-            copy.wait_recv()
-
-        def add(j):
-            at = pl.ds(pl.multiple_of(j * rows, rows), rows)
-            value = src[pl.ds(pl.multiple_of(place.tree * share + j * rows, rows), rows), :].astype(f32)
-            for k in range(1, place.trees):
-                value = value + box[k - 1, at, :].astype(f32)
-            total[j] = value.astype(bf16)
-
-        pl.loop(0, TREE_SEGS)(add)
-        self.start(place, total, *outs, *sems)
-        self.finish(place, total, *outs, *sems)
-        for copy in copies:
-            copy.wait_send()
-
-
 class HeadRows(Extra):
     def __init__(self, shard):
         self.rows = shard.shape[0]
@@ -402,25 +406,24 @@
             signal(place.of_flat(place.at * per_head + b))
         return place.trees
 
-    def stages(self, place, src, out, send, recv):
+    def each(self, place, src, out, send, recv, do_far, do_own):
         at = place.flat * self.rows
         head = at // HEAD_DIM
         dst = out.at[pl.ds(pl.multiple_of(lax.rem(at, HEAD_DIM), self.rows), self.rows)]
-
-        def each(do_far, do_own):
-            for t in range(place.trees):
-                own = (place.tree == t) & (place.at == head)
-                pl.when(jnp.logical_not(own))(lambda t=t: do_far(
-                    push(src, dst, send.at[t], recv, (t, head // 2, lax.rem(head, 2)))
-                ))
-                if do_own:
-                    pl.when(own)(lambda: do_own(pltpu.make_async_copy(src, dst, recv)))
-
-        each(lambda copy: copy.start(), lambda copy: copy.start())
-        while not place.closing:
-            yield
-        each(lambda copy: copy.wait_send(), None)
-        drain(out, recv)
+        for t in range(place.trees):
+            own = (place.tree == t) & (place.at == head)
+            pl.when(jnp.logical_not(own))(lambda t=t: do_far(
+                push(src, dst, send.at[t], recv, (t, head // 2, lax.rem(head, 2)))
+            ))
+            if do_own:
+                pl.when(own)(lambda: do_own(pltpu.make_async_copy(src, dst, recv)))
+
+    def start(self, place, *refs):
+        self.each(place, *refs, lambda copy: copy.start(), lambda copy: copy.start())
+
+    def finish(self, place, *refs):
+        self.each(place, *refs, lambda copy: copy.wait_send(), None)
+        drain(refs[1], refs[3])
 
 
 class HeadRowsBack(Extra):
@@ -455,6 +458,28 @@
     def finish(self, place, *refs):
         self.each(place, *refs, lambda copy: copy.wait_send(), None)
         drain(refs[1], refs[3])
+
+
+class Product(Extra):
+    def __init__(self, left, right, dim, kind):
+        self.dim = dim
+        m, n = left.shape[1 - dim], right.shape[1]
+        self.ins, self.in_specs = (left, right), (ANYWHERE, IN_VMEM)
+        self.outs, self.out_specs = (jax.ShapeDtypeStruct((m, n), kind),), (IN_VMEM,)
+        self.scratch = (pltpu.VMEM(left.shape, left.dtype), DMA)
+
+    def stages(self, place, left, right, out, held, sem):
+        copy = pltpu.make_async_copy(left, held, sem)
+        copy.start()
+        yield
+        copy.wait()
+        count = 4
+        block = out.shape[0] // count
+        for j in range(count):
+            at = pl.ds(j * block, block)
+            part = held[at, :] if self.dim == 1 else held[:, at]
+            out[at, :] = dot(part, right[...], self.dim, 0).astype(out.dtype)
+            yield
 
 
 def finish(place, extras, running):
@@ -497,6 +522,8 @@
 
 
 class GatherRows(Extra):
+    bulk = 1
+
     def __init__(self, x, plan):
         tok, width = x.shape
         self.plan = plan
@@ -590,8 +617,9 @@
     place = Place(trees)
     greet(place, extras)
     running = [e.stages(place, *r) for e, r in zip(extras, extra_refs)]
+    turn = sorted(zip(extras, running), key=lambda e: e[0].bulk)
     for _ in range(8):
-        for stages in running:
+        for _, stages in turn:
             next(stages, None)
     finish(place, extras, running)
 
@@ -641,12 +669,15 @@
         )
 
     groups = (Z | Y, Z, Y, 0)
-    for k, zy in enumerate(groups):
-        def put_out(at, res, k=k):
+
+    def for_partner(k):
+        def put_out(at, res):
             pout[k, :, pl.ds(at, tile)] = res.astype(bf16)
-        product(zy, 1, put_out)
+        product(groups[k], 1, put_out)
         pair(k).start()
-    advance()
+
+    for_partner(0)
+    for_partner(1)
 
     def hop(p, r, step, slot):
         lo, n = cols[p]
@@ -661,6 +692,10 @@
         def put_own(at, res, k=k):
             acc[k, :, pl.ds(at, tile)] = res
         product(zy, 0, put_own)
+        if k + 2 < len(groups):
+            for_partner(k + 2)
+        if k == 1:
+            advance()
         pair(k).wait_recv()
         for rx in (X, 0):
             r = zy | rx
@@ -739,7 +774,7 @@
     return call(
         functools.partial(scatter_kernel, plan, rhs_dim, tok), extras, [left, right], [IN_VMEM, IN_VMEM],
         [jax.ShapeDtypeStruct((tok, width), f32)], [IN_VMEM],
-        scratch, cid, name, 2 * tokens * width * inner, 48 * 2**20,
+        scratch, cid, name, 2 * tokens * width * inner, 56 * 2**20,
     )
 
 
@@ -802,16 +837,17 @@
     return q, k, v, probs, own, trunk, branches, parent
 
 
-def attend_kernel(deal, trees, *refs):
-    (parent_ref, x_ref, gain_ref, bias_ref, w_ref, b_ref), (n_ref, qkv_ref, ctx_ref), (held,), deal_refs = sorted_refs(
-        (deal,), refs, 6, 3
-    )
+def attend_kernel(extras, trees, *refs):
+    own_in, own_out, (held,), extra_refs = sorted_refs(extras, refs, 6, 3)
+    parent_ref, x_ref, gain_ref, bias_ref, w_ref, b_ref = own_in
+    n_ref, qkv_ref, ctx_ref = own_out
     place = Place(trees)
 
     @pl.when(pl.program_id(0) == 0)
     def _():
-        greet(place, (deal,))
-        deal.start(place, *deal_refs[0])
+        greet(place, extras)
+        for e, r in zip(extras, extra_refs):
+            e.start(place, *r)
 
     step = pl.program_id(0)
     rows = x_ref.shape[0]
@@ -830,38 +866,42 @@
             ctx_ref[own, :] = dot(probs.astype(bf16), v, 1, 0).astype(bf16)
 
         pl.loop(0, TREE_SEGS, unroll=2)(one)
-        deal.finish(place, *deal_refs[0])
-
-
-def attend(parent, x_full, gain, bias, w, b, deal, cid):
+        for e, r in zip(extras, extra_refs):
+            e.finish(place, *r)
+
+
+def attend(parent, x_full, gain, bias, w, b, extras, cid):
     tokens, width = x_full.shape
     n = 3 * HEAD_DIM
     rows = 256
     whole = lambda shape: pl.BlockSpec(shape, lambda i: (0,) * len(shape))
     by_row = lambda cols: pl.BlockSpec((rows, cols), lambda i: (i, 0))
     return pl.pallas_call(
-        functools.partial(attend_kernel, deal, lax.axis_size("tree")),
+        functools.partial(attend_kernel, extras, lax.axis_size("tree")),
         grid=(tokens // rows,),
         in_specs=[
             pl.BlockSpec(memory_space=pltpu.SMEM), by_row(width), whole((1, width)), whole((1, width)), whole((width, n)),
-            whole((1, n)), *deal.in_specs,
+            whole((1, n)), *[i for e in extras for i in e.in_specs],
         ],
-        out_specs=[by_row(width), by_row(n), whole((tokens, HEAD_DIM)), *deal.out_specs],
-        scratch_shapes=[*deal.scratch, pltpu.VMEM((tokens, n), bf16)],
+        out_specs=[by_row(width), by_row(n), whole((tokens, HEAD_DIM)), *[o for e in extras for o in e.out_specs]],
+        scratch_shapes=[*[i for e in extras for i in e.scratch], pltpu.VMEM((tokens, n), bf16)],
         out_shape=[
             jax.ShapeDtypeStruct((tokens, width), bf16),
             jax.ShapeDtypeStruct((tokens, n), bf16),
             jax.ShapeDtypeStruct((tokens, HEAD_DIM), bf16),
-            *deal.outs,
+            *[o for e in extras for o in e.outs],
         ],
         compiler_params=pltpu.CompilerParams(collective_id=cid, has_side_effects=True, vmem_limit_bytes=40 * 2**20),
         cost_estimate=pl.CostEstimate(flops=2 * tokens * width * n, bytes_accessed=60_000_000, transcendentals=0),
         name="attend",
-    )(parent, x_full, gain, bias, w, b, *deal.ins)
+    )(parent, x_full, gain, bias, w, b, *[a for e in extras for a in e.ins])
 
 
 def attend_back_kernel(extras, trees, *refs):
-    (parent_ref, qkv_ref, d_ref, w_ref), (o_ref,), (dk, dv, d_ctx), extra_refs = sorted_refs(extras, refs, 4, 1)
+    own_in, own_out, own_scratch, extra_refs = sorted_refs(extras, refs, 5, 2)
+    parent_ref, qkv_ref, d_ref, w_ref, n_ref = own_in
+    o_ref, g_ref = own_out
+    dk, dv, d_ctx, held, sem = own_scratch
     place = Place(trees)
     step = pl.program_id(0)
 
@@ -870,6 +910,7 @@
         greet(place, extras)
         for e, r in zip(extras, extra_refs):
             e.start(place, *r)
+        pltpu.make_async_copy(n_ref, held, sem).start()
 
     rows = d_ref.shape[0]
     tok = qkv_ref.shape[0] // TREE_SEGS
@@ -900,11 +941,16 @@
         pl.loop(0, TREE_SEGS, unroll=2)(one)
         o_ref[:, pl.ds(hd, hd)] = (dk[...] * scale).astype(bf16)
         o_ref[:, pl.ds(2 * hd, hd)] = dv[...].astype(bf16)
+        drain(held, sem)
+        block = 512
+        for j in range(held.shape[1] // block):
+            at = pl.ds(j * block, block)
+            g_ref[at, :] = dot(held[:, at], o_ref[...], 0, 0)
         for e, r in zip(extras, extra_refs):
             e.finish(place, *r)
 
 
-def attend_back(parent, qkv, d_full, w_rows, extras, cid):
+def attend_back(parent, qkv, d_full, w_rows, norm_one, extras, cid):
     tokens, width = d_full.shape
     n = qkv.shape[1]
     rows = 256
@@ -914,18 +960,52 @@
         grid=(tokens // rows,),
         in_specs=[
             pl.BlockSpec(memory_space=pltpu.SMEM), whole((tokens, n)), pl.BlockSpec((rows, width), lambda i: (i, 0)),
-            whole((HEAD_DIM, width)), *[i for e in extras for i in e.in_specs],
+            whole((HEAD_DIM, width)), ANYWHERE, *[i for e in extras for i in e.in_specs],
         ],
-        out_specs=[whole((tokens, n)), *[o for e in extras for o in e.out_specs]],
+        out_specs=[whole((tokens, n)), whole((width, n)), *[o for e in extras for o in e.out_specs]],
         scratch_shapes=[
             *[i for e in extras for i in e.scratch],
             pltpu.VMEM((tokens, HEAD_DIM), f32), pltpu.VMEM((tokens, HEAD_DIM), f32), pltpu.VMEM((tokens, HEAD_DIM), bf16),
+            pltpu.VMEM((tokens, width), bf16), DMA,
         ],
-        out_shape=[jax.ShapeDtypeStruct((tokens, n), bf16), *[o for e in extras for o in e.outs]],
+        out_shape=[
+            jax.ShapeDtypeStruct((tokens, n), bf16), jax.ShapeDtypeStruct((width, n), f32), *[o for e in extras for o in e.outs],
+        ],
         compiler_params=pltpu.CompilerParams(collective_id=cid, has_side_effects=True, vmem_limit_bytes=40 * 2**20),
         cost_estimate=pl.CostEstimate(flops=2 * tokens * width * HEAD_DIM, bytes_accessed=60_000_000, transcendentals=0),
         name="attend_back",
-    )(parent, qkv, d_full, w_rows, *[a for e in extras for a in e.ins])
+    )(parent, qkv, d_full, w_rows, norm_one, *[a for e in extras for a in e.ins])
+
+
+def feed_forward_kernel(n_ref, c_ref, wu_ref, wd_ref, b_ref, active_ref, d_ref, sum_ref):
+    act, der = gelu_pair(dot(n_ref[...], wu_ref[...], 1, 0) + b_ref[...])
+    active_ref[...] = act.astype(bf16)
+    d = (dot(c_ref[...], wd_ref[...], 1, 0) * der).astype(bf16)
+    d_ref[...] = d
+
+    @pl.when(pl.program_id(0) == 0)
+    def _():
+        sum_ref[...] = jnp.zeros_like(sum_ref)
+
+    sum_ref[...] += jnp.sum(d.astype(f32).reshape(-1, 8, d.shape[1]), axis=0)
+
+
+def feed_forward(n_full, c_full, wu, wd, b):
+    tokens, width = n_full.shape
+    n = wu.shape[1]
+    rows = 256
+    whole = lambda shape: pl.BlockSpec(shape, lambda i: (0,) * len(shape))
+    by_row = lambda cols: pl.BlockSpec((rows, cols), lambda i: (i, 0))
+    return pl.pallas_call(
+        feed_forward_kernel,
+        grid=(tokens // rows,),
+        in_specs=[by_row(width), by_row(width), whole((width, n)), whole((width, n)), whole((1, n))],
+        out_specs=[by_row(n), by_row(n), whole((8, n))],
+        out_shape=[jax.ShapeDtypeStruct((tokens, n), bf16)] * 2 + [jax.ShapeDtypeStruct((8, n), f32)],
+        compiler_params=pltpu.CompilerParams(vmem_limit_bytes=40 * 2**20),
+        cost_estimate=pl.CostEstimate(flops=4 * tokens * width * n, bytes_accessed=4 * tokens * width, transcendentals=0),
+        name="feed_forward",
+    )(n_full, c_full, wu, wd, b[None])
 
 
 def body(
@@ -942,12 +1022,17 @@
     me = lax.axis_index(GROUP)
     head = lambda v: lax.dynamic_slice_in_dim(v, me * HEAD_DIM, HEAD_DIM)
 
-    smalls = jnp.concatenate([gain_one, bias_one, b_query, b_value, b_out, gain_two, bias_two, b_down, b_up])
-    n_small = smalls.shape[0]
-    block = jnp.pad(smalls, (0, 16 * 128 - n_small)).reshape(16, 128)
-
-    x_full, box, w_orow, w_att, share_up = tree_gather(inputs, 0, "gather_inputs", ROOM, extras=(
-        SpreadSmall(block), HeadRows(w_out), DealColumns((w_query, w_key, w_value), all_trees=True), DealColumns((w_up,)),
+    vectors = (gain_one, bias_one, b_query, b_value, b_out, gain_two, bias_two, b_down, b_up)
+    n_small = sum(v.shape[0] for v in vectors)
+    block = jnp.zeros((16 * 128,), bf16)
+    at = 0
+    for v in vectors:
+        block = block + jnp.pad(v, (at, 16 * 128 - at - v.shape[0]))
+        at += v.shape[0]
+    block = block.reshape(16, 128)
+
+    x_full, box, w_att = tree_gather(inputs, 0, "gather_inputs", LIGHT, extras=(
+        SpreadSmall(block), DealAll(w_query, w_key, w_value),
     ))
     w_att = w_att.reshape(width, -1)
     packed = box.transpose(1, 0, 2, 3).reshape(devices, -1)[:, :n_small]
@@ -960,42 +1045,39 @@
     parent = jnp.where(local_seg >= 2 * TRUNK_SEGS, own_parents, local_seg)
 
     b_qkv = jnp.concatenate([head(b_query), jnp.zeros((HEAD_DIM,), f32), head(b_value)])
-    norm_one, qkv, context, share_down = attend(
-        parent, x_full, gain_one[None], bias_one[None], w_att, b_qkv[None], DealColumns((w_down,)), 9
+    norm_one, qkv, context, w_orow, share_up, share_down = attend(
+        parent, x_full, gain_one[None], bias_one[None], w_att, b_qkv[None],
+        (HeadRows(w_out), DealColumns(w_up), DealColumns(w_down)), 9
     )
-    att, wu, c_full = product_scatter(context, w_orow, 0, 2, "scatter_attended", ROOM, extras=(
-        ToTrees(share_up.reshape(-1, fs)), GatherRows(cotangent, ROOM),
+    att, wd, c_full = product_scatter(context, w_orow, 0, 2, "scatter_attended", LIGHT, extras=(
+        ToTrees(share_down.reshape(-1, fs)), GatherRows(cotangent, ROOM),
     ))
-    wu = wu.reshape(width, fs)
+    wd = wd.reshape(width, fs)
     x_own = inputs.astype(f32)
     residual = x_own + att + b_out
     n_two, root_two = norm_stats(residual)
     norm_two = (n_two * gain_two + bias_two).astype(bf16)
-    nt_full, wd = tree_gather(norm_two, 3, "gather_norm_two", ROOM, extras=(ToTrees(share_down.reshape(-1, fs)),))
-    wd = wd.reshape(width, fs)
-
-    upward = dot(nt_full, wu, 1, 0) + lax.dynamic_slice_in_dim(b_up, me * fs, fs)
-    act, der = gelu_pair(upward)
-    active = act.astype(bf16)
-    d_up = (dot(c_full, wd, 1, 0) * der).astype(bf16)
+    nt_full, wu = tree_gather(norm_two, 3, "gather_norm_two", LIGHT, extras=(ToTrees(share_up.reshape(-1, fs)),))
+    wu = wu.reshape(width, fs)
+
+    active, d_up, gb_up = feed_forward(nt_full, c_full, wu, wd, lax.dynamic_slice_in_dim(b_up, me * fs, fs))
     g_up = dot(nt_full, d_up, 0, 0).astype(bf16)
-    g_down = dot(c_full, active, 0, 0).astype(bf16)
-    g_up, g_down, d_up = lax.optimization_barrier((g_up, g_down, d_up))
-    d_norm_two, swap_up = product_scatter(d_up, wu, 1, 4, "scatter_d_norm_two", LIGHT, extras=(SwapTrees(g_up),))
+    d_norm_two, g_up, g_down = product_scatter(d_up, wu, 1, 4, "scatter_d_norm_two", MIXED, extras=(
+        DealAllRows(g_up.reshape(devices, rows, fs), (fs,)), Product(c_full, active, 0, bf16),
+    ))
 
     cot = cotangent.astype(f32)
     d_res = cot + norm_back(d_norm_two, n_two, root_two, gain_two)
     d_att = d_res.astype(bf16)
-    mlp, swap_down, da_full = product_scatter(active, wd, 1, 5, "scatter_mlp", ROOM, extras=(
+    mlp, swap_down, da_full = product_scatter(active, wd, 1, 5, "scatter_mlp", LIGHT, extras=(
         SwapTrees(g_down), GatherRows(d_att, ROOM),
     ))
-    g_up, g_down = own_rows(g_up, swap_up, rows), own_rows(g_down, swap_down, rows)
+    g_down = own_rows(g_down, swap_down, rows)
     g_orow = dot(context, da_full, 0, 0).astype(bf16)
-    d_qkv, g_up, g_o = attend_back(
-        parent, qkv, da_full, w_orow, (DealRows(g_up, (fs,)), HeadRowsBack(g_orow, rows)), 10
+    d_qkv, g_qkv, g_down, g_o = attend_back(
+        parent, qkv, da_full, w_orow, norm_one, (DealRows(g_down, (fs,)), HeadRowsBack(g_orow, rows)), 10
     )
 
-    g_qkv = dot(norm_one, d_qkv, 0, 0)
     s_qkv = jnp.sum(d_qkv.astype(f32), axis=0)
     w_f = w_att.astype(f32)
     gb_one = jnp.sum(w_f * s_qkv, axis=1)
@@ -1011,10 +1093,10 @@
         col(d_att.astype(f32)), col(d_norm_two * n_two), col(d_norm_two), col(cot),
     ]
     sums = jnp.stack(sums).reshape(8, devices, rows).transpose(1, 0, 2).reshape(devices, 8 * rows)
-    sums = jnp.concatenate([sums, placed(col(d_up.astype(f32)), ff).reshape(devices, -1)], axis=1)
+    sums = jnp.concatenate([sums, placed(col(gb_up), ff).reshape(devices, -1)], axis=1)
     sums = jnp.pad(sums, ((0, 0), (0, 1024 - n_small))).reshape(trees, TREE_SEGS, 8, 128).transpose(1, 0, 2, 3)
-    d_norm_one, g_q, g_k, g_v, sums, g_down = product_scatter(d_qkv, w_att, 1, 7, "scatter_d_norm_one", LIGHT, extras=(
-        SwapAndDeal(g_att, rows, (HEAD_DIM,) * 3), ReduceSmall(sums), DealRows(g_down, (fs,)),
+    d_norm_one, g_q, g_k, g_v, sums = product_scatter(d_qkv, w_att, 1, 7, "scatter_d_norm_one", LIGHT, extras=(
+        DealAllRows(g_att.reshape(devices, rows, -1), (HEAD_DIM,) * 3), ReduceSmall(sums),
     ))
     sums = sums.reshape(-1)
     parts = [sums[j * rows : (j + 1) * rows] for j in range(8)]
@@ -1024,8 +1106,8 @@
     grad_inputs = d_res + norm_back(d_norm_one, n_one, root_one, gain_one)
 
     layer_output = (residual + mlp + b_down).astype(bf16)
-    g_q, g_k, g_v, g_up, g_down = (g.astype(f32) for g in (g_q, g_k, g_v, g_up, g_down))
-    g_o = jnp.sum(g_o.astype(f32), axis=0)
+    g_q, g_k, g_v, g_o, g_up = (jnp.sum(g.astype(f32), axis=0) for g in (g_q, g_k, g_v, g_o, g_up))
+    g_down = g_down.astype(f32)
     return (
         layer_output, grad_inputs, parts[0], parts[1], g_q, parts[2], g_k, g_v, parts[3], g_o, parts[4],
         parts[5], parts[6], g_up, gb_up, g_down, parts[7],

time: 580 us -> 538 us (0.928)
  matrix products: 41.3 us -> 10.6 us
  Pallas kernels: 475 us -> 467 us
    pallas_call x6, Pallas kernels: 425 us -> 388 us  [call(): pl.pallas_call(functools.partial(kernel, extras, lax.axis_size('tree')),...]
    dot_general x6 -> x2, matrix products: 41.3 us -> 10.6 us  [dot(): lax.dot_general(a, b, (((ca,), (cb,)), ((), ())), preferred_element_type=...]
    pallas_call x1 -> x2, Pallas kernels: 24.9 us -> 49.9 us  [the longest x1 36.5 us: attend(): pl.pallas_call(functools.partial(attend_kernel, extras, lax.axis_size('tr...]
    reduce_sum x1 -> x6, other arithmetic: 0.87 us -> 9.68 us  [the longest x5 5.17 us: body(): jnp.sum(g.astype(f32), axis=0)]
    concatenate x1 -> x0, local copies, waits for them, and re-layouts: 6.08 us -> none  [body(): jnp.concatenate([gain_one, bias_one, b_query, b_value, b_out, gain_two, b...]
    unnamed x69 -> x71, local copies, waits for them, and re-layouts: 11.1 us -> 14.1 us
where the time goes in v3:
time: 538 us; the launch traced here: 528 us
  Pallas kernels  467 us (87%)
  other arithmetic  29.6 us (6%)
  local copies, waits for them, and re-layouts  19.8 us (4%)
  matrix products  10.6 us (2%)
    pallas_call x6, Pallas kernels, call(): pl.pallas_call(functools.partial(kernel, extras, lax.axis_size('tree')),...  388 us
    pallas_call x1, Pallas kernels, attend(): pl.pallas_call(functools.partial(attend_kernel, extras, lax.axis_size('tr...  36.5 us
    pallas_call x1, Pallas kernels, attend_back(): pl.pallas_call(functools.partial(attend_back_kernel, extras, lax.axis_siz...  28.9 us
    unnamed x71, local copies, waits for them, and re-layouts  14.1 us
    pallas_call x1, Pallas kernels, feed_forward(): pl.pallas_call(feed_forward_kernel, grid=(tokens // rows,), in_specs=[by_...  13.4 us

profile of v3, /device:TPU:0, one launch (start us, length us, event | category | flops | bytes accessed | tf_op | source)
XLA Modules:
  0.0 528.3 jit_solution(14101851035510489827)
XLA Ops:
  0.7 1.5 add_bitcast_fusion.refs_0_
  2.2 62.7 %gather_inputs.1 = (bf16[16,2,16,128]{3,2,1,0:T(8,128)(2,1)}, bf16[32,64,384]{2,1,0:T(8,128)(2,1)}, bf16[2048,2048]{1,0:T(8,128)(2,1)}) custom-call(bf16[16,128]{1,0:T(8,128)(2,1)} %add_bitcast_fusion.refs_0_, bf16[64,2048]{1,0:T(8,128)(2,1)} %refs_1_.1, bf16[64,2048]{1,0:T(8,128)(2,1)} %refs_2_.1, bf16[64,2048]{1,0:T(8,128)(2,1)} %refs_3_.2, ...), custom_call_target="tpu_custom_call" | custom-call | bytes 120000000 | tf_op jit(solution)/shard_map/gather_inputs/pallas_call | solution.py:504
  66.9 1.4 copy-done
  68.3 1.2 copy-done.10
  69.5 36.5 %attend.1 = (bf16[2048,2048]{1,0:T(8,128)(2,1)}, bf16[2048,384]{1,0:T(8,128)(2,1)S(1)}, bf16[2048,128]{1,0:T(8,128)(2,1)S(1)}, bf16[128,2048]{1,0:T(8,128)(2,1)S...) custom-call(s32[16]{0:T(128)S(1)} %compare_select_fusion.refs_0_, ...), custom_call_target="tpu_custom_call" | custom-call | flops 3221225472 | bytes 60000000 | tf_op jit(solution)/shard_map/attend/pallas_call | solution.py:879
  106.8 1.0 copy-done.11
  108.6 1.0 copy-done.17
  109.6 72.0 %scatter_attended.1 = (f32[128,2048]{1,0:T(8,128)}, bf16[2,1024,512]{2,1,0:T(8,128)(2,1)}, bf16[2048,2048]{1,0:T(8,128)(2,1)}) custom-call(bf16[2048,128]{1,0:T(8,128)(2,1)} %copy-done.6, bf16[128,2048]{1,0:T(8,128)(2,1)} %copy-done.12, bf16[1024,512]{1,0:T(8,128)(2,1)} %bitcast.62, bf16[128,2048]{1,0:T(8,128)(2,1)} %refs_3_.3), custom_call_target="tpu_custom_call" | custom-call | flops 1073741824 | bytes 120000000 | tf_op jit(solution)/shard_map/scatter_attended/pallas_call | solution.py:504
  181.8 1.6 fusion.15
  183.8 1.1 add_convert_fusion.1.refs_1_
  184.9 51.3 %gather_norm_two.1 = (bf16[2,1024,512]{2,1,0:T(8,128)(2,1)}, bf16[2048,2048]{1,0:T(8,128)(2,1)}) custom-call(bf16[1024,512]{1,0:T(8,128)(2,1)} %bitcast.60, bf16[128,2048]{1,0:T(8,128)(2,1)} %add_convert_fusion.1.refs_1_), custom_call_target="tpu_custom_call" | custom-call | bytes 120000000 | tf_op jit(solution)/shard_map/gather_norm_two/pallas_call | solution.py:504
  236.3 1.6 copy-done.4
  237.9 1.6 copy-done.18
  239.5 13.4 %feed_forward.1 = (bf16[2048,512]{1,0:T(8,128)(2,1)S(1)}, bf16[2048,512]{1,0:T(8,128)(2,1)S(1)}, f32[8,512]{1,0:T(8,128)S(1)}) custom-call(bf16[2048,2048]{1,0:T(8,128)(2,1)} %get-tuple-element.57.n_ref, bf16[2048,2048]{1,0:T(8,128)(2,1)} %get-tuple-element.58.c_ref.refs_3_, bf16[2048,512]{1,0:T(8,128)(2,1)S(1)} %bitcast.59, bf16[2048,512]{1,0:T(8,128)(2,1)S(1)} %bitcast.64, ...), custom_call_target="tpu_custom_call" | custom-call | flops 8589934592 | bytes 16777216 | tf_op jit(solution)/shard_map/feed_forward/pallas_call | solution.py:999
  253.0 5.8 %convolution_convert_fusion = bf16[2048,512]{1,0:T(8,128)(2,1)} fusion(bf16[2048,2048]{1,0:T(8,128)(2,1)S(1)} %copy-done.33, bf16[2048,512]{1,0:T(8,128)(2,1)S(1)} %get-tuple-element.62.refs_0_), kind=kOutput, calls=%fused_computation.4 | convolution fusion | flops 4296015872 | bytes 12582912 | tf_op jit(solution)/shard_map/dot_general | solution.py:21
  258.8 65.4 %scatter_d_norm_two.1 = (f32[128,2048]{1,0:T(8,128)}, bf16[2,64,8192]{2,1,0:T(8,128)(2,1)}, bf16[2048,512]{1,0:T(8,128)(2,1)}) custom-call(bf16[2048,512]{1,0:T(8,128)(2,1)} %copy-done.5, bf16[2048,512]{1,0:T(8,128)(2,1)} %bitcast.58, bf16[32,64,512]{2,1,0:T(8,128)(2,1)} %bitcast.65, bf16[2048,2048]{1,0:T(8,128)(2,1)} %get-tuple-element.58.c_ref.refs_3_, ...), custom_call_target="tpu_custom_call" | custom-call | flops 4294967296 | bytes 120000000 | tf_op jit(solution)/shard_map/scatter_d_norm_two/pallas_call | solution.py:504
  324.3 1.8 multiply_reduce_fusion.2
  326.1 1.8 convert_reduce_fusion.8
  327.9 71.9 %scatter_mlp.1 = (f32[128,2048]{1,0:T(8,128)}, bf16[1,1024,512]{2,1,0:T(8,128)(2,1)}, bf16[2048,2048]{1,0:T(8,128)(2,1)}) custom-call(bf16[2048,512]{1,0:T(8,128)(2,1)} %copy-done.3, bf16[2048,512]{1,0:T(8,128)(2,1)} %bitcast.63, bf16[2048,512]{1,0:T(8,128)(2,1)} %get-tuple-element.63.refs_2_, bf16[128,2048]{1,0:T(8,128)(2,1)} %get-tuple-element.96.refs_3_), custom_call_target="tpu_custom_call" | custom-call | flops 4294967296 | bytes 120000000 | tf_op jit(solution)/shard_map/scatter_mlp/pallas_call | solution.py:504
  399.8 4.7 convolution_convert_fusion.1.refs_6_
  404.6 1.5 fusion
  406.1 1.0 copy-done.13
  407.2 28.9 %attend_back.1 = (bf16[2048,384]{1,0:T(8,128)(2,1)S(1)}, f32[2048,384]{1,0:T(8,128)S(1)}, bf16[64,8192]{1,0:T(8,128)(2,1)S(1)}, bf16[2,64,2048]{2,1,0:T(8,128)(2,1)S(1)}) custom-call(s32[16]{0:T(128)S(1)} %compare_select_fusion.refs_0_, bf16[2048,384]{1,0:T(8,128)(2,1)S(1)} %get-tuple-element.66.refs_1_, bf16[2048,2048]{1,0:T(8,128)(2,1)} %get-tuple-element.67.refs_2_, ...), custom_call_target="tpu_custom_call" | custom-call | flops 1073741824 | bytes 60000000 | tf_op jit(solution)/shard_map/attend_back/pallas_call | solution.py:958
  436.1 1.7 copy-done.2
  437.7 1.1 copy-done.8
  440.4 4.5 multiply_reduce_fusion.1
  448.7 64.6 %scatter_d_norm_one.1 = (f32[128,2048]{1,0:T(8,128)}, bf16[2,64,2048]{2,1,0:T(8,128)(2,1)}, bf16[2,64,2048]{2,1,0:T(8,128)(2,1)}, bf16[2,64,2048]{2,1,0:T(8,128)(2,1)}, f32[8,128]{1,0:T(8,128)}) custom-call(bf16[2048,384]{1,0:T(8,128)(2,1)} %copy-done.8, bf16[2048,384]{1,0:T(8,128)(2,1)} %bitcast.55, bf16[32,64,384]{2,1,0:T(8,128)(2,1)} %bitcast.66, ...), custom_call_target="tpu_custom_call" | custom-call | flops 3221225472 | bytes 120000000 | tf_op jit(solution)/shard_map/scatter_d_norm_one/pallas_call | solution.py:504
  513.4 1.6 multiply_reduce_fusion.5
  515.1 2.8 fusion.8
  521.6 1.5 convert_element_type.121
  524.1 2.1 add_convert_fusion
  526.2 1.7 convert_reduce_fusion
  (124 shorter events, 14.3 us)
Async XLA Ops:
  0.7 66.0 %copy-start.32 = (s32[32]{0:T(128)S(1)}, s32[32]{0:T(128)}, u32[]{:S(2)}) copy-start(s32[32]{0:T(128)} %param.34) | copy-start | bytes 388
  0.7 66.2 %copy-start.16 = (bf16[64,2048]{1,0:T(8,128)(2,1)S(1)}, bf16[64,2048]{1,0:T(8,128)(2,1)}, u32[]{:S(2)}) copy-start(bf16[64,2048]{1,0:T(8,128)(2,1)} %refs_6_.1) | copy-start | bytes 786436
  0.7 66.2 %copy-start.9 = (bf16[64,8192]{1,0:T(8,128)(2,1)S(1)}, bf16[64,8192]{1,0:T(8,128)(2,1)}, u32[]{:S(2)}) copy-start(bf16[64,8192]{1,0:T(8,128)(2,1)} %refs_7_.1) | copy-start | bytes 3145732
  66.9 1.4 copy-start
  68.3 1.2 copy-start.10
  106.8 1.0 copy-start.11
  108.6 1.0 copy-start.17
  109.6 72.1 %copy-start.21 = (bf16[128,2048]{1,0:T(8,128)(2,1)S(1)}, bf16[128,2048]{1,0:T(8,128)(2,1)}, u32[]{:S(2)}) copy-start(bf16[128,2048]{1,0:T(8,128)(2,1)} %refs_4_.1) | copy-start | bytes 1572868
  183.4 142.6 %copy-start.19 = (f32[128,2048]{1,0:T(8,128)}, f32[128,2048]{1,0:T(8,128)S(1)}, u32[]{:S(2)}) copy-start(f32[128,2048]{1,0:T(8,128)S(1)} %get-tuple-element.99) | copy-start | bytes 3145732
  236.3 1.6 copy-start.4
  237.9 1.6 copy-start.18
  239.5 13.5 %copy-start.33 = (bf16[2048,2048]{1,0:T(8,128)(2,1)S(1)}, bf16[2048,2048]{1,0:T(8,128)(2,1)}, u32[]{:S(2)}) copy-start(bf16[2048,2048]{1,0:T(8,128)(2,1)} %get-tuple-element.57.n_ref) | copy-start | bytes 25165828
  252.9 5.8 %copy-start.3 = (bf16[2048,512]{1,0:T(8,128)(2,1)}, bf16[2048,512]{1,0:T(8,128)(2,1)S(1)}, u32[]{:S(2)}) copy-start(bf16[2048,512]{1,0:T(8,128)(2,1)S(1)} %get-tuple-element.61.refs_4_.refs_0_) | copy-start | bytes 6291460
  253.0 5.8 %copy-start.5 = (bf16[2048,512]{1,0:T(8,128)(2,1)}, bf16[2048,512]{1,0:T(8,128)(2,1)S(1)}, u32[]{:S(2)}) copy-start(bf16[2048,512]{1,0:T(8,128)(2,1)S(1)} %get-tuple-element.62.refs_0_) | copy-start | bytes 6291460
  324.2 1.8 copy-start.24
  324.3 1.8 copy-start.30
  327.9 71.9 %copy-start.7 = (bf16[2048,128]{1,0:T(8,128)(2,1)S(1)}, bf16[2048,128]{1,0:T(8,128)(2,1)}, u32[]{:S(2)}) copy-start(bf16[2048,128]{1,0:T(8,128)(2,1)} %copy-done.6) | copy-start | bytes 1572868
  399.8 4.8 copy-start.26
  406.1 1.0 copy-start.13
  436.1 1.7 copy-start.2
  437.7 1.1 copy-start.8
  437.7 1.4 copy-start.14
  437.7 2.2 copy-start.1
  448.7 64.7 %copy-start.22 = (bf16[128,2048]{1,0:T(8,128)(2,1)S(1)}, bf16[128,2048]{1,0:T(8,128)(2,1)}, u32[]{:S(2)}) copy-start(bf16[128,2048]{1,0:T(8,128)(2,1)} %refs_4_.1) | copy-start | bytes 1572868
  513.3 1.8 copy-start.23
  515.0 2.8 copy-start.29
  515.1 3.7 copy-start.28
  515.1 4.5 copy-start.27
  517.8 2.6 copy-start.31
  519.6 3.5 copy-start.15
  521.6 2.4 copy-start.20
  523.1 3.1 copy-start.25
  (2 other events, 1.6 us)

commit v4 on v3

--- a/solution.py
+++ b/solution.py
@@ -27,7 +27,8 @@
 EVEN = ((6, (X, Y, Z)), (5, (Y, Z, X)), (5, (Z, X, Y)))
 ROOM = ((8, (X, Z, Y)), (8, (Y, Z, X)))
 LIGHT = ((7, (Z, X, Y)), (7, (Z, Y, X)), (2, (X, Y, Z)))
-MIXED = ((6, (X, Z, Y)), (6, (Y, Z, X)), (4, (Z, X, Y)))
+MIXED = ((6, (X, Z, Y)), (6, (Y, Z, X)), (2, (Z, X, Y)), (2, (Z, Y, X)))
+FIRST = ((6, (Z, X, Y)), (6, (Z, Y, X)), (4, (X, Y, Z)))
 
 
 class Place:
@@ -137,16 +138,20 @@
             new[-1].start()
         done = list(new)
         yield
-        for j, dim in enumerate(((X, 0), (Y, 0), (Z, 0), (0, 1))):
+        held = [(0, 0)]
+        for j, (bit, other) in enumerate(((X, 0), (Y, 0), (0, 1), (Z, 0))):
             for copy in new:
                 copy.wait_recv()
             new = []
-            for sub in range(1 << j):
-                block = box.at[place.index(sub)]
-                slot = (1 << j) - 1 + sub
-                new.append(push(block, block, send.at[slot], recv.at[slot], place.device(*dim)))
+            for k, (r, o) in enumerate(held):
+                block = box.at[place.index(r, o)]
+                slot = (1 << j) - 1 + k
+                new.append(push(block, block, send.at[slot], recv.at[slot], place.device(bit, other)))
                 new[-1].start()
+            held += [(r | bit, o | other) for r, o in held]
             done += new
+            yield
+        while not place.closing:
             yield
         for copy in new:
             copy.wait_recv()
@@ -163,44 +168,46 @@
         self.ins, self.in_specs = (sums,), (IN_VMEM,)
         self.outs, self.out_specs = (jax.ShapeDtypeStruct(tail, f32),), (IN_VMEM,)
         self.scratch = (
-            pltpu.VMEM((8, n) + tail, f32), pltpu.VMEM((15, n) + tail, f32), pltpu.VMEM((max(n - 1, 1),) + tail, f32),
-            DMA((14 + n,)), DMA((14 + n,)),
+            pltpu.VMEM((TREE_SEGS,) + tail, f32), pltpu.VMEM((15,) + tail, f32),
+            pltpu.VMEM((max(n - 1, 1), TREE_SEGS) + tail, f32), DMA((14 + n,)), DMA((14 + n,)),
         )
 
     def stages(self, place, src, out, acc, inbox, tbox, send, recv):
-        done = []
-
-        def go(block, slot, target):
-            done.append(push(block, inbox.at[slot], send.at[slot], recv.at[slot], target))
-            done[-1].start()
-
-        for r in range(8):
-            go(src.at[place.index(r, 1)], r, place.device(0, 1))
-        yield
-        for r in range(8):
-            done[r].wait_recv()
-            acc[r] = src[place.index(r)] + inbox[r]
-        at = 8
-        for bit in (Z, Y, X):
-            for r in range(bit):
-                go(acc.at[bit | r], at + r, place.device(bit))
-            yield
-            for r in range(bit):
-                done[at + r].wait_recv()
-                acc[r] = acc[r] + inbox[at + r]
-            at += bit
         far = []
         for k in range(1, place.trees):
             tree = lax.rem(place.tree + k, place.trees)
-            far.append(push(acc.at[0, tree], tbox.at[k - 1], send.at[14 + k], recv.at[14 + k], place.in_tree(k)))
+            far.append(push(src.at[:, tree], tbox.at[k - 1], send.at[14 + k], recv.at[14 + k], place.in_tree(k)))
             far[-1].start()
         yield
-        total = acc[0, place.tree]
-        for k in range(1, place.trees):
-            far[k - 1].wait_recv()
-            total = total + tbox[k - 1]
-        out[...] = total
-        for copy in done + far:
+        for copy in far:
+            copy.wait_recv()
+        for j in range(TREE_SEGS):
+            total = src[j, place.tree]
+            for k in range(1, place.trees):
+                total = total + tbox[k - 1, j]
+            acc[j] = total
+        left = [(r, o) for r in range(8) for o in range(2)]
+        done = []
+        for bit, other in ((0, 1), (X, 0), (Y, 0), (Z, 0)):
+            new = []
+            keep = [(r, o) for r, o in left if not (r & bit or o & other)]
+            for r, o in keep:
+                slot = len(done) + len(new)
+                block = acc.at[place.index(r | bit, o | other)]
+                new.append(push(block, inbox.at[slot], send.at[slot], recv.at[slot], place.device(bit, other)))
+                new[-1].start()
+            yield
+            if bit == Z:
+                while not place.closing:
+                    yield
+            for k, (r, o) in enumerate(keep):
+                new[k].wait_recv()
+                at = place.index(r, o)
+                acc[at] = acc[at] + inbox[len(done) + k]
+            done += new
+            left = keep
+        out[...] = acc[place.index(0)]
+        for copy in far + done:
             copy.wait_send()
 
 
@@ -891,16 +898,21 @@
             jax.ShapeDtypeStruct((tokens, HEAD_DIM), bf16),
             *[o for e in extras for o in e.outs],
         ],
-        compiler_params=pltpu.CompilerParams(collective_id=cid, has_side_effects=True, vmem_limit_bytes=40 * 2**20),
+        compiler_params=pltpu.CompilerParams(collective_id=cid, has_side_effects=True, vmem_limit_bytes=58 * 2**20),
         cost_estimate=pl.CostEstimate(flops=2 * tokens * width * n, bytes_accessed=60_000_000, transcendentals=0),
         name="attend",
     )(parent, x_full, gain, bias, w, b, *[a for e in extras for a in e.ins])
 
 
+def halves(v):
+    high = v.astype(bf16)
+    return high, (v - high.astype(f32)).astype(bf16)
+
+
 def attend_back_kernel(extras, trees, *refs):
-    own_in, own_out, own_scratch, extra_refs = sorted_refs(extras, refs, 5, 2)
-    parent_ref, qkv_ref, d_ref, w_ref, n_ref = own_in
-    o_ref, g_ref = own_out
+    own_in, own_out, own_scratch, extra_refs = sorted_refs(extras, refs, 6, 4)
+    parent_ref, qkv_ref, d_ref, w_ref, w_qkv_ref, n_ref = own_in
+    o_ref, g_ref, f_ref, s_ref = own_out
     dk, dv, d_ctx, held, sem = own_scratch
     place = Place(trees)
     step = pl.program_id(0)
@@ -942,15 +954,23 @@
         o_ref[:, pl.ds(hd, hd)] = (dk[...] * scale).astype(bf16)
         o_ref[:, pl.ds(2 * hd, hd)] = dv[...].astype(bf16)
         drain(held, sem)
+        total = jnp.sum(o_ref[...].astype(f32).reshape(-1, 8, o_ref.shape[1]), axis=0)
+        total = jnp.broadcast_to(jnp.sum(total, axis=0, keepdims=True), total.shape)
+        s_ref[...] = total
+        ones = jnp.ones(total.shape, bf16)
         block = 512
         for j in range(held.shape[1] // block):
             at = pl.ds(j * block, block)
-            g_ref[at, :] = dot(held[:, at], o_ref[...], 0, 0)
+            g = dot(held[:, at], o_ref[...], 0, 0)
+            g_ref[at, :] = g.astype(bf16)
+            w = w_qkv_ref[at, :]
+            f_ref[pl.ds(0, 8), at] = sum(dot(ones, part, 1, 1) for part in halves(w.astype(f32) * g))
+            f_ref[pl.ds(8, 8), at] = sum(dot(part, w, 1, 1) for part in halves(total))
         for e, r in zip(extras, extra_refs):
             e.finish(place, *r)
 
 
-def attend_back(parent, qkv, d_full, w_rows, norm_one, extras, cid):
+def attend_back(parent, qkv, d_full, w_rows, w_qkv, norm_one, extras, cid):
     tokens, width = d_full.shape
     n = qkv.shape[1]
     rows = 256
@@ -960,21 +980,22 @@
         grid=(tokens // rows,),
         in_specs=[
             pl.BlockSpec(memory_space=pltpu.SMEM), whole((tokens, n)), pl.BlockSpec((rows, width), lambda i: (i, 0)),
-            whole((HEAD_DIM, width)), ANYWHERE, *[i for e in extras for i in e.in_specs],
+            whole((HEAD_DIM, width)), whole((width, n)), ANYWHERE, *[i for e in extras for i in e.in_specs],
         ],
-        out_specs=[whole((tokens, n)), whole((width, n)), *[o for e in extras for o in e.out_specs]],
+        out_specs=[whole((tokens, n)), whole((width, n)), whole((16, width)), whole((8, n)), *[o for e in extras for o in e.out_specs]],
         scratch_shapes=[
             *[i for e in extras for i in e.scratch],
             pltpu.VMEM((tokens, HEAD_DIM), f32), pltpu.VMEM((tokens, HEAD_DIM), f32), pltpu.VMEM((tokens, HEAD_DIM), bf16),
             pltpu.VMEM((tokens, width), bf16), DMA,
         ],
         out_shape=[
-            jax.ShapeDtypeStruct((tokens, n), bf16), jax.ShapeDtypeStruct((width, n), f32), *[o for e in extras for o in e.outs],
+            jax.ShapeDtypeStruct((tokens, n), bf16), jax.ShapeDtypeStruct((width, n), bf16),
+            jax.ShapeDtypeStruct((16, width), f32), jax.ShapeDtypeStruct((8, n), f32), *[o for e in extras for o in e.outs],
         ],
-        compiler_params=pltpu.CompilerParams(collective_id=cid, has_side_effects=True, vmem_limit_bytes=40 * 2**20),
+        compiler_params=pltpu.CompilerParams(collective_id=cid, has_side_effects=True, vmem_limit_bytes=58 * 2**20),
         cost_estimate=pl.CostEstimate(flops=2 * tokens * width * HEAD_DIM, bytes_accessed=60_000_000, transcendentals=0),
         name="attend_back",
-    )(parent, qkv, d_full, w_rows, norm_one, *[a for e in extras for a in e.ins])
+    )(parent, qkv, d_full, w_rows, w_qkv, norm_one, *[a for e in extras for a in e.ins])
 
 
 def feed_forward_kernel(n_ref, c_ref, wu_ref, wd_ref, b_ref, active_ref, d_ref, sum_ref):
@@ -1008,6 +1029,39 @@
     )(n_full, c_full, wu, wd, b[None])
 
 
+def last_kernel(*refs):
+    dn_ref, x_ref, d_res_ref, gain_ref, res_ref, mlp_ref, b_ref, down_ref, *shares = refs[:13]
+    grad_ref, out_ref, down_out, *sums = refs[13:]
+    n, root = norm_stats(x_ref[...].astype(f32))
+    grad_ref[...] = d_res_ref[...] + norm_back(dn_ref[...], n, root, gain_ref[...])
+    out_ref[...] = (res_ref[...] + mlp_ref[...] + b_ref[...]).astype(bf16)
+    down_out[...] = down_ref[...].astype(f32)
+    for share, total in zip(shares, sums):
+        total[...] = jnp.sum(share[...].astype(f32), axis=0)
+
+
+def last(d_norm, x, d_res, gain, residual, mlp, b, g_down, shares):
+    tok, width = x.shape
+    steps = 4
+    by_row = pl.BlockSpec((tok // steps, width), lambda i: (i, 0))
+    vector = pl.BlockSpec((1, width), lambda i: (0, 0))
+    by_column = lambda v: pl.BlockSpec((v.shape[0], v.shape[1] // steps), lambda i: (0, i))
+    by_column_3 = lambda v: pl.BlockSpec(v.shape[:2] + (v.shape[2] // steps,), lambda i: (0, 0, i))
+    flat = [jax.ShapeDtypeStruct(v.shape[1:], f32) for v in shares]
+    return pl.pallas_call(
+        last_kernel,
+        grid=(steps,),
+        in_specs=[by_row, by_row, by_row, vector, by_row, by_row, vector, by_column(g_down), *map(by_column_3, shares)],
+        out_specs=[by_row, by_row, by_column(g_down), *map(by_column, flat)],
+        out_shape=[
+            jax.ShapeDtypeStruct((tok, width), f32), jax.ShapeDtypeStruct((tok, width), bf16),
+            jax.ShapeDtypeStruct(g_down.shape, f32), *flat,
+        ],
+        compiler_params=pltpu.CompilerParams(vmem_limit_bytes=58 * 2**20),
+        name="last",
+    )(d_norm, x, d_res, gain[None], residual, mlp, b[None], g_down, *shares)
+
+
 def body(
     inputs, gain_one, bias_one, w_query, b_query, w_key, w_value, b_value, w_out, b_out,
     gain_two, bias_two, w_up, b_up, w_down, b_down, parents, cotangent,
@@ -1031,7 +1085,7 @@
         at += v.shape[0]
     block = block.reshape(16, 128)
 
-    x_full, box, w_att = tree_gather(inputs, 0, "gather_inputs", LIGHT, extras=(
+    x_full, box, w_att = tree_gather(inputs, 0, "gather_inputs", FIRST, extras=(
         SpreadSmall(block), DealAll(w_query, w_key, w_value),
     ))
     w_att = w_att.reshape(width, -1)
@@ -1074,15 +1128,13 @@
     ))
     g_down = own_rows(g_down, swap_down, rows)
     g_orow = dot(context, da_full, 0, 0).astype(bf16)
-    d_qkv, g_qkv, g_down, g_o = attend_back(
-        parent, qkv, da_full, w_orow, norm_one, (DealRows(g_down, (fs,)), HeadRowsBack(g_orow, rows)), 10
+    d_qkv, g_att, shares, s_qkv, g_down, g_o = attend_back(
+        parent, qkv, da_full, w_orow, w_att, norm_one, (DealRows(g_down, (fs,)), HeadRowsBack(g_orow, rows)), 10
     )
 
-    s_qkv = jnp.sum(d_qkv.astype(f32), axis=0)
-    w_f = w_att.astype(f32)
-    gb_one = jnp.sum(w_f * s_qkv, axis=1)
-    gg_one = (jnp.sum(w_f * g_qkv, axis=1) - bias_one * gb_one) / gain_one
-    g_att = g_qkv.astype(bf16)
+    gb_one = shares[8]
+    gg_one = (shares[0] - bias_one * gb_one) / gain_one
+    s_qkv = s_qkv[0]
 
     def placed(vec, total):
         return lax.dynamic_update_slice_in_dim(jnp.zeros((total,), f32), vec, me * vec.shape[0], axis=0)
@@ -1095,19 +1147,16 @@
     sums = jnp.stack(sums).reshape(8, devices, rows).transpose(1, 0, 2).reshape(devices, 8 * rows)
     sums = jnp.concatenate([sums, placed(col(gb_up), ff).reshape(devices, -1)], axis=1)
     sums = jnp.pad(sums, ((0, 0), (0, 1024 - n_small))).reshape(trees, TREE_SEGS, 8, 128).transpose(1, 0, 2, 3)
-    d_norm_one, g_q, g_k, g_v, sums = product_scatter(d_qkv, w_att, 1, 7, "scatter_d_norm_one", LIGHT, extras=(
-        DealAllRows(g_att.reshape(devices, rows, -1), (HEAD_DIM,) * 3), ReduceSmall(sums),
+    d_norm_one, sums, g_q, g_k, g_v = product_scatter(d_qkv, w_att, 1, 7, "scatter_d_norm_one", MIXED, extras=(
+        ReduceSmall(sums), DealAllRows(g_att.reshape(devices, rows, -1), (HEAD_DIM,) * 3),
     ))
     sums = sums.reshape(-1)
     parts = [sums[j * rows : (j + 1) * rows] for j in range(8)]
     gb_up = sums[8 * rows : n_small]
 
-    n_one, root_one = norm_stats(x_own)
-    grad_inputs = d_res + norm_back(d_norm_one, n_one, root_one, gain_one)
-
-    layer_output = (residual + mlp + b_down).astype(bf16)
-    g_q, g_k, g_v, g_o, g_up = (jnp.sum(g.astype(f32), axis=0) for g in (g_q, g_k, g_v, g_o, g_up))
-    g_down = g_down.astype(f32)
+    grad_inputs, layer_output, g_down, g_q, g_k, g_v, g_o, g_up = last(
+        d_norm_one, inputs, d_res, gain_one, residual, mlp, b_down, g_down, (g_q, g_k, g_v, g_o, g_up)
+    )
     return (
         layer_output, grad_inputs, parts[0], parts[1], g_q, parts[2], g_k, g_v, parts[3], g_o, parts[4],
         parts[5], parts[6], g_up, gb_up, g_down, parts[7],

time: 538 us -> 521 us (0.968)
  other arithmetic: 29.6 us -> 12 us
  Pallas kernels: 467 us -> 476 us
  local copies, waits for them, and re-layouts: 19.8 us -> 11.1 us
    unnamed x71 -> x35, local copies, waits for them, and re-layouts: 14.1 us -> 1.74 us
    reduce_sum x9 -> x0, other arithmetic: 12 us -> none  [the longest x5 5.17 us: body(): jnp.sum(g.astype(f32), axis=0)]
    pallas_call x0 -> x1, Pallas kernels: none -> 7.56 us  [last(): pl.pallas_call(last_kernel, grid=(steps,), in_specs=[by_row, by_row, by_r...]
where the time goes in v4:
time: 521 us; the launch traced here: 512 us
  Pallas kernels  476 us (91%)
  other arithmetic  12 us (2%)
  matrix products  11.4 us (2%)
  local copies, waits for them, and re-layouts  11.1 us (2%)
    pallas_call x6, Pallas kernels, call(): pl.pallas_call(functools.partial(kernel, extras, lax.axis_size('tree')),...  384 us
    pallas_call x1, Pallas kernels, attend(): pl.pallas_call(functools.partial(attend_kernel, extras, lax.axis_size('tr...  37.6 us
    pallas_call x1, Pallas kernels, attend_back(): pl.pallas_call(functools.partial(attend_back_kernel, extras, lax.axis_siz...  33.3 us
    pallas_call x1, Pallas kernels, feed_forward(): pl.pallas_call(feed_forward_kernel, grid=(tokens // rows,), in_specs=[by_...  13.5 us
    dot_general x2, matrix products, dot(): lax.dot_general(a, b, (((ca,), (cb,)), ((), ())), preferred_element_type=...  11.4 us

profile of v4, /device:TPU:0, one launch (start us, length us, event | category | flops | bytes accessed | tf_op | source)
XLA Modules:
  0.0 512.0 jit_solution(3804189389953108964)
XLA Ops:
  0.7 1.5 add_bitcast_fusion.refs_0_
  2.1 61.4 %gather_inputs.1 = (bf16[16,2,16,128]{3,2,1,0:T(8,128)(2,1)}, bf16[32,64,384]{2,1,0:T(8,128)(2,1)}, bf16[2048,2048]{1,0:T(8,128)(2,1)}) custom-call(bf16[16,128]{1,0:T(8,128)(2,1)} %add_bitcast_fusion.refs_0_, bf16[64,2048]{1,0:T(8,128)(2,1)} %refs_1_.2, bf16[64,2048]{1,0:T(8,128)(2,1)} %refs_2_.1, bf16[64,2048]{1,0:T(8,128)(2,1)} %refs_3_.2, ...), custom_call_target="tpu_custom_call" | custom-call | bytes 120000000 | tf_op jit(solution)/shard_map/gather_inputs/pallas_call | solution.py:511
  63.5 0.9 copy.35
  65.7 0.6 compare_select_fusion.refs_0_
  66.3 0.7 unstack.39.refs_2_.refs_3_
  67.0 0.7 unstack.41.refs_3_
  67.6 37.6 %attend.1 = (bf16[2048,2048]{1,0:T(8,128)(2,1)}, bf16[2048,384]{1,0:T(8,128)(2,1)}, bf16[2048,128]{1,0:T(8,128)(2,1)}, bf16[128,2048]{1,0:T(8,128)(2,1)}, bf16[1...) custom-call(s32[16]{0:T(128)} %compare_select_fusion.refs_0_, bf16[2048,2048]{1,0:T(8,128)(2,1)} %get-tuple-element.59.refs_1_, ...), custom_call_target="tpu_custom_call" | custom-call | flops 3221225472 | bytes 60000000 | tf_op jit(solution)/shard_map/attend/pallas_call | solution.py:886
  105.3 72.0 %scatter_attended.1 = (f32[128,2048]{1,0:T(8,128)}, bf16[2,1024,512]{2,1,0:T(8,128)(2,1)}, bf16[2048,2048]{1,0:T(8,128)(2,1)}) custom-call(bf16[2048,128]{1,0:T(8,128)(2,1)} %get-tuple-element.64.refs_0_, bf16[128,2048]{1,0:T(8,128)(2,1)} %get-tuple-element.65.refs_1_.refs_3_, bf16[1024,512]{1,0:T(8,128)(2,1)} %bitcast.71, bf16[128,2048]{1,0:T(8,128)(2,1)} %refs_3_.3), custom_call_target="tpu_custom_call" | custom-call | flops 1073741824 | bytes 120000000 | tf_op jit(solution)/shard_map/scatter_attended/pallas_call | solution.py:511
  177.3 1.4 fusion.5
  179.2 1.0 add_convert_fusion.refs_1_
  180.3 51.3 %gather_norm_two.1 = (bf16[2,1024,512]{2,1,0:T(8,128)(2,1)}, bf16[2048,2048]{1,0:T(8,128)(2,1)}) custom-call(bf16[1024,512]{1,0:T(8,128)(2,1)} %bitcast.58, bf16[128,2048]{1,0:T(8,128)(2,1)} %add_convert_fusion.refs_1_), custom_call_target="tpu_custom_call" | custom-call | bytes 120000000 | tf_op jit(solution)/shard_map/gather_norm_two/pallas_call | solution.py:511
  231.7 1.6 copy-done.1
  233.3 13.5 %feed_forward.1 = (bf16[2048,512]{1,0:T(8,128)(2,1)S(1)}, bf16[2048,512]{1,0:T(8,128)(2,1)S(1)}, f32[8,512]{1,0:T(8,128)S(1)}) custom-call(bf16[2048,2048]{1,0:T(8,128)(2,1)} %get-tuple-element.68.n_ref, bf16[2048,2048]{1,0:T(8,128)(2,1)} %get-tuple-element.69.c_ref.refs_3_, bf16[2048,512]{1,0:T(8,128)(2,1)S(1)} %bitcast.49, bf16[2048,512]{1,0:T(8,128)(2,1)S(1)} %bitcast.52, ...), custom_call_target="tpu_custom_call" | custom-call | flops 8589934592 | bytes 16777216 | tf_op jit(solution)/shard_map/feed_forward/pallas_call | solution.py:1020
  246.9 5.8 %convolution_convert_fusion = bf16[2048,512]{1,0:T(8,128)(2,1)} fusion(bf16[2048,2048]{1,0:T(8,128)(2,1)S(1)} %copy-done.15, bf16[2048,512]{1,0:T(8,128)(2,1)S(1)} %get-tuple-element.73.refs_0_), kind=kOutput, calls=%fused_computation | convolution fusion | flops 4296015872 | bytes 12582912 | tf_op jit(solution)/shard_map/dot_general | solution.py:21
  252.7 63.5 %scatter_d_norm_two.1 = (f32[128,2048]{1,0:T(8,128)}, bf16[2,64,8192]{2,1,0:T(8,128)(2,1)}, bf16[2048,512]{1,0:T(8,128)(2,1)}) custom-call(bf16[2048,512]{1,0:T(8,128)(2,1)} %copy-done.2, bf16[2048,512]{1,0:T(8,128)(2,1)} %bitcast.48, bf16[32,64,512]{2,1,0:T(8,128)(2,1)} %bitcast.57, bf16[2048,2048]{1,0:T(8,128)(2,1)} %get-tuple-element.69.c_ref.refs_3_, ...), custom_call_target="tpu_custom_call" | custom-call | flops 4294967296 | bytes 120000000 | tf_op jit(solution)/shard_map/scatter_d_norm_two/pallas_call | solution.py:511
  316.2 1.8 multiply_reduce_fusion
  318.0 1.8 convert_reduce_fusion.1
  319.8 74.2 %scatter_mlp.1 = (f32[128,2048]{1,0:T(8,128)}, bf16[1,1024,512]{2,1,0:T(8,128)(2,1)}, bf16[2048,2048]{1,0:T(8,128)(2,1)}) custom-call(bf16[2048,512]{1,0:T(8,128)(2,1)} %copy-done, bf16[2048,512]{1,0:T(8,128)(2,1)} %bitcast.51, bf16[2048,512]{1,0:T(8,128)(2,1)} %get-tuple-element.74.refs_2_, bf16[128,2048]{1,0:T(8,128)(2,1)} %get-tuple-element.116.refs_3_), custom_call_target="tpu_custom_call" | custom-call | flops 4294967296 | bytes 120000000 | tf_op jit(solution)/shard_map/scatter_mlp/pallas_call | solution.py:511
  394.1 5.6 %convolution_convert_fusion.1.refs_7_ = bf16[128,2048]{1,0:T(8,128)(2,1)} fusion(bf16[2048,128]{1,0:T(8,128)(2,1)S(1)} %copy-done.7, bf16[2048,2048]{1,0:T(8,128)(2,1)} %get-tuple-element.76.refs_2_), kind=kOutput, calls=%fused_computation.1 | convolution fusion | flops 1074003968 | bytes 9437184 | tf_op jit(solution)/shard_map/dot_general | solution.py:21
  399.7 1.3 fusion
  400.9 33.3 %attend_back.1 = (bf16[2048,384]{1,0:T(8,128)(2,1)}, bf16[2048,384]{1,0:T(8,128)(2,1)}, f32[16,2048]{1,0:T(8,128)}, f32[8,384]{1,0:T(8,128)}, bf16[64,8192]{1,0:T(8,128)(2,1)}, /*index=5*/bf16[2,64,2048]{2,1,0:T(8,128)(2,1)}) custom-call(s32[16]{0:T(128)} %compare_select_fusion.refs_0_, bf16[2048,384]{1,0:T(8,128)(2,1)} %get-tuple-element.62.refs_1_, ...), custom_call_target="tpu_custom_call" | custom-call | flops 1073741824 | bytes 60000000 | tf_op jit(solution)/shard_map/attend_back/pallas_call | solution.py:978
  434.2 0.9 slice_reduce_fusion.8
  435.3 0.7 constant_dynamic-update-slice_fusion.1
  436.5 0.7 reduce.46
  437.3 0.7 constant_dynamic-update-slice_fusion
  438.0 0.7 reduce.47
  439.7 0.7 copy_bitcast_fusion.1.refs_2_
  440.4 61.7 %scatter_d_norm_one.1 = (f32[128,2048]{1,0:T(8,128)}, f32[8,128]{1,0:T(8,128)}, bf16[2,64,2048]{2,1,0:T(8,128)(2,1)}, bf16[2,64,2048]{2,1,0:T(8,128)(2,1)}, bf16[2,64,2048]{2,1,0:T(8,128)(2,1)}) custom-call(bf16[2048,384]{1,0:T(8,128)(2,1)} %get-tuple-element.79.refs_0_, bf16[2048,384]{1,0:T(8,128)(2,1)} %bitcast.55, ...), custom_call_target="tpu_custom_call" | custom-call | flops 3221225472 | bytes 120000000 | tf_op jit(solution)/shard_map/scatter_d_norm_one/pallas_call | solution.py:511
  502.1 0.7 unstack.50.refs_6_
  502.8 7.6 %last.1 = (f32[128,2048]{1,0:T(8,128)}, bf16[128,2048]{1,0:T(8,128)(2,1)}, f32[64,8192]{1,0:T(8,128)}, f32[64,2048]{1,0:T(8,128)}, f32[64,2048]{1,0:T(8,128)}, /...) custom-call(f32[128,2048]{1,0:T(8,128)} %get-tuple-element.84.refs_0_, bf16[128,2048]{1,0:T(8,128)(2,1)} %refs_1_.3, ...), custom_call_target="tpu_custom_call" | custom-call | tf_op jit(solution)/shard_map/last/pallas_call | solution.py:1051
  510.3 0.6 fusion.6
  511.0 0.6 slice_bitcast_fusion
  (71 shorter events, 3.7 us)
Async XLA Ops:
  0.7 65.0 %copy-start.14 = (s32[32]{0:T(128)S(1)}, s32[32]{0:T(128)}, u32[]{:S(2)}) copy-start(s32[32]{0:T(128)} %param.34) | copy-start | bytes 388
  105.3 72.1 %copy-start.5 = (bf16[128,2048]{1,0:T(8,128)(2,1)S(1)}, bf16[128,2048]{1,0:T(8,128)(2,1)}, u32[]{:S(2)}) copy-start(bf16[128,2048]{1,0:T(8,128)(2,1)} %refs_1_.3) | copy-start | bytes 1572868
  178.8 139.2 %copy-start.4 = (f32[128,2048]{1,0:T(8,128)}, f32[128,2048]{1,0:T(8,128)S(1)}, u32[]{:S(2)}) copy-start(f32[128,2048]{1,0:T(8,128)S(1)} %get-tuple-element.119.refs_4_) | copy-start | bytes 3145732
  178.8 52.9 %copy-start.3 = (bf16[2,1024,512]{2,1,0:T(8,128)(2,1)S(1)}, bf16[2,1024,512]{2,1,0:T(8,128)(2,1)}, u32[]{:S(2)}) copy-start(bf16[2,1024,512]{2,1,0:T(8,128)(2,1)} %get-tuple-element.71) | copy-start | bytes 6291460
  231.7 1.6 copy-start.1
  233.3 13.6 %copy-start.15 = (bf16[2048,2048]{1,0:T(8,128)(2,1)S(1)}, bf16[2048,2048]{1,0:T(8,128)(2,1)}, u32[]{:S(2)}) copy-start(bf16[2048,2048]{1,0:T(8,128)(2,1)} %get-tuple-element.68.n_ref) | copy-start | bytes 25165828
  246.8 5.8 %copy-start = (bf16[2048,512]{1,0:T(8,128)(2,1)}, bf16[2048,512]{1,0:T(8,128)(2,1)S(1)}, u32[]{:S(2)}) copy-start(bf16[2048,512]{1,0:T(8,128)(2,1)S(1)} %get-tuple-element.72.refs_4_.refs_0_) | copy-start | bytes 6291460
  246.8 5.8 %copy-start.2 = (bf16[2048,512]{1,0:T(8,128)(2,1)}, bf16[2048,512]{1,0:T(8,128)(2,1)S(1)}, u32[]{:S(2)}) copy-start(bf16[2048,512]{1,0:T(8,128)(2,1)S(1)} %get-tuple-element.73.refs_0_) | copy-start | bytes 6291460
  316.2 1.8 copy-start.6
  316.2 1.8 copy-start.10
  319.8 74.2 %copy-start.7 = (bf16[2048,128]{1,0:T(8,128)(2,1)S(1)}, bf16[2048,128]{1,0:T(8,128)(2,1)}, u32[]{:S(2)}) copy-start(bf16[2048,128]{1,0:T(8,128)(2,1)} %get-tuple-element.64.refs_0_) | copy-start | bytes 1572868
  394.0 5.6 %copy-start.8 = (bf16[1,1024,512]{2,1,0:T(8,128)(2,1)S(1)}, bf16[1,1024,512]{2,1,0:T(8,128)(2,1)}, u32[]{:S(2)}) copy-start(bf16[1,1024,512]{2,1,0:T(8,128)(2,1)} %get-tuple-element.78) | copy-start | bytes 3145732
  394.1 5.6 %copy-start.9 = (bf16[2048,512]{1,0:T(8,128)(2,1)S(1)}, bf16[2048,512]{1,0:T(8,128)(2,1)}, u32[]{:S(2)}) copy-start(bf16[2048,512]{1,0:T(8,128)(2,1)} %get-tuple-element.74.refs_2_) | copy-start | bytes 6291460
  400.9 33.3 %copy-start.11 = (f32[1,2048]{1,0:T(1,128)S(1)}, f32[1,2048]{1,0:T(1,128)}, u32[]{:S(2)}) copy-start(f32[1,2048]{1,0:T(1,128)} %unstack.39.refs_2_.refs_3_) | copy-start | bytes 24580
  400.9 33.3 %copy-start.12 = (f32[1,2048]{1,0:T(1,128)S(1)}, f32[1,2048]{1,0:T(1,128)}, u32[]{:S(2)}) copy-start(f32[1,2048]{1,0:T(1,128)} %unstack.41.refs_3_) | copy-start | bytes 24580
  502.8 7.6 %copy-start.13 = (f32[8,128]{1,0:T(8,128)S(1)}, f32[8,128]{1,0:T(8,128)}, u32[]{:S(2)}) copy-start(f32[8,128]{1,0:T(8,128)} %get-tuple-element.94) | copy-start | bytes 12292

commit v5 on v4

--- a/solution.py
+++ b/solution.py
@@ -434,11 +434,10 @@
 
 
 class HeadRowsBack(Extra):
-    def __init__(self, grad, rows):
+    def __init__(self, width, rows):
         self.rows = rows
         n = lax.axis_size("tree")
-        self.ins, self.in_specs = (grad,), (ANYWHERE,)
-        self.outs, self.out_specs = (jax.ShapeDtypeStruct((n, rows, grad.shape[1]), grad.dtype),), (ANYWHERE,)
+        self.outs, self.out_specs = (jax.ShapeDtypeStruct((n, rows, width), bf16),), (ANYWHERE,)
         self.scratch = (DMA((HEAD_DIM // rows,)), DMA)
 
     def greet(self, place):
@@ -845,8 +844,8 @@
 
 
 def attend_kernel(extras, trees, *refs):
-    own_in, own_out, (held,), extra_refs = sorted_refs(extras, refs, 6, 3)
-    parent_ref, x_ref, gain_ref, bias_ref, w_ref, b_ref = own_in
+    own_in, own_out, (held,), extra_refs = sorted_refs(extras, refs, 4, 3)
+    parent_ref, x_ref, vecs_ref, w_ref = own_in
     n_ref, qkv_ref, ctx_ref = own_out
     place = Place(trees)
 
@@ -860,9 +859,12 @@
     rows = x_ref.shape[0]
     tok = held.shape[0] // TREE_SEGS
     n, _ = norm_stats(x_ref[...].astype(f32))
-    norm = (n * gain_ref[...] + bias_ref[...]).astype(bf16)
+    norm = (n * vecs_ref[pl.ds(0, 1), :] + vecs_ref[pl.ds(1, 1), :]).astype(bf16)
     n_ref[...] = norm
-    qkv = (dot(norm, w_ref[...], 1, 0) + b_ref[...]).astype(bf16)
+    head = pl.ds(pl.multiple_of(place.at * HEAD_DIM, HEAD_DIM), HEAD_DIM)
+    b_query, b_value = vecs_ref[pl.ds(2, 1), head], vecs_ref[pl.ds(3, 1), head]
+    b = jnp.concatenate([b_query, jnp.zeros_like(b_query), b_value], axis=1)
+    qkv = (dot(norm, w_ref[...], 1, 0) + b).astype(bf16)
     qkv_ref[...] = qkv
     held[pl.ds(pl.multiple_of(step * rows, rows), rows), :] = qkv
 
@@ -877,7 +879,7 @@
             e.finish(place, *r)
 
 
-def attend(parent, x_full, gain, bias, w, b, extras, cid):
+def attend(parent, x_full, vecs, w, extras, cid):
     tokens, width = x_full.shape
     n = 3 * HEAD_DIM
     rows = 256
@@ -887,8 +889,7 @@
         functools.partial(attend_kernel, extras, lax.axis_size("tree")),
         grid=(tokens // rows,),
         in_specs=[
-            pl.BlockSpec(memory_space=pltpu.SMEM), by_row(width), whole((1, width)), whole((1, width)), whole((width, n)),
-            whole((1, n)), *[i for e in extras for i in e.in_specs],
+            pl.BlockSpec(memory_space=pltpu.SMEM), by_row(width), whole(vecs.shape), whole((width, n)), *[i for e in extras for i in e.in_specs],
         ],
         out_specs=[by_row(width), by_row(n), whole((tokens, HEAD_DIM)), *[o for e in extras for o in e.out_specs]],
         scratch_shapes=[*[i for e in extras for i in e.scratch], pltpu.VMEM((tokens, n), bf16)],
@@ -901,7 +902,7 @@
         compiler_params=pltpu.CompilerParams(collective_id=cid, has_side_effects=True, vmem_limit_bytes=58 * 2**20),
         cost_estimate=pl.CostEstimate(flops=2 * tokens * width * n, bytes_accessed=60_000_000, transcendentals=0),
         name="attend",
-    )(parent, x_full, gain, bias, w, b, *[a for e in extras for a in e.ins])
+    )(parent, x_full, vecs, w, *[a for e in extras for a in e.ins])
 
 
 def halves(v):
@@ -910,18 +911,20 @@
 
 
 def attend_back_kernel(extras, trees, *refs):
-    own_in, own_out, own_scratch, extra_refs = sorted_refs(extras, refs, 6, 4)
-    parent_ref, qkv_ref, d_ref, w_ref, w_qkv_ref, n_ref = own_in
-    o_ref, g_ref, f_ref, s_ref = own_out
-    dk, dv, d_ctx, held, sem = own_scratch
+    own_in, own_out, own_scratch, extra_refs = sorted_refs(extras, refs, 7, 3)
+    parent_ref, qkv_ref, d_ref, w_ref, w_qkv_ref, ctx_ref, n_ref = own_in
+    o_ref, g_ref, f_ref = own_out
+    dk, dv, d_ctx, held, sem, g_rows, g_rows_low = own_scratch
+    *soon, later = list(zip(extras, extra_refs))
     place = Place(trees)
     step = pl.program_id(0)
 
     @pl.when(step == 0)
     def _():
         greet(place, extras)
-        for e, r in zip(extras, extra_refs):
+        for e, r in soon:
             e.start(place, *r)
+        g_rows[...] = jnp.zeros_like(g_rows)
         pltpu.make_async_copy(n_ref, held, sem).start()
 
     rows = d_ref.shape[0]
@@ -929,9 +932,15 @@
     hd = HEAD_DIM
     scale = HEAD_DIM ** -0.5
     d_ctx[pl.ds(pl.multiple_of(step * rows, rows), rows), :] = dot(d_ref[...], w_ref[...], 1, 1).astype(bf16)
+    tile = 512
+    for j in range(d_ref.shape[1] // tile):
+        at = pl.ds(j * tile, tile)
+        g_rows[:, at] += dot(ctx_ref[...], d_ref[:, at], 0, 0)
 
     @pl.when(step == pl.num_programs(0) - 1)
     def _():
+        g_rows_low[...] = g_rows[...].astype(bf16)
+        later[0].start(place, g_rows_low, *later[1])
         dk[...] = jnp.zeros_like(dk)
         dv[...] = jnp.zeros_like(dv)
 
@@ -956,7 +965,10 @@
         drain(held, sem)
         total = jnp.sum(o_ref[...].astype(f32).reshape(-1, 8, o_ref.shape[1]), axis=0)
         total = jnp.broadcast_to(jnp.sum(total, axis=0, keepdims=True), total.shape)
-        s_ref[...] = total
+        f_ref[pl.ds(16, 16), :] = jnp.zeros((16, f_ref.shape[1]), f32)
+        head = pl.ds(pl.multiple_of(place.at * hd, hd), hd)
+        f_ref[pl.ds(16, 8), head] = total[:, :hd]
+        f_ref[pl.ds(24, 8), head] = total[:, 2 * hd :]
         ones = jnp.ones(total.shape, bf16)
         block = 512
         for j in range(held.shape[1] // block):
@@ -966,11 +978,12 @@
             w = w_qkv_ref[at, :]
             f_ref[pl.ds(0, 8), at] = sum(dot(ones, part, 1, 1) for part in halves(w.astype(f32) * g))
             f_ref[pl.ds(8, 8), at] = sum(dot(part, w, 1, 1) for part in halves(total))
-        for e, r in zip(extras, extra_refs):
+        for e, r in soon:
             e.finish(place, *r)
-
-
-def attend_back(parent, qkv, d_full, w_rows, w_qkv, norm_one, extras, cid):
+        later[0].finish(place, g_rows_low, *later[1])
+
+
+def attend_back(parent, qkv, d_full, w_rows, w_qkv, context, norm_one, extras, cid):
     tokens, width = d_full.shape
     n = qkv.shape[1]
     rows = 256
@@ -980,26 +993,31 @@
         grid=(tokens // rows,),
         in_specs=[
             pl.BlockSpec(memory_space=pltpu.SMEM), whole((tokens, n)), pl.BlockSpec((rows, width), lambda i: (i, 0)),
-            whole((HEAD_DIM, width)), whole((width, n)), ANYWHERE, *[i for e in extras for i in e.in_specs],
+            whole((HEAD_DIM, width)), whole((width, n)),
+            pl.BlockSpec((rows, HEAD_DIM), lambda i: (i, 0)), ANYWHERE, *[i for e in extras for i in e.in_specs],
         ],
-        out_specs=[whole((tokens, n)), whole((width, n)), whole((16, width)), whole((8, n)), *[o for e in extras for o in e.out_specs]],
+        out_specs=[whole((tokens, n)), whole((width, n)), whole((32, width)), *[o for e in extras for o in e.out_specs]],
         scratch_shapes=[
             *[i for e in extras for i in e.scratch],
             pltpu.VMEM((tokens, HEAD_DIM), f32), pltpu.VMEM((tokens, HEAD_DIM), f32), pltpu.VMEM((tokens, HEAD_DIM), bf16),
             pltpu.VMEM((tokens, width), bf16), DMA,
+            pltpu.VMEM((HEAD_DIM, width), f32), pltpu.VMEM((HEAD_DIM, width), bf16),
         ],
         out_shape=[
             jax.ShapeDtypeStruct((tokens, n), bf16), jax.ShapeDtypeStruct((width, n), bf16),
-            jax.ShapeDtypeStruct((16, width), f32), jax.ShapeDtypeStruct((8, n), f32), *[o for e in extras for o in e.outs],
+            jax.ShapeDtypeStruct((32, width), f32), *[o for e in extras for o in e.outs],
         ],
         compiler_params=pltpu.CompilerParams(collective_id=cid, has_side_effects=True, vmem_limit_bytes=58 * 2**20),
         cost_estimate=pl.CostEstimate(flops=2 * tokens * width * HEAD_DIM, bytes_accessed=60_000_000, transcendentals=0),
         name="attend_back",
-    )(parent, qkv, d_full, w_rows, w_qkv, norm_one, *[a for e in extras for a in e.ins])
+    )(parent, qkv, d_full, w_rows, w_qkv, context, norm_one, *[a for e in extras for a in e.ins])
 
 
 def feed_forward_kernel(n_ref, c_ref, wu_ref, wd_ref, b_ref, active_ref, d_ref, sum_ref):
-    act, der = gelu_pair(dot(n_ref[...], wu_ref[...], 1, 0) + b_ref[...])
+    fs = wu_ref.shape[1]
+    at = lax.axis_index("blk") * 2 + lax.axis_index("rep")
+    b = b_ref[:, pl.ds(pl.multiple_of(at * fs, fs), fs)]
+    act, der = gelu_pair(dot(n_ref[...], wu_ref[...], 1, 0) + b)
     active_ref[...] = act.astype(bf16)
     d = (dot(c_ref[...], wd_ref[...], 1, 0) * der).astype(bf16)
     d_ref[...] = d
@@ -1014,13 +1032,13 @@
 def feed_forward(n_full, c_full, wu, wd, b):
     tokens, width = n_full.shape
     n = wu.shape[1]
-    rows = 256
+    rows = 512
     whole = lambda shape: pl.BlockSpec(shape, lambda i: (0,) * len(shape))
     by_row = lambda cols: pl.BlockSpec((rows, cols), lambda i: (i, 0))
     return pl.pallas_call(
         feed_forward_kernel,
         grid=(tokens // rows,),
-        in_specs=[by_row(width), by_row(width), whole((width, n)), whole((width, n)), whole((1, n))],
+        in_specs=[by_row(width), by_row(width), whole((width, n)), whole((width, n)), whole((1, b.shape[0]))],
         out_specs=[by_row(n), by_row(n), whole((8, n))],
         out_shape=[jax.ShapeDtypeStruct((tokens, n), bf16)] * 2 + [jax.ShapeDtypeStruct((8, n), f32)],
         compiler_params=pltpu.CompilerParams(vmem_limit_bytes=40 * 2**20),
@@ -1030,28 +1048,28 @@
 
 
 def last_kernel(*refs):
-    dn_ref, x_ref, d_res_ref, gain_ref, res_ref, mlp_ref, b_ref, down_ref, *shares = refs[:13]
-    grad_ref, out_ref, down_out, *sums = refs[13:]
+    dn_ref, x_ref, d_res_ref, vecs_ref, res_ref, mlp_ref, down_ref, *shares = refs[:12]
+    grad_ref, out_ref, down_out, *sums = refs[12:]
     n, root = norm_stats(x_ref[...].astype(f32))
-    grad_ref[...] = d_res_ref[...] + norm_back(dn_ref[...], n, root, gain_ref[...])
-    out_ref[...] = (res_ref[...] + mlp_ref[...] + b_ref[...]).astype(bf16)
+    grad_ref[...] = d_res_ref[...] + norm_back(dn_ref[...], n, root, vecs_ref[pl.ds(0, 1), :])
+    out_ref[...] = (res_ref[...] + mlp_ref[...] + vecs_ref[pl.ds(7, 1), :]).astype(bf16)
     down_out[...] = down_ref[...].astype(f32)
     for share, total in zip(shares, sums):
         total[...] = jnp.sum(share[...].astype(f32), axis=0)
 
 
-def last(d_norm, x, d_res, gain, residual, mlp, b, g_down, shares):
+def last(d_norm, x, d_res, vecs, residual, mlp, g_down, shares):
     tok, width = x.shape
     steps = 4
     by_row = pl.BlockSpec((tok // steps, width), lambda i: (i, 0))
-    vector = pl.BlockSpec((1, width), lambda i: (0, 0))
+    vectors = pl.BlockSpec(vecs.shape, lambda i: (0, 0))
     by_column = lambda v: pl.BlockSpec((v.shape[0], v.shape[1] // steps), lambda i: (0, i))
     by_column_3 = lambda v: pl.BlockSpec(v.shape[:2] + (v.shape[2] // steps,), lambda i: (0, 0, i))
     flat = [jax.ShapeDtypeStruct(v.shape[1:], f32) for v in shares]
     return pl.pallas_call(
         last_kernel,
         grid=(steps,),
-        in_specs=[by_row, by_row, by_row, vector, by_row, by_row, vector, by_column(g_down), *map(by_column_3, shares)],
+        in_specs=[by_row, by_row, by_row, vectors, by_row, by_row, by_column(g_down), *map(by_column_3, shares)],
         out_specs=[by_row, by_row, by_column(g_down), *map(by_column, flat)],
         out_shape=[
             jax.ShapeDtypeStruct((tok, width), f32), jax.ShapeDtypeStruct((tok, width), bf16),
@@ -1059,7 +1077,7 @@
         ],
         compiler_params=pltpu.CompilerParams(vmem_limit_bytes=58 * 2**20),
         name="last",
-    )(d_norm, x, d_res, gain[None], residual, mlp, b[None], g_down, *shares)
+    )(d_norm, x, d_res, vecs, residual, mlp, g_down, *shares)
 
 
 def body(
@@ -1074,7 +1092,6 @@
     devices = trees * TREE_SEGS
     tree = lax.axis_index("tree")
     me = lax.axis_index(GROUP)
-    head = lambda v: lax.dynamic_slice_in_dim(v, me * HEAD_DIM, HEAD_DIM)
 
     vectors = (gain_one, bias_one, b_query, b_value, b_out, gain_two, bias_two, b_down, b_up)
     n_small = sum(v.shape[0] for v in vectors)
@@ -1091,16 +1108,15 @@
     w_att = w_att.reshape(width, -1)
     packed = box.transpose(1, 0, 2, 3).reshape(devices, -1)[:, :n_small]
     vecs = packed[:, : 8 * rows].reshape(devices, 8, rows).transpose(1, 0, 2).reshape(8, width).astype(f32)
-    gain_one, bias_one, b_query, b_value, b_out, gain_two, bias_two, b_down = vecs
+    gain_one, bias_one, _, _, b_out, gain_two, bias_two, _ = vecs
     b_up = packed[:, 8 * rows :].reshape(-1).astype(f32)
 
     local_seg = jnp.arange(TREE_SEGS, dtype=jnp.int32)
     own_parents = lax.dynamic_slice_in_dim(parents, tree * TREE_SEGS, TREE_SEGS) - tree * TREE_SEGS
     parent = jnp.where(local_seg >= 2 * TRUNK_SEGS, own_parents, local_seg)
 
-    b_qkv = jnp.concatenate([head(b_query), jnp.zeros((HEAD_DIM,), f32), head(b_value)])
     norm_one, qkv, context, w_orow, share_up, share_down = attend(
-        parent, x_full, gain_one[None], bias_one[None], w_att, b_qkv[None],
+        parent, x_full, vecs, w_att,
         (HeadRows(w_out), DealColumns(w_up), DealColumns(w_down)), 9
     )
     att, wd, c_full = product_scatter(context, w_orow, 0, 2, "scatter_attended", LIGHT, extras=(
@@ -1114,7 +1130,7 @@
     nt_full, wu = tree_gather(norm_two, 3, "gather_norm_two", LIGHT, extras=(ToTrees(share_up.reshape(-1, fs)),))
     wu = wu.reshape(width, fs)
 
-    active, d_up, gb_up = feed_forward(nt_full, c_full, wu, wd, lax.dynamic_slice_in_dim(b_up, me * fs, fs))
+    active, d_up, gb_up = feed_forward(nt_full, c_full, wu, wd, b_up)
     g_up = dot(nt_full, d_up, 0, 0).astype(bf16)
     d_norm_two, g_up, g_down = product_scatter(d_up, wu, 1, 4, "scatter_d_norm_two", MIXED, extras=(
         DealAllRows(g_up.reshape(devices, rows, fs), (fs,)), Product(c_full, active, 0, bf16),
@@ -1127,21 +1143,19 @@
         SwapTrees(g_down), GatherRows(d_att, ROOM),
     ))
     g_down = own_rows(g_down, swap_down, rows)
-    g_orow = dot(context, da_full, 0, 0).astype(bf16)
-    d_qkv, g_att, shares, s_qkv, g_down, g_o = attend_back(
-        parent, qkv, da_full, w_orow, w_att, norm_one, (DealRows(g_down, (fs,)), HeadRowsBack(g_orow, rows)), 10
+    d_qkv, g_att, shares, g_down, g_o = attend_back(
+        parent, qkv, da_full, w_orow, w_att, context, norm_one, (DealRows(g_down, (fs,)), HeadRowsBack(width, rows)), 10
     )
 
     gb_one = shares[8]
     gg_one = (shares[0] - bias_one * gb_one) / gain_one
-    s_qkv = s_qkv[0]
 
     def placed(vec, total):
         return lax.dynamic_update_slice_in_dim(jnp.zeros((total,), f32), vec, me * vec.shape[0], axis=0)
 
     col = lambda a: jnp.sum(a, axis=0)
     sums = [
-        gg_one, gb_one, placed(s_qkv[:HEAD_DIM], width), placed(s_qkv[2 * HEAD_DIM :], width),
+        gg_one, gb_one, shares[16], shares[24],
         col(d_att.astype(f32)), col(d_norm_two * n_two), col(d_norm_two), col(cot),
     ]
     sums = jnp.stack(sums).reshape(8, devices, rows).transpose(1, 0, 2).reshape(devices, 8 * rows)
@@ -1155,7 +1169,7 @@
     gb_up = sums[8 * rows : n_small]
 
     grad_inputs, layer_output, g_down, g_q, g_k, g_v, g_o, g_up = last(
-        d_norm_one, inputs, d_res, gain_one, residual, mlp, b_down, g_down, (g_q, g_k, g_v, g_o, g_up)
+        d_norm_one, inputs, d_res, vecs, residual, mlp, g_down, (g_q, g_k, g_v, g_o, g_up)
     )
     return (
         layer_output, grad_inputs, parts[0], parts[1], g_q, parts[2], g_k, g_v, parts[3], g_o, parts[4],

time: 521 us -> 515 us (0.988)
  matrix products: 11.4 us -> 5.94 us
    dot_general x2 -> x1, matrix products: 11.4 us -> 5.94 us  [dot(): lax.dot_general(a, b, (((ca,), (cb,)), ((), ())), preferred_element_type=...]
where the time goes in v5:
time: 515 us; the launch traced here: 507 us
  Pallas kernels  480 us (93%)
  other arithmetic  12.6 us (2%)
  local copies, waits for them, and re-layouts  7.1 us (1%)
  matrix products  5.94 us (1%)
    pallas_call x6, Pallas kernels, call(): pl.pallas_call(functools.partial(kernel, extras, lax.axis_size('tree')),...  388 us
    pallas_call x1, Pallas kernels, attend(): pl.pallas_call(functools.partial(attend_kernel, extras, lax.axis_size('tr...  37.6 us
    pallas_call x1, Pallas kernels, attend_back(): pl.pallas_call(functools.partial(attend_back_kernel, extras, lax.axis_siz...  34 us
    pallas_call x1, Pallas kernels, feed_forward(): pl.pallas_call(feed_forward_kernel, grid=(tokens // rows,), in_specs=[by_...  12.2 us

profile of v5, /device:TPU:0, one launch (start us, length us, event | category | flops | bytes accessed | tf_op | source)
XLA Modules:
  0.0 506.9 jit_solution(7413686780162026585)
XLA Ops:
  0.7 1.2 compare_select_fusion.refs_0_
  1.9 1.5 add_bitcast_fusion.refs_0_
  3.4 61.4 %gather_inputs.1 = (bf16[16,2,16,128]{3,2,1,0:T(8,128)(2,1)}, bf16[32,64,384]{2,1,0:T(8,128)(2,1)}, bf16[2048,2048]{1,0:T(8,128)(2,1)}) custom-call(bf16[16,128]{1,0:T(8,128)(2,1)} %add_bitcast_fusion.refs_0_, bf16[64,2048]{1,0:T(8,128)(2,1)} %refs_1_.2, bf16[64,2048]{1,0:T(8,128)(2,1)} %refs_2_.1, bf16[64,2048]{1,0:T(8,128)(2,1)} %refs_3_.2, ...), custom_call_target="tpu_custom_call" | custom-call | bytes 120000000 | tf_op jit(solution)/shard_map/gather_inputs/pallas_call | solution.py:510
  64.7 0.9 copy.35
  65.7 0.1 reshape.154
  65.8 0.7 convert_element_type.70.refs_2_.refs_3_
  66.5 37.6 %attend.1 = (bf16[2048,2048]{1,0:T(8,128)(2,1)}, bf16[2048,384]{1,0:T(8,128)(2,1)}, bf16[2048,128]{1,0:T(8,128)(2,1)}, bf16[128,2048]{1,0:T(8,128)(2,1)}, bf16[1...) custom-call(s32[16]{0:T(128)} %compare_select_fusion.refs_0_, bf16[2048,2048]{1,0:T(8,128)(2,1)} %get-tuple-element.58.refs_1_, ...), custom_call_target="tpu_custom_call" | custom-call | flops 3221225472 | bytes 60000000 | tf_op jit(solution)/shard_map/attend/pallas_call | solution.py:888
  104.2 72.0 %scatter_attended.1 = (f32[128,2048]{1,0:T(8,128)}, bf16[2,1024,512]{2,1,0:T(8,128)(2,1)}, bf16[2048,2048]{1,0:T(8,128)(2,1)}) custom-call(bf16[2048,128]{1,0:T(8,128)(2,1)} %get-tuple-element.63.refs_0_.refs_5_, bf16[128,2048]{1,0:T(8,128)(2,1)} %get-tuple-element.64.refs_1_.refs_3_, bf16[1024,512]{1,0:T(8,128)(2,1)} %bitcast.69, bf16[128,2048]{1,0:T(8,128)(2,1)} %refs_3_.3), custom_call_target="tpu_custom_call" | custom-call | flops 1073741824 | bytes 120000000 | tf_op jit(solution)/shard_map/scatter_attended/pallas_call | solution.py:510
  176.2 0.2 slice_reduce_fusion.1
  176.5 1.4 fusion.3
  178.0 0.3 multiply_reduce_fusion.2
  178.4 1.0 add_convert_fusion.refs_1_
  179.4 51.3 %gather_norm_two.1 = (bf16[2,1024,512]{2,1,0:T(8,128)(2,1)}, bf16[2048,2048]{1,0:T(8,128)(2,1)}) custom-call(bf16[1024,512]{1,0:T(8,128)(2,1)} %bitcast.54, bf16[128,2048]{1,0:T(8,128)(2,1)} %add_convert_fusion.refs_1_), custom_call_target="tpu_custom_call" | custom-call | bytes 120000000 | tf_op jit(solution)/shard_map/gather_norm_two/pallas_call | solution.py:510
  230.8 1.6 copy-done.1
  232.4 12.2 %feed_forward.1 = (bf16[2048,512]{1,0:T(8,128)(2,1)S(1)}, bf16[2048,512]{1,0:T(8,128)(2,1)S(1)}, f32[8,512]{1,0:T(8,128)S(1)}) custom-call(bf16[2048,2048]{1,0:T(8,128)(2,1)} %get-tuple-element.67.n_ref, bf16[2048,2048]{1,0:T(8,128)(2,1)} %get-tuple-element.68.c_ref.refs_3_, bf16[2048,512]{1,0:T(8,128)(2,1)S(1)} %bitcast.45, bf16[2048,512]{1,0:T(8,128)(2,1)S(1)} %bitcast.48, ...), custom_call_target="tpu_custom_call" | custom-call | flops 8589934592 | bytes 16777216 | tf_op jit(solution)/shard_map/feed_forward/pallas_call | solution.py:1038
  244.6 5.9 %convolution_convert_fusion = bf16[2048,512]{1,0:T(8,128)(2,1)} fusion(bf16[2048,2048]{1,0:T(8,128)(2,1)S(1)} %copy-done.10, bf16[2048,512]{1,0:T(8,128)(2,1)S(1)} %get-tuple-element.72.refs_0_), kind=kOutput, calls=%fused_computation | convolution fusion | flops 4296015872 | bytes 12582912 | tf_op jit(solution)/shard_map/dot_general | solution.py:21
  250.6 63.5 %scatter_d_norm_two.1 = (f32[128,2048]{1,0:T(8,128)}, bf16[2,64,8192]{2,1,0:T(8,128)(2,1)}, bf16[2048,512]{1,0:T(8,128)(2,1)}) custom-call(bf16[2048,512]{1,0:T(8,128)(2,1)} %copy-done.2, bf16[2048,512]{1,0:T(8,128)(2,1)} %bitcast.44, bf16[32,64,512]{2,1,0:T(8,128)(2,1)} %bitcast.53, bf16[2048,2048]{1,0:T(8,128)(2,1)} %get-tuple-element.68.c_ref.refs_3_, ...), custom_call_target="tpu_custom_call" | custom-call | flops 4294967296 | bytes 120000000 | tf_op jit(solution)/shard_map/scatter_d_norm_two/pallas_call | solution.py:510
  314.1 1.8 multiply_reduce_fusion
  315.9 1.8 convert_reduce_fusion.1
  317.7 74.5 %scatter_mlp.1 = (f32[128,2048]{1,0:T(8,128)}, bf16[1,1024,512]{2,1,0:T(8,128)(2,1)}, bf16[2048,2048]{1,0:T(8,128)(2,1)}) custom-call(bf16[2048,512]{1,0:T(8,128)(2,1)} %copy-done, bf16[2048,512]{1,0:T(8,128)(2,1)} %bitcast.47, bf16[2048,512]{1,0:T(8,128)(2,1)} %get-tuple-element.73.refs_2_, bf16[128,2048]{1,0:T(8,128)(2,1)} %get-tuple-element.113.refs_3_), custom_call_target="tpu_custom_call" | custom-call | flops 4294967296 | bytes 120000000 | tf_op jit(solution)/shard_map/scatter_mlp/pallas_call | solution.py:510
  392.2 2.5 fusion
  394.7 34.0 %attend_back.1 = (bf16[2048,384]{1,0:T(8,128)(2,1)}, bf16[2048,384]{1,0:T(8,128)(2,1)}, f32[32,2048]{1,0:T(8,128)}, bf16[64,8192]{1,0:T(8,128)(2,1)}, bf16[2,64,2048]{2,1,0:T(8,128)(2,1)}) custom-call(s32[16]{0:T(128)} %compare_select_fusion.refs_0_, bf16[2048,384]{1,0:T(8,128)(2,1)} %get-tuple-element.61.refs_1_, ...), custom_call_target="tpu_custom_call" | custom-call | flops 1073741824 | bytes 60000000 | tf_op jit(solution)/shard_map/attend_back/pallas_call | solution.py:991
  428.8 1.0 slice_reduce_fusion.5
  430.2 0.1 stack.31
  430.5 0.2 stack.32
  430.7 0.1 reshape.147
  430.8 0.3 dynamic_update_slice.3
  431.2 0.7 copy_bitcast_fusion.1.refs_2_
  431.8 65.6 %scatter_d_norm_one.1 = (f32[128,2048]{1,0:T(8,128)}, f32[8,128]{1,0:T(8,128)}, bf16[2,64,2048]{2,1,0:T(8,128)(2,1)}, bf16[2,64,2048]{2,1,0:T(8,128)(2,1)}, bf16[2,64,2048]{2,1,0:T(8,128)(2,1)}) custom-call(bf16[2048,384]{1,0:T(8,128)(2,1)} %get-tuple-element.78.refs_0_, bf16[2048,384]{1,0:T(8,128)(2,1)} %bitcast.51, ...), custom_call_target="tpu_custom_call" | custom-call | flops 3221225472 | bytes 120000000 | tf_op jit(solution)/shard_map/scatter_d_norm_one/pallas_call | solution.py:510
  497.5 7.8 %last.1 = (f32[128,2048]{1,0:T(8,128)}, bf16[128,2048]{1,0:T(8,128)(2,1)}, f32[64,8192]{1,0:T(8,128)}, f32[64,2048]{1,0:T(8,128)}, f32[64,2048]{1,0:T(8,128)}, /...) custom-call(f32[128,2048]{1,0:T(8,128)} %get-tuple-element.82.refs_0_, bf16[128,2048]{1,0:T(8,128)(2,1)} %refs_1_.3, ...), custom_call_target="tpu_custom_call" | custom-call | tf_op jit(solution)/shard_map/last/pallas_call | solution.py:1069
  505.3 0.6 fusion.4
  505.9 0.6 slice_bitcast_fusion
  (46 shorter events, 1.1 us)
Async XLA Ops:
  104.2 72.3 %copy-start.5 = (bf16[128,2048]{1,0:T(8,128)(2,1)S(1)}, bf16[128,2048]{1,0:T(8,128)(2,1)}, u32[]{:S(2)}) copy-start(bf16[128,2048]{1,0:T(8,128)(2,1)} %refs_1_.3) | copy-start | bytes 1572868
  178.0 137.9 %copy-start.4 = (f32[128,2048]{1,0:T(8,128)}, f32[128,2048]{1,0:T(8,128)S(1)}, u32[]{:S(2)}) copy-start(f32[128,2048]{1,0:T(8,128)S(1)} %get-tuple-element.116.refs_4_) | copy-start | bytes 3145732
  178.0 52.8 %copy-start.3 = (bf16[2,1024,512]{2,1,0:T(8,128)(2,1)S(1)}, bf16[2,1024,512]{2,1,0:T(8,128)(2,1)}, u32[]{:S(2)}) copy-start(bf16[2,1024,512]{2,1,0:T(8,128)(2,1)} %get-tuple-element.70) | copy-start | bytes 6291460
  230.8 1.6 copy-start.1
  232.4 12.2 %copy-start.10 = (bf16[2048,2048]{1,0:T(8,128)(2,1)S(1)}, bf16[2048,2048]{1,0:T(8,128)(2,1)}, u32[]{:S(2)}) copy-start(bf16[2048,2048]{1,0:T(8,128)(2,1)} %get-tuple-element.67.n_ref) | copy-start | bytes 25165828
  244.6 6.0 %copy-start = (bf16[2048,512]{1,0:T(8,128)(2,1)}, bf16[2048,512]{1,0:T(8,128)(2,1)S(1)}, u32[]{:S(2)}) copy-start(bf16[2048,512]{1,0:T(8,128)(2,1)S(1)} %get-tuple-element.71.refs_4_.refs_0_) | copy-start | bytes 6291460
  244.6 6.0 %copy-start.2 = (bf16[2048,512]{1,0:T(8,128)(2,1)}, bf16[2048,512]{1,0:T(8,128)(2,1)S(1)}, u32[]{:S(2)}) copy-start(bf16[2048,512]{1,0:T(8,128)(2,1)S(1)} %get-tuple-element.72.refs_0_) | copy-start | bytes 6291460
  314.1 1.8 copy-start.6
  314.1 1.8 copy-start.8
  317.7 74.5 %copy-start.7 = (bf16[2048,512]{1,0:T(8,128)(2,1)S(1)}, bf16[2048,512]{1,0:T(8,128)(2,1)}, u32[]{:S(2)}) copy-start(bf16[2048,512]{1,0:T(8,128)(2,1)} %get-tuple-element.73.refs_2_) | copy-start | bytes 6291460
  497.5 7.9 %copy-start.9 = (f32[8,128]{1,0:T(8,128)S(1)}, f32[8,128]{1,0:T(8,128)}, u32[]{:S(2)}) copy-start(f32[8,128]{1,0:T(8,128)} %get-tuple-element.92) | copy-start | bytes 12292

commit v6 on v5

--- a/solution.py
+++ b/solution.py
@@ -1119,8 +1119,8 @@
         parent, x_full, vecs, w_att,
         (HeadRows(w_out), DealColumns(w_up), DealColumns(w_down)), 9
     )
-    att, wd, c_full = product_scatter(context, w_orow, 0, 2, "scatter_attended", LIGHT, extras=(
-        ToTrees(share_down.reshape(-1, fs)), GatherRows(cotangent, ROOM),
+    att, c_full, wd = product_scatter(context, w_orow, 0, 2, "scatter_attended", ROOM, extras=(
+        GatherRows(cotangent, LIGHT), ToTrees(share_down.reshape(-1, fs)),
     ))
     wd = wd.reshape(width, fs)
     x_own = inputs.astype(f32)
@@ -1139,8 +1139,8 @@
     cot = cotangent.astype(f32)
     d_res = cot + norm_back(d_norm_two, n_two, root_two, gain_two)
     d_att = d_res.astype(bf16)
-    mlp, swap_down, da_full = product_scatter(active, wd, 1, 5, "scatter_mlp", LIGHT, extras=(
-        SwapTrees(g_down), GatherRows(d_att, ROOM),
+    mlp, da_full, swap_down = product_scatter(active, wd, 1, 5, "scatter_mlp", ROOM, extras=(
+        GatherRows(d_att, LIGHT), SwapTrees(g_down),
     ))
     g_down = own_rows(g_down, swap_down, rows)
     d_qkv, g_att, shares, g_down, g_o = attend_back(

time: 515 us -> 515 us (level)
  no operation moved by 1% of the time
where the time goes in v6:
time: 515 us; the launch traced here: 506 us
  Pallas kernels  479 us (93%)
  other arithmetic  12.6 us (2%)
  local copies, waits for them, and re-layouts  7.1 us (1%)
  matrix products  5.94 us (1%)
    pallas_call x6, Pallas kernels, call(): pl.pallas_call(functools.partial(kernel, extras, lax.axis_size('tree')),...  387 us
    pallas_call x1, Pallas kernels, attend(): pl.pallas_call(functools.partial(attend_kernel, extras, lax.axis_size('tr...  37.6 us
    pallas_call x1, Pallas kernels, attend_back(): pl.pallas_call(functools.partial(attend_back_kernel, extras, lax.axis_siz...  34.2 us
    pallas_call x1, Pallas kernels, feed_forward(): pl.pallas_call(feed_forward_kernel, grid=(tokens // rows,), in_specs=[by_...  12.2 us

profile of v6, /device:TPU:0, one launch (start us, length us, event | category | flops | bytes accessed | tf_op | source)
XLA Modules:
  0.0 506.1 jit_solution(8199481092057307877)
XLA Ops:
  0.7 1.2 compare_select_fusion.refs_0_
  1.9 1.5 add_bitcast_fusion.refs_0_
  3.4 61.4 %gather_inputs.1 = (bf16[16,2,16,128]{3,2,1,0:T(8,128)(2,1)}, bf16[32,64,384]{2,1,0:T(8,128)(2,1)}, bf16[2048,2048]{1,0:T(8,128)(2,1)}) custom-call(bf16[16,128]{1,0:T(8,128)(2,1)} %add_bitcast_fusion.refs_0_, bf16[64,2048]{1,0:T(8,128)(2,1)} %refs_1_.2, bf16[64,2048]{1,0:T(8,128)(2,1)} %refs_2_.2, bf16[64,2048]{1,0:T(8,128)(2,1)} %refs_3_.1, ...), custom_call_target="tpu_custom_call" | custom-call | bytes 120000000 | tf_op jit(solution)/shard_map/gather_inputs/pallas_call | solution.py:510
  64.7 0.9 copy.35
  65.7 0.1 reshape.154
  65.8 0.7 convert_element_type.70.refs_2_.refs_3_
  66.5 37.6 %attend.1 = (bf16[2048,2048]{1,0:T(8,128)(2,1)}, bf16[2048,384]{1,0:T(8,128)(2,1)}, bf16[2048,128]{1,0:T(8,128)(2,1)}, bf16[128,2048]{1,0:T(8,128)(2,1)}, bf16[1...) custom-call(s32[16]{0:T(128)} %compare_select_fusion.refs_0_, bf16[2048,2048]{1,0:T(8,128)(2,1)} %get-tuple-element.58.refs_1_, ...), custom_call_target="tpu_custom_call" | custom-call | flops 3221225472 | bytes 60000000 | tf_op jit(solution)/shard_map/attend/pallas_call | solution.py:888
  104.2 72.9 %scatter_attended.1 = (f32[128,2048]{1,0:T(8,128)}, bf16[2048,2048]{1,0:T(8,128)(2,1)}, bf16[2,1024,512]{2,1,0:T(8,128)(2,1)}) custom-call(bf16[2048,128]{1,0:T(8,128)(2,1)} %get-tuple-element.63.refs_0_.refs_5_, bf16[128,2048]{1,0:T(8,128)(2,1)} %get-tuple-element.64.refs_1_.refs_3_, bf16[128,2048]{1,0:T(8,128)(2,1)} %refs_2_.3, bf16[1024,512]{1,0:T(8,128)(2,1)} %bitcast.69), custom_call_target="tpu_custom_call" | custom-call | flops 1073741824 | bytes 120000000 | tf_op jit(solution)/shard_map/scatter_attended/pallas_call | solution.py:510
  177.1 0.2 slice_reduce_fusion.1
  177.4 1.4 fusion.3
  178.9 0.3 multiply_reduce_fusion.2
  179.3 1.0 add_convert_fusion.refs_1_
  180.3 51.0 %gather_norm_two.1 = (bf16[2,1024,512]{2,1,0:T(8,128)(2,1)}, bf16[2048,2048]{1,0:T(8,128)(2,1)}) custom-call(bf16[1024,512]{1,0:T(8,128)(2,1)} %bitcast.54, bf16[128,2048]{1,0:T(8,128)(2,1)} %add_convert_fusion.refs_1_), custom_call_target="tpu_custom_call" | custom-call | bytes 120000000 | tf_op jit(solution)/shard_map/gather_norm_two/pallas_call | solution.py:510
  231.4 1.6 copy-done.1
  233.0 12.2 %feed_forward.1 = (bf16[2048,512]{1,0:T(8,128)(2,1)S(1)}, bf16[2048,512]{1,0:T(8,128)(2,1)S(1)}, f32[8,512]{1,0:T(8,128)S(1)}) custom-call(bf16[2048,2048]{1,0:T(8,128)(2,1)} %get-tuple-element.67.n_ref, bf16[2048,2048]{1,0:T(8,128)(2,1)} %get-tuple-element.68.c_ref.refs_3_, bf16[2048,512]{1,0:T(8,128)(2,1)S(1)} %bitcast.45, bf16[2048,512]{1,0:T(8,128)(2,1)S(1)} %bitcast.48, ...), custom_call_target="tpu_custom_call" | custom-call | flops 8589934592 | bytes 16777216 | tf_op jit(solution)/shard_map/feed_forward/pallas_call | solution.py:1038
  245.2 5.9 %convolution_convert_fusion = bf16[2048,512]{1,0:T(8,128)(2,1)} fusion(bf16[2048,2048]{1,0:T(8,128)(2,1)S(1)} %copy-done.10, bf16[2048,512]{1,0:T(8,128)(2,1)S(1)} %get-tuple-element.72.refs_0_), kind=kOutput, calls=%fused_computation | convolution fusion | flops 4296015872 | bytes 12582912 | tf_op jit(solution)/shard_map/dot_general | solution.py:21
  251.2 63.4 %scatter_d_norm_two.1 = (f32[128,2048]{1,0:T(8,128)}, bf16[2,64,8192]{2,1,0:T(8,128)(2,1)}, bf16[2048,512]{1,0:T(8,128)(2,1)}) custom-call(bf16[2048,512]{1,0:T(8,128)(2,1)} %copy-done.2, bf16[2048,512]{1,0:T(8,128)(2,1)} %bitcast.44, bf16[32,64,512]{2,1,0:T(8,128)(2,1)} %bitcast.53, bf16[2048,2048]{1,0:T(8,128)(2,1)} %get-tuple-element.68.c_ref.refs_3_, ...), custom_call_target="tpu_custom_call" | custom-call | flops 4294967296 | bytes 120000000 | tf_op jit(solution)/shard_map/scatter_d_norm_two/pallas_call | solution.py:510
  314.6 1.8 multiply_reduce_fusion
  316.4 1.8 convert_reduce_fusion.1
  318.2 73.0 %scatter_mlp.1 = (f32[128,2048]{1,0:T(8,128)}, bf16[2048,2048]{1,0:T(8,128)(2,1)}, bf16[1,1024,512]{2,1,0:T(8,128)(2,1)}) custom-call(bf16[2048,512]{1,0:T(8,128)(2,1)} %copy-done, bf16[2048,512]{1,0:T(8,128)(2,1)} %bitcast.47, bf16[128,2048]{1,0:T(8,128)(2,1)} %get-tuple-element.113.refs_2_, bf16[2048,512]{1,0:T(8,128)(2,1)} %get-tuple-element.74.refs_3_), custom_call_target="tpu_custom_call" | custom-call | flops 4294967296 | bytes 120000000 | tf_op jit(solution)/shard_map/scatter_mlp/pallas_call | solution.py:510
  391.2 2.5 fusion
  393.7 34.2 %attend_back.1 = (bf16[2048,384]{1,0:T(8,128)(2,1)}, bf16[2048,384]{1,0:T(8,128)(2,1)}, f32[32,2048]{1,0:T(8,128)}, bf16[64,8192]{1,0:T(8,128)(2,1)}, bf16[2,64,2048]{2,1,0:T(8,128)(2,1)}) custom-call(s32[16]{0:T(128)} %compare_select_fusion.refs_0_, bf16[2048,384]{1,0:T(8,128)(2,1)} %get-tuple-element.61.refs_1_, ...), custom_call_target="tpu_custom_call" | custom-call | flops 1073741824 | bytes 60000000 | tf_op jit(solution)/shard_map/attend_back/pallas_call | solution.py:991
  428.0 1.0 slice_reduce_fusion.5
  429.4 0.1 stack.31
  429.6 0.2 stack.32
  429.8 0.1 reshape.147
  429.9 0.3 dynamic_update_slice.3
  430.3 0.7 copy_bitcast_fusion.1.refs_2_
  431.0 65.6 %scatter_d_norm_one.1 = (f32[128,2048]{1,0:T(8,128)}, f32[8,128]{1,0:T(8,128)}, bf16[2,64,2048]{2,1,0:T(8,128)(2,1)}, bf16[2,64,2048]{2,1,0:T(8,128)(2,1)}, bf16[2,64,2048]{2,1,0:T(8,128)(2,1)}) custom-call(bf16[2048,384]{1,0:T(8,128)(2,1)} %get-tuple-element.78.refs_0_, bf16[2048,384]{1,0:T(8,128)(2,1)} %bitcast.51, ...), custom_call_target="tpu_custom_call" | custom-call | flops 3221225472 | bytes 120000000 | tf_op jit(solution)/shard_map/scatter_d_norm_one/pallas_call | solution.py:510
  496.6 7.8 %last.1 = (f32[128,2048]{1,0:T(8,128)}, bf16[128,2048]{1,0:T(8,128)(2,1)}, f32[64,8192]{1,0:T(8,128)}, f32[64,2048]{1,0:T(8,128)}, f32[64,2048]{1,0:T(8,128)}, /...) custom-call(f32[128,2048]{1,0:T(8,128)} %get-tuple-element.82.refs_0_, bf16[128,2048]{1,0:T(8,128)(2,1)} %refs_1_.3, ...), custom_call_target="tpu_custom_call" | custom-call | tf_op jit(solution)/shard_map/last/pallas_call | solution.py:1069
  504.4 0.6 fusion.4
  505.0 0.6 slice_bitcast_fusion
  (46 shorter events, 1.1 us)
Async XLA Ops:
  104.2 73.2 %copy-start.5 = (bf16[128,2048]{1,0:T(8,128)(2,1)S(1)}, bf16[128,2048]{1,0:T(8,128)(2,1)}, u32[]{:S(2)}) copy-start(bf16[128,2048]{1,0:T(8,128)(2,1)} %refs_1_.3) | copy-start | bytes 1572868
  178.9 137.5 %copy-start.4 = (f32[128,2048]{1,0:T(8,128)}, f32[128,2048]{1,0:T(8,128)S(1)}, u32[]{:S(2)}) copy-start(f32[128,2048]{1,0:T(8,128)S(1)} %get-tuple-element.116.refs_4_) | copy-start | bytes 3145732
  178.9 52.5 %copy-start.3 = (bf16[2,1024,512]{2,1,0:T(8,128)(2,1)S(1)}, bf16[2,1024,512]{2,1,0:T(8,128)(2,1)}, u32[]{:S(2)}) copy-start(bf16[2,1024,512]{2,1,0:T(8,128)(2,1)} %get-tuple-element.70) | copy-start | bytes 6291460
  231.4 1.6 copy-start.1
  233.0 12.2 %copy-start.10 = (bf16[2048,2048]{1,0:T(8,128)(2,1)S(1)}, bf16[2048,2048]{1,0:T(8,128)(2,1)}, u32[]{:S(2)}) copy-start(bf16[2048,2048]{1,0:T(8,128)(2,1)} %get-tuple-element.67.n_ref) | copy-start | bytes 25165828
  245.2 6.0 %copy-start = (bf16[2048,512]{1,0:T(8,128)(2,1)}, bf16[2048,512]{1,0:T(8,128)(2,1)S(1)}, u32[]{:S(2)}) copy-start(bf16[2048,512]{1,0:T(8,128)(2,1)S(1)} %get-tuple-element.71.refs_4_.refs_0_) | copy-start | bytes 6291460
  245.2 6.0 %copy-start.2 = (bf16[2048,512]{1,0:T(8,128)(2,1)}, bf16[2048,512]{1,0:T(8,128)(2,1)S(1)}, u32[]{:S(2)}) copy-start(bf16[2048,512]{1,0:T(8,128)(2,1)S(1)} %get-tuple-element.72.refs_0_) | copy-start | bytes 6291460
  314.6 1.8 copy-start.6
  314.6 1.8 copy-start.8
  318.2 73.0 %copy-start.7 = (bf16[2048,512]{1,0:T(8,128)(2,1)S(1)}, bf16[2048,512]{1,0:T(8,128)(2,1)}, u32[]{:S(2)}) copy-start(bf16[2048,512]{1,0:T(8,128)(2,1)} %get-tuple-element.74.refs_3_) | copy-start | bytes 6291460
  496.6 7.9 %copy-start.9 = (f32[8,128]{1,0:T(8,128)S(1)}, f32[8,128]{1,0:T(8,128)}, u32[]{:S(2)}) copy-start(f32[8,128]{1,0:T(8,128)} %get-tuple-element.92) | copy-start | bytes 12292
